TPU v7x, 32 devices: a whole 2x2x4 slice. The times are simulated.
32 devices in a mesh: ulysses: 4 (over z), dp: 8 (over y, x, core).
Axes of the slice: x: 2, y: 2, z: 4, core: 2. Of those that a mesh axis runs over, the one named last changes fastest.
Arguments:
- tokens: bfloat16 [8, 1024, 2048], P('dp', 'ulysses'), may hold values from -60 to 60
- d_out: bfloat16 [8, 1024, 2048], P('dp', 'ulysses'), may hold values from -6 to 6
- lengths: int32 [8, 10], P('dp'), may hold values from 1 to 384, 1024 in all within a row
- gain: bfloat16 [2048], P('dp'), may hold values from 0.5 to 1.5
- w_qkv: bfloat16 [2048, 1536], P('dp'), may hold values from -16 to 16
- w_out: bfloat16 [2048, 1024], P('dp'), may hold values from -0.1875 to 0.1875
Outputs:
- d_tokens: bfloat16 [8, 1024, 2048], P('dp', 'ulysses')
- d_w_qkv: float32 [2048, 1536], P(('ulysses', 'dp'))
- d_w_out: float32 [2048, 1024], P(('ulysses', 'dp'))
- d_gain: float32 [2048], P(('ulysses', 'dp'))
Inputs may be any that keep to these rules, and one draw needn't show every extreme that they name: Each row holds whole document lengths of 1 to 384 tokens that sum to 1024; the longest is exactly 384.
All inputs are finite; a program needn't handle non-finite values.
Results may differ from a plain program's by a relative error of at most 0.01.
The roundings to bfloat16 on the way count: a program that leaves them out, or rounds other values in their place, can miss the bound.
Values may be sent and summed in bfloat16 or wider, within the bound.
No kernel may reach another device: no remote copies, remote signals or barrier semaphores. Data moves between devices by JAX's collectives and lax.ppermute only.
A program may use at most 128 MiB of HBM per device.

v0:
```python
import math

import jax
import jax.numpy as jnp
from jax import lax
from jax.sharding import PartitionSpec as P

HEADS = 16
KV_HEADS = 4
HEAD_DIM = 64
QW = 1024
KW = 256


EPS = 1e-05
ROPE_BASE = 500000.0


def doc_positions(doc_lengths, length):
    bounds = jnp.cumsum(doc_lengths) - doc_lengths
    places = jnp.arange(length, dtype=jnp.int32)
    begins = jnp.max(jnp.where(bounds[None, :] <= places[:, None], bounds[None, :], 0), axis=1)
    return (begins, places - begins)


def rotary_tables(places):
    inverse = ROPE_BASE ** (-jnp.arange(0, HEAD_DIM, 2).astype(jnp.float32) / HEAD_DIM)
    angles = places.astype(jnp.float32)[:, None] * inverse[None, :]
    angles = jnp.concatenate([angles, angles], axis=1)
    return (jnp.cos(angles), jnp.sin(angles))


def rotate(values, cos_table, sin_table):
    half_dim = HEAD_DIM // 2
    turned = jnp.concatenate([-values[..., half_dim:], values[..., :half_dim]], axis=-1)
    return values * cos_table[:, None, :] + turned * sin_table[:, None, :]


def attend(query_head, key_head, value_head, grad_head, begins):
    length, heads_here, _ = query_head.shape
    block_len = min(512, length)
    blocks = length // block_len
    scale = HEAD_DIM ** (-0.5)
    filler = jnp.zeros((block_len, HEAD_DIM), key_head.dtype)
    key_blocks = jnp.concatenate([filler, key_head], axis=0).reshape(
        blocks + 1, block_len, HEAD_DIM
    )
    key_window = jnp.concatenate([key_blocks[:-1], key_blocks[1:]], axis=1)
    value_blocks = jnp.concatenate([filler, value_head], axis=0).reshape(
        blocks + 1, block_len, HEAD_DIM
    )
    value_window = jnp.concatenate([value_blocks[:-1], value_blocks[1:]], axis=1)
    query_blocks = query_head.reshape(blocks, block_len * heads_here, HEAD_DIM)
    grad_blocks = grad_head.reshape(blocks, block_len * heads_here, HEAD_DIM)
    begin_blocks = begins.reshape(blocks, block_len)

    def one_block(inputs):
        block_index, query_b, grad_b, key_w, value_w, begin_b = inputs
        query_pos = block_index * block_len + jnp.arange(block_len, dtype=jnp.int32)
        key_pos = (block_index - 1) * block_len + jnp.arange(2 * block_len, dtype=jnp.int32)
        allowed = (key_pos[None, :] >= begin_b[:, None]) & (key_pos[None, :] <= query_pos[:, None])
        allowed = jnp.broadcast_to(allowed[:, None, :], (block_len, heads_here, 2 * block_len))
        allowed = allowed.reshape(block_len * heads_here, 2 * block_len)
        scores = jnp.einsum("qd,kd->qk", query_b, key_w, preferred_element_type=jnp.float32) * scale
        scores = jnp.where(allowed, scores, -1e30)
        peak = jnp.max(scores, axis=1, keepdims=True)
        weights = jnp.where(allowed, jnp.exp(scores - peak), 0.0)
        shares = weights / jnp.sum(weights, axis=1, keepdims=True)
        shares_low = shares.astype(jnp.bfloat16)
        mixed = jnp.dot(shares_low, value_w, preferred_element_type=jnp.float32)
        row_dot = jnp.sum(grad_b.astype(jnp.float32) * mixed, axis=1, keepdims=True)
        d_shares = jnp.einsum("qd,kd->qk", grad_b, value_w, preferred_element_type=jnp.float32)
        d_scores = (shares * (d_shares - row_dot) * scale).astype(jnp.bfloat16)
        d_query = jnp.dot(d_scores, key_w, preferred_element_type=jnp.float32)
        d_keys = jnp.einsum("qk,qd->kd", d_scores, query_b, preferred_element_type=jnp.float32)
        d_values = jnp.einsum("qk,qd->kd", shares_low, grad_b, preferred_element_type=jnp.float32)
        return (mixed.astype(jnp.bfloat16), d_query, d_keys, d_values)

    block_ids = jnp.arange(blocks, dtype=jnp.int32)
    mixed, d_query, d_keys, d_values = lax.map(
        one_block, (block_ids, query_blocks, grad_blocks, key_window, value_window, begin_blocks)
    )
    mixed = mixed.reshape(length, heads_here * HEAD_DIM)
    d_query = d_query.reshape(length, heads_here, HEAD_DIM)
    pad_front = ((1, 0), (0, 0), (0, 0))
    pad_back = ((0, 1), (0, 0), (0, 0))
    d_keys = (jnp.pad(d_keys[:, :block_len], pad_back) + jnp.pad(d_keys[:, block_len:], pad_front))[
        1:
    ]
    d_values = (
        jnp.pad(d_values[:, :block_len], pad_back) + jnp.pad(d_values[:, block_len:], pad_front)
    )[1:]
    return (mixed, d_query, d_keys.reshape(length, HEAD_DIM), d_values.reshape(length, HEAD_DIM))


def body(tokens, d_out, lengths, gain, w_qkv, w_out):
    groups = lax.axis_size("ulysses")
    member = lax.axis_index("ulysses")
    full_qkv, full_out, full_gain = (
        lax.all_gather(w_qkv, "dp", axis=0, tiled=True),
        lax.all_gather(w_out, "dp", axis=0, tiled=True),
        lax.all_gather(gain, "dp", axis=0, tiled=True),
    )
    token_rows = tokens[0]
    grad_rows = d_out[0]
    local_rows = token_rows.shape[0]
    length = local_rows * groups
    heads_here = HEADS // groups
    repeat = groups // KV_HEADS
    q_width = heads_here * HEAD_DIM
    factor = 1.0 / math.sqrt(length * lax.axis_size("dp"))
    begins, places = doc_positions(lengths[0], length)
    local_places = lax.dynamic_slice_in_dim(places, member * local_rows, local_rows)
    gain_wide = full_gain.astype(jnp.float32)
    wide_rows = token_rows.astype(jnp.float32)
    inv_rms = lax.rsqrt(jnp.mean(wide_rows * wide_rows, axis=1, keepdims=True) + EPS)
    unit_rows = wide_rows * inv_rms
    normed = (unit_rows * gain_wide[None, :]).astype(jnp.bfloat16)
    projected = jnp.dot(normed, full_qkv, preferred_element_type=jnp.float32)
    cos_local, sin_local = rotary_tables(local_places)
    query = rotate(
        projected[:, :QW].reshape(local_rows, HEADS, HEAD_DIM), cos_local, sin_local
    ).astype(jnp.bfloat16)
    key_rows = rotate(
        projected[:, QW : QW + KW].reshape(local_rows, KV_HEADS, HEAD_DIM), cos_local, sin_local
    ).astype(jnp.bfloat16)
    value_rows = (
        projected[:, QW + KW :].astype(jnp.bfloat16).reshape(local_rows, KV_HEADS, HEAD_DIM)
    )
    key_rows = jnp.repeat(key_rows, repeat, axis=1)
    value_rows = jnp.repeat(value_rows, repeat, axis=1)
    d_attn = jnp.dot(grad_rows, full_out, preferred_element_type=jnp.float32).astype(jnp.bfloat16)
    packed = jnp.concatenate(
        [
            query.reshape(local_rows, groups, q_width),
            key_rows,
            value_rows,
            d_attn.reshape(local_rows, groups, q_width),
        ],
        axis=2,
    )
    arrived = lax.all_to_all(packed, "ulysses", split_axis=1, concat_axis=0, tiled=True)
    head_block = arrived[:, 0, :]
    query_head = head_block[:, :q_width].reshape(length, heads_here, HEAD_DIM)
    key_head = head_block[:, q_width : q_width + HEAD_DIM]
    value_head = head_block[:, q_width + HEAD_DIM : q_width + 2 * HEAD_DIM]
    grad_head = head_block[:, q_width + 2 * HEAD_DIM :].reshape(length, heads_here, HEAD_DIM)
    mixed, d_query, d_keys, d_values = attend(query_head, key_head, value_head, grad_head, begins)
    cos_table, sin_table = rotary_tables(places)
    d_query = rotate(d_query, cos_table, -sin_table).astype(jnp.bfloat16).reshape(length, q_width)
    d_keys = rotate(d_keys[:, None, :], cos_table, -sin_table)[:, 0, :].astype(jnp.bfloat16)
    d_values = d_values.astype(jnp.bfloat16)
    outgoing = jnp.concatenate([mixed, d_query, d_keys, d_values], axis=1)[:, None, :]
    returned = lax.all_to_all(outgoing, "ulysses", split_axis=0, concat_axis=1, tiled=True)
    mixed_rows = returned[:, :, :q_width].reshape(local_rows, QW)
    dq_rows = returned[:, :, q_width : 2 * q_width].reshape(local_rows, QW)
    dk_rows = returned[:, :, 2 * q_width : 2 * q_width + HEAD_DIM].astype(jnp.float32)
    dk_rows = (
        dk_rows.reshape(local_rows, KV_HEADS, repeat, HEAD_DIM)
        .sum(axis=2)
        .astype(jnp.bfloat16)
        .reshape(local_rows, KW)
    )
    dv_rows = returned[:, :, 2 * q_width + HEAD_DIM :].astype(jnp.float32)
    dv_rows = (
        dv_rows.reshape(local_rows, KV_HEADS, repeat, HEAD_DIM)
        .sum(axis=2)
        .astype(jnp.bfloat16)
        .reshape(local_rows, KW)
    )
    d_proj = jnp.concatenate([dq_rows, dk_rows, dv_rows], axis=1)
    grad_qkv = jnp.einsum("td,tc->dc", normed, d_proj, preferred_element_type=jnp.float32) * factor
    grad_out = (
        jnp.einsum("td,tc->dc", grad_rows, mixed_rows, preferred_element_type=jnp.float32) * factor
    )
    d_normed = jnp.einsum("tc,dc->td", d_proj, full_qkv, preferred_element_type=jnp.float32)
    grad_gain = jnp.sum(d_normed * unit_rows, axis=0) * factor
    scaled = d_normed * gain_wide[None, :]
    d_rows = inv_rms * (scaled - unit_rows * jnp.mean(scaled * unit_rows, axis=1, keepdims=True))
    d_tokens = (grad_rows.astype(jnp.float32) + d_rows).astype(jnp.bfloat16)
    summed = (
        lax.psum_scatter(grad_qkv, ("ulysses", "dp"), scatter_dimension=0, tiled=True),
        lax.psum_scatter(grad_out, ("ulysses", "dp"), scatter_dimension=0, tiled=True),
        lax.psum_scatter(grad_gain, ("ulysses", "dp"), scatter_dimension=0, tiled=True),
    )
    return (d_tokens[None], summed[0], summed[1], summed[2])


def solution(mesh):
    in_specs = (
        P("dp", "ulysses", None),
        P("dp", "ulysses", None),
        P("dp", None),
        P("dp"),
        P("dp", None),
        P("dp", None),
    )
    out_specs = (
        P("dp", "ulysses", None),
        P(("ulysses", "dp"), None),
        P(("ulysses", "dp"), None),
        P(("ulysses", "dp")),
    )
    return jax.shard_map(body, mesh=mesh, in_specs=in_specs, out_specs=out_specs, check_vma=False)
```

profile of v0, /device:TPU:0, one launch (start us, length us, event | category | flops | bytes accessed | tf_op | source)
XLA Modules:
  0.0 591.9 jit_solution(10540584775463450468)
XLA Ops:
  10.2 10.3 %all-gather = bf16[8,1,256]{2,1,0:T(2,128)(2,1)S(1)} all-gather(bf16[1,1,256]{2,1,0:T(2,128)(2,1)S(1)} %reshape.320), channel_id=1, replica_groups=mesh['ulysses'=4,'dp'=8] {'dp'}, dimensions={0}, use_global_device_ids=true | all-gather | bytes 4608 | tf_op jit(solution)/shard_map/all_gather | solution.py:102
  21.9 27.4 %all-gather.6.cloned.1.call-done = bf16[2048,1024]{1,0:T(8,128)(2,1)} async-done(((bf16[256,1024]{1,0:T(8,128)(2,1)}), bf16[2048,1024]{1,0:T(8,128)(2,1)}) %all-gather.6.cloned.1.call-update) | async-done | bytes 4194320 | tf_op jit(solution)/shard_map/all_gather | solution.py:101
  49.4 3.4 convolution_convert_fusion
  53.0 43.8 %all-gather.4.cloned.1.call-done = bf16[2048,1536]{1,0:T(8,128)(2,1)} async-done(((bf16[256,1536]{1,0:T(8,128)(2,1)}), bf16[2048,1536]{1,0:T(8,128)(2,1)}) %all-gather.4.cloned.1.call-update) | async-done | bytes 6291472 | tf_op jit(solution)/shard_map/all_gather | solution.py:100
  96.8 4.6 fusion.56
  105.2 1.2 pad_maximum_fusion
  106.3 4.6 all-to-all-start
  111.7 31.0 %all-to-all-done = bf16[256,4,640]{0,2,1:T(8,128)(2,1)S(1)} async-done(((bf16[256,4,640]{0,2,1:T(8,128)(2,1)}), bf16[256,4,640]{0,2,1:T(8,128)(2,1)S(1)}, u32[]{:S(2)}, u32[]{:S(2)}) %all-to-all-start) | async-done | bytes 1310752 | tf_op jit(solution)/shard_map/all_to_all | solution.py:142
  144.4 1.4 reshape_reshape.6
  146.8 51.7 %while.18 = (s32[]{:T(128)}, bf16[2,2048,64]{1,2,0:T(8,128)(2,1)}, f32[2,2048,64]{1,2,0:T(8,128)}, f32[2,1024,64]{1,2,0:T(8,128)}, f32[2,1024,64]{1,2,0:T(8,128)...) while((s32[]{:T(128)}, bf16[2,2048,64]{1,2,0:T(8,128)(2,1)}, ...), condition=%wide.region_7.8_spmd, body=%wide.region_3.7_spmd.sunk | while | flops 1652551168 | bytes 118571504 | solution.py:80
  149.4 1.9 broadcast_in_dim.121
  151.3 3.9 reshape.328
  155.3 3.7 copy.163
  159.0 1.6 fusion.106
  160.6 2.5 fusion.107
  163.1 2.5 fusion.108
  166.7 1.3 multiply_convert_fusion.2
  169.0 1.4 fusion.110
  170.4 1.4 fusion.111
  175.1 1.9 broadcast_in_dim.121
  177.0 3.9 reshape.328
  180.9 3.7 copy.163
  184.6 1.6 fusion.106
  186.2 2.5 fusion.107
  188.8 2.5 fusion.108
  192.3 1.3 multiply_convert_fusion.2
  194.7 1.4 fusion.110
  196.1 1.4 fusion.111
  198.5 1.8 copy.135
  200.9 3.1 slice_negate_fusion
  206.9 3.5 maximum_multiply_fusion
  210.5 1.6 copy.139
  212.1 1.6 copy.140
  214.7 1.6 copy.136
  216.5 2.4 copy.134
  218.8 2.6 reshape.314
  225.2 1.6 reduce
  227.2 34.1 %all_to_all.33 = bf16[4,2,81920]{2,1,0:T(2,128)(2,1)} all-to-all(bf16[4,2,81920]{2,1,0:T(2,128)(2,1)S(1)} %reshape.325), channel_id=1, replica_groups=mesh['ulysses'=4,'dp'=8] {'ulysses'}, dimensions={0} | all-to-all | bytes 2621440 | tf_op jit(solution)/shard_map/all_to_all | solution.py:154
  261.3 2.8 reshape.326
  266.1 4.5 multiply_bitcast_fusion
  270.6 9.2 %copy.156 = f32[2048,1024]{1,0:T(8,128)} copy(f32[2048,1024]{0,1:T(8,128)} %multiply_bitcast_fusion) | data formatting | bytes 16777216
  280.4 1.2 fusion.73
  281.9 6.5 %convolution_multiply_fusion = f32[2048,1536]{1,0:T(8,128)} fusion(bf16[256,256]{0,1:T(8,128)(2,1)S(1)} %bitcast.182, bf16[256,256]{0,1:T(8,128)(2,1)S(1)} %bitcast.180, bf16[256,1024]{0,1:T(8,128)(2,1)S(1)} %bitcast.174, bf16[1,256,2048]{2,1,0:T(8,128)(2,1)S(1)} %copy-done.3, f32[2048]{0:T(1024)S(1)} %bitcast.187, f32[256]{0:T(256)S(1)} %copy-done.24), kind=kOutput, calls=%fused_computation.45 | convolution fusion | flops 1618214912 | bytes 14427136 | tf_op jit(solution)/shard_map/td,tc->dc/dot_general | solution.py:172
  288.4 6.3 %fusion.48 = (f32[2048]{0:T(1024)S(1)}, f32[256]{0:T(256)S(1)}, f32[256,2048]{1,0:T(8,128)}) fusion(bf16[1,256,2048]{2,1,0:T(8,128)(2,1)S(1)} %copy-done.3, f32[256]{0:T(256)S(1)} %copy-done.24, f32[2048]{0:T(1024)S(1)} %bitcast.188, bf16[2048,1536]{1,0:T(8,128)(2,1)} %all-gather.4.cloned.1.call-done, bf16[256,256]{0,1:T(8,128)(2,1)S(1)} %bitcast.183, ...), kind=kOutput, calls=%fused_computation.59 | convolution fusion | flops 1616639744 | bytes 10242048 | tf_op jit(solution)/shard_map/tc,dc->td/dot_general | solution.py:176
  294.6 40.1 %all-reduce.6 = f32[2048]{0:T(1024)S(1)} all-reduce(f32[2048]{0:T(1024)S(1)} %broadcast_multiply_fusion.2), channel_id=4, replica_groups=mesh['ulysses'=4,'dp'=8] {'ulysses','dp'}, use_global_device_ids=true, to_apply=%region_12.13.clone | all-reduce | flops 2048 | bytes 16384
  335.3 3.3 fusion.50
  338.6 88.7 %reduce-scatter.7.cloned.1.call-done = f32[64,1024]{1,0:T(8,128)} async-done(((f32[2048,1024]{1,0:T(8,128)}), f32[64,1024]{1,0:T(8,128)}) %reduce-scatter.7.cloned.1.call-update) | async-done | bytes 262160
  427.2 157.8 %reduce-scatter.5.cloned.1.call-done = f32[64,1536]{1,0:T(8,128)} async-done(((f32[2048,1536]{1,0:T(8,128)}), f32[64,1536]{1,0:T(8,128)}) %reduce-scatter.5.cloned.1.call-update) | async-done | bytes 393232 | tf_op jit(solution)/shard_map/reduce_scatter | solution.py:182
  (162 shorter events, 31.8 us)
Async XLA Ops:
  7.2 14.4 %copy-start.2 = (bf16[1,256,2048]{2,1,0:T(8,128)(2,1)S(1)}, bf16[1,256,2048]{2,1,0:T(8,128)(2,1)}, u32[]{:S(2)}) copy-start(bf16[1,256,2048]{2,1,0:T(8,128)(2,1)} %param.8) | copy-start | bytes 3145732
  7.2 42.2 %copy-start.5 = (bf16[1,256,2048]{2,1,0:T(8,128)(2,1)S(1)}, bf16[1,256,2048]{2,1,0:T(8,128)(2,1)}, u32[]{:S(2)}) copy-start(bf16[1,256,2048]{2,1,0:T(8,128)(2,1)} %param.9) | copy-start | bytes 3145732
  7.2 42.2 %all-gather.6.cloned.1.call-start = ((), (), s32[]{:S(2)}) async-start(), calls=%async_computation.5 | async-start | bytes 4718592 | tf_op jit(solution)/shard_map/all_gather | solution.py:101
  7.9 88.9 %all-gather.4.cloned.1.call-start = ((), (), s32[]{:S(2)}) async-start(), calls=%async_computation.4 | async-start | bytes 7077888 | tf_op jit(solution)/shard_map/all_gather | solution.py:100
  20.5 76.3 %copy-start.21 = (f32[8,1,256]{2,1,0:T(1,128)}, f32[8,1,256]{2,1,0:T(1,128)S(1)}, u32[]{:S(2)}) copy-start(f32[8,1,256]{2,1,0:T(1,128)S(1)} %convert_element_type.120) | copy-start | bytes 24580
  21.9 74.9 %copy-start.23 = (f32[256]{0:T(256)}, f32[256]{0:T(256)S(1)}, u32[]{:S(2)}) copy-start(f32[256]{0:T(256)S(1)} %add_rsqrt_fusion) | copy-start | bytes 3076
  101.4 1.2 copy-start.8
  103.3 0.9 slice-start
  103.6 0.9 copy-start.20
  106.3 36.4 %all-to-all-start = ((bf16[256,4,640]{0,2,1:T(8,128)(2,1)}), bf16[256,4,640]{0,2,1:T(8,128)(2,1)S(1)}, u32[]{:S(2)}, u32[]{:S(2)}) async-start(bf16[256,4,640]{0,2,1:T(8,128)(2,1)} %pad_maximum_fusion), calls=%async_computation | async-start | bytes 2621440 | tf_op jit(solution)/shard_map/all_to_all | solution.py:142
  110.9 316.3 %reduce-scatter.7.cloned.1.call-start = ((), (), s32[]{:S(2)}) async-start(), calls=%async_computation.7 | async-start | bytes 8650752
  155.3 3.7 copy-start
  155.3 3.7 copy-start.1
  163.1 2.5 copy-start.12
  166.5 1.4 copy-start.13
  166.6 1.3 copy-start.9
  168.0 1.0 copy-start.15
  168.9 1.5 copy-start.10
  169.0 1.4 copy-start.18
  170.4 1.4 copy-start.16
  171.9 0.8 copy-start.19
  180.9 3.7 copy-start
  180.9 3.7 copy-start.1
  188.8 2.5 copy-start.12
  192.2 1.4 copy-start.13
  192.3 1.3 copy-start.9
  193.6 1.0 copy-start.15
  194.5 1.5 copy-start.10
  194.7 1.4 copy-start.18
  196.1 1.4 copy-start.16
  197.5 0.8 copy-start.19
  200.9 3.1 copy-start.17
  204.0 0.9 copy-start.14
  223.4 1.0 copy-start.7
  223.4 1.1 copy-start.11
  264.4 1.1 copy-start.4
  264.4 1.7 copy-start.6
  279.9 2.0 copy-start.3
  279.9 2.0 copy-start.22
  279.9 2.0 copy-start.24
  279.9 305.1 %reduce-scatter.5.cloned.1.call-start = ((), (), s32[]{:S(2)}) async-start(), calls=%async_computation.6 | async-start | bytes 12976128 | tf_op jit(solution)/shard_map/reduce_scatter | solution.py:182
Sparse Core Ops, SparseCore 0:
  9.9 39.4 all-gather.5
  51.2 45.5 all-gather.3
  280.0 147.1 reduce-scatter.6
  433.7 151.2 reduce-scatter.4
where the time goes:
time: 598 us; the launch traced here: 592 us
  waiting for transfers between devices  350 us (59%)
  blocking collectives  84.5 us (14%)
  local copies, waits for them, and re-layouts  64.4 us (11%)
  matrix products  40.2 us (7%)
  other arithmetic  29.8 us (5%)
  between operations  14.7 us (2%)
    reduce_scatter x1, waiting for transfers between devices, body(): lax.psum_scatter(grad_qkv, ('ulysses', 'dp'), scatter_dimension=0, tiled=...  158 us
    unnamed x5, waiting for transfers between devices  90.1 us
    all_gather x1, waiting for transfers between devices, body(): lax.all_gather(w_qkv, 'dp', axis=0, tiled=True)  43.8 us
    unnamed x1, blocking collectives  40.1 us
    all_to_all x1, blocking collectives, body(): lax.all_to_all(outgoing, 'ulysses', split_axis=0, concat_axis=1, tiled=True)  34.1 us
    all_to_all x1, waiting for transfers between devices, body(): lax.all_to_all(packed, 'ulysses', split_axis=1, concat_axis=0, tiled=True)  31 us
    all_gather x1, waiting for transfers between devices, body(): lax.all_gather(w_out, 'dp', axis=0, tiled=True)  27.4 us
    unnamed x36, local copies, waits for them, and re-layouts  17.8 us
  transfers between devices with their start and end apart: 5, of which 5 were waited for; matrix products, arithmetic and copies ran while one was open for 4% of the time, Pallas kernels for 0%

commit v1 on v0

v1 whole, which is shorter than its diff:
```python
import functools
import math

import jax
import jax.numpy as jnp
from jax import lax
from jax.experimental import pallas as pl
from jax.experimental.pallas import tpu as pltpu
from jax.sharding import PartitionSpec as P

HEADS = 16
KV_HEADS = 4
HEAD_DIM = 64
QW = 1024
KW = 256
DOC_MOST = 384
Q_BLOCK = 128

EPS = 1e-05
ROPE_BASE = 500000.0
SCALE = HEAD_DIM ** (-0.5)

bf16 = jnp.bfloat16
f32 = jnp.float32


def params(mib):
    return pltpu.CompilerParams(vmem_limit_bytes=mib << 20)


SMEM = pl.BlockSpec(memory_space=pltpu.SMEM)
VMEM = pl.BlockSpec(memory_space=pltpu.VMEM)


def nt(a, b):
    return lax.dot_general(a, b, (((1,), (1,)), ((), ())), preferred_element_type=f32)


def tn(a, b):
    return lax.dot_general(a, b, (((0,), (0,)), ((), ())), preferred_element_type=f32)


def nn(a, b):
    return jnp.dot(a, b, preferred_element_type=f32)


def swap(a, axis, bit):
    n = lax.axis_size(axis)
    return lax.ppermute(a, axis, [(i, i ^ bit) for i in range(n)])


def gather_slots(a, axis, split):
    n = lax.axis_size(axis)
    slots = {0: [a]}
    if n >= 4:
        first, second = n // 4, n // 2
        over_first, over_second = swap(a, axis, first), swap(a, axis, second)
        upper = swap(over_first[:split], axis, second)
        lower = swap(over_second[split:], axis, first)
        slots[first], slots[second] = [over_first], [over_second]
        slots[first | second] = [upper, lower]
        bit = n // 8
    else:
        bit = n // 2
    while bit >= 1:
        for j in list(slots):
            slots[j ^ bit] = [swap(piece, axis, bit) for piece in slots[j]]
        bit //= 2
    return [slots[j] for j in range(n)]


def flat(slots):
    return [piece for slot in slots for piece in slot], [len(slot) for slot in slots]


def regroup(refs, counts):
    out, at = [], 0
    for c in counts:
        out.append(refs[at : at + c])
        at += c
    return out


def whole_slot(pieces, rows):
    values = [p[...] for p in pieces]
    value = values[0] if len(values) == 1 else jnp.concatenate(values, axis=0)
    return value[:rows], value


def turn(x, lower):
    return jnp.where(lower, pltpu.roll(x, 96, 1), pltpu.roll(x, 32, 1))


def lower_lanes(rows):
    return lax.broadcasted_iota(jnp.int32, (rows, 128), 1) % HEAD_DIM < HEAD_DIM // 2


def inverse_rms(x):
    return lax.rsqrt(jnp.mean(x * x, axis=1, keepdims=True) + EPS)


def proj_kernel(counts, groups, me_ref, tok_ref, cos_ref, sin_ref, *refs):
    n = len(counts)
    slots = regroup(refs[: sum(counts)], counts)
    outs = refs[sum(counts) : sum(counts) + groups]
    normed_ref, acc = refs[sum(counts) + groups :]
    u, d = me_ref[0], me_ref[1]
    rows, width = tok_ref.shape
    part = width // n
    inv = inverse_rms(tok_ref[...].astype(f32))
    for j in range(n):
        at = pl.multiple_of((d ^ j) * part, part)
        w, ext = whole_slot(slots[j], part)
        gain = ext[part : part + 1, :part].astype(f32)
        normed = (tok_ref[:, pl.ds(at, part)].astype(f32) * inv * gain).astype(bf16)
        normed_ref[:, pl.ds(at, part)] = normed
        term = nn(normed, w)
        if j == 0:
            acc[...] = term
        else:
            acc[...] += term
    lower = lower_lanes(rows)
    cos, sin = cos_ref[...], sin_ref[...]
    turned = []
    for c in range((QW + KW) // 128):
        x = acc[:, c * 128 : (c + 1) * 128]
        turned.append((x * cos + turn(x, lower) * sin).astype(bf16))
    heads = HEADS // groups
    repeat = groups // KV_HEADS
    for g in range(groups):
        qw = heads * HEAD_DIM
        q = jnp.concatenate(turned[g * qw // 128 : (g + 1) * qw // 128], axis=1)
        kh = g // repeat
        at = QW // 128 + kh // 2
        half = (kh % 2) * HEAD_DIM
        k = turned[at][:, half : half + HEAD_DIM]
        v = acc[:, QW + KW + kh * HEAD_DIM : QW + KW + (kh + 1) * HEAD_DIM].astype(bf16)
        piece = jnp.concatenate([q, k, v], axis=1)
        for j in range(groups):

            @pl.when((u ^ g) == j)
            def _():
                outs[j][...] = piece


def d_attn_kernel(counts, groups, me_ref, d_out_ref, *refs):
    n = len(counts)
    slots = regroup(refs[: sum(counts)], counts)
    outs = refs[sum(counts) : sum(counts) + groups]
    acc = refs[-1]
    u, d = me_ref[0], me_ref[1]
    part = d_out_ref.shape[1] // n
    for j in range(n):
        at = pl.multiple_of((d ^ j) * part, part)
        w, _ = whole_slot(slots[j], part)
        term = nn(d_out_ref[:, pl.ds(at, part)], w)
        if j == 0:
            acc[...] = term
        else:
            acc[...] += term
    qw = QW // groups
    for g in range(groups):
        piece = acc[:, g * qw : (g + 1) * qw].astype(bf16)
        for j in range(groups):

            @pl.when((u ^ g) == j)
            def _():
                outs[j][...] = piece


def slices_kernel(n, groups, me_ref, normed_ref, d_out_ref, *refs):
    outs = refs[:n]
    turned = refs[n]
    d = me_ref[1]
    width = normed_ref.shape[1]
    block = width // (groups * n)
    for side, ref in enumerate((normed_ref, d_out_ref)):
        turned[...] = ref[...].T
        for j in range(n):
            for g in range(groups):
                at = pl.multiple_of(g * (width // groups) + (d ^ j) * block, block)
                outs[j][pl.ds((side * groups + g) * block, block), :] = turned[pl.ds(at, block), :]


def attend_kernel(groups, me_ref, begin_ref, cos_ref, sin_ref, *refs):
    qkv_refs, grad_refs = refs[:groups], refs[groups : 2 * groups]
    attn_outs, back_outs = refs[2 * groups : 3 * groups], refs[3 * groups : 4 * groups]
    q_all, kv_all, g_all, attn_all, dq_all, dkv_all, acc, p_low, s_low = refs[4 * groups :]
    u = me_ref[0]
    length, qw = q_all.shape
    heads = qw // HEAD_DIM
    rows = length // groups
    for j in range(groups):
        at = pl.ds(pl.multiple_of((u ^ j) * rows, rows), rows)
        q_all[at, :] = qkv_refs[j][:, :qw] * jnp.asarray(SCALE, bf16)
        kv_all[at, :] = qkv_refs[j][:, qw:]
        g_all[at, :] = grad_refs[j][...]
    acc[...] = jnp.zeros_like(acc)
    for b in range(length // Q_BLOCK):
        q0 = b * Q_BLOCK
        w0 = max(0, q0 - DOC_MOST)
        w1 = q0 + Q_BLOCK
        win = w1 - w0
        here = slice(q0, w1)
        keys = kv_all[w0:w1, :HEAD_DIM]
        values = kv_all[w0:w1, HEAD_DIM:]
        key_pos = w0 + lax.broadcasted_iota(jnp.int32, (Q_BLOCK, win), 1)
        row_pos = q0 + lax.broadcasted_iota(jnp.int32, (Q_BLOCK, win), 0)
        allowed = (key_pos >= begin_ref[here, :]) & (key_pos <= row_pos)
        bias = jnp.where(allowed, 0.0, -1e30).astype(f32)
        queries, grads, mixes, d_queries = [], [], [], []
        for h in range(heads):
            lanes = slice(h * HEAD_DIM, (h + 1) * HEAD_DIM)
            query, grad = q_all[here, lanes], g_all[here, lanes]
            scores = nt(query, keys) + bias
            peak = jnp.max(scores, axis=1, keepdims=True)
            weights = jnp.exp(scores - peak)
            shares = weights * (1.0 / jnp.sum(weights, axis=1, keepdims=True))
            shares_low = shares.astype(bf16)
            mixed = nn(shares_low, values)
            row_dot = jnp.sum(grad.astype(f32) * mixed, axis=1, keepdims=True)
            d_scores = (shares * (nt(grad, values) - row_dot)).astype(bf16)
            d_queries.append(nn(d_scores, keys) * SCALE)
            mixes.append(mixed)
            p_low[h * Q_BLOCK : (h + 1) * Q_BLOCK, :win] = shares_low
            s_low[h * Q_BLOCK : (h + 1) * Q_BLOCK, :win] = d_scores
            queries.append(query)
            grads.append(grad)
        attn_all[here, :] = jnp.concatenate(mixes, axis=1).astype(bf16)
        dq_all[here, :] = jnp.concatenate(d_queries, axis=1)
        acc[:HEAD_DIM, w0:w1] += tn(jnp.concatenate(queries, axis=0), s_low[:, :win])
        acc[HEAD_DIM:, w0:w1] += tn(jnp.concatenate(grads, axis=0), p_low[:, :win])
    dkv_all[...] = acc[...].T
    lower = lower_lanes(rows)
    value_lane = lax.broadcasted_iota(jnp.int32, (rows, 128), 1) >= HEAD_DIM
    for g in range(groups):
        here = slice(g * rows, (g + 1) * rows)
        cos, sin = cos_ref[here, :], sin_ref[here, :]
        parts = []
        for c in range(qw // 128):
            x = dq_all[here, c * 128 : (c + 1) * 128]
            parts.append(x * cos - turn(x, lower) * sin)
        x = dkv_all[here, :]
        parts.append(jnp.where(value_lane, x, x * cos - turn(x, lower) * sin))
        back = jnp.concatenate(parts, axis=1).astype(bf16)
        mixed = attn_all[here, :]
        for j in range(groups):

            @pl.when((u ^ g) == j)
            def _():
                attn_outs[j][...] = mixed
                back_outs[j][...] = back


def join_attn_kernel(groups, me_ref, *refs):
    u, out = me_ref[0], refs[groups]
    qw = QW // groups
    for j in range(groups):
        at = pl.multiple_of((u ^ j) * qw, qw)
        out[:, pl.ds(at, qw)] = refs[j][...]


def join_proj_kernel(groups, me_ref, *refs):
    u, out = me_ref[0], refs[groups]
    wide = refs[groups + 1]
    qw = QW // groups
    repeat = groups // KV_HEADS
    wide[...] = jnp.zeros_like(wide)
    for j in range(groups):
        at = pl.multiple_of((u ^ j) * qw, qw)
        out[:, pl.ds(at, qw)] = refs[j][:, :qw]
        back = refs[j][:, qw:].astype(f32)
        for kh in range(KV_HEADS):

            @pl.when((u ^ j) // repeat == kh)
            def _():
                wide[:, kh * 128 : (kh + 1) * 128] += back

    low = wide[...].astype(bf16)
    for at, half in ((QW, 0), (QW + KW, HEAD_DIM)):
        heads = [low[:, kh * 128 + half : kh * 128 + half + HEAD_DIM] for kh in range(KV_HEADS)]
        out[:, at : at + KW] = jnp.concatenate(heads, axis=1)


def tokens_kernel(counts, groups, factor, me_ref, tok_ref, d_out_ref, d_proj_ref, *refs):
    n = len(counts)
    slots = regroup(refs[: sum(counts)], counts)
    d_tok_ref, d_gain_ref, wide, gains = refs[sum(counts) :]
    d = me_ref[1]
    width = tok_ref.shape[1]
    part = width // n
    d_proj = d_proj_ref[...]
    for j in range(n):
        at = pl.multiple_of((d ^ j) * part, part)
        w, ext = whole_slot(slots[j], part)
        wide[:, pl.ds(at, part)] = nt(d_proj, w)
        gains[:, pl.ds(at, part)] = ext[part : part + 1, :part].astype(f32)
    x = tok_ref[...].astype(f32)
    inv = inverse_rms(x)
    unit = x * inv
    d_normed = wide[...]
    d_gain = jnp.sum(d_normed * unit, axis=0, keepdims=True) * factor
    scaled = d_normed * gains[...]
    mean = jnp.mean(scaled * unit, axis=1, keepdims=True)
    d_tok_ref[...] = (d_out_ref[...].astype(f32) + inv * (scaled - unit * mean)).astype(bf16)
    block = width // (groups * n)
    for e in range(n):
        starts = [g * (width // groups) + e * block for g in range(groups)]
        mine = jnp.concatenate([d_gain[:, s : s + block] for s in starts], axis=1)
        d_gain_ref[pl.ds(d ^ e, 1)] = mine[None]


def grads_kernel(counts, side, groups, factor, has_gain, *refs):
    n = len(counts)
    slices = refs[:n]
    slots = regroup(refs[n : n + sum(counts)], counts)
    rest = refs[n + sum(counts) :]
    gains, (out, acc) = (rest[:n], rest[n:]) if has_gain else ((), rest)
    kept = acc.shape[0]
    for j in range(n):
        a = slices[j][side * kept : (side + 1) * kept, :]
        b, _ = whole_slot(slots[j], a.shape[1])
        term = nn(a, b)
        if j == 0:
            acc[...] = term
        else:
            acc[...] += term
    block = kept // groups
    for g in range(groups):
        out[g, :block, :] = acc[g * block : (g + 1) * block, :] * factor
    if has_gain:
        total = gains[0][0]
        for j in range(1, n):
            total = total + gains[j][0]
        for g in range(groups):
            out[g, block:, :] = jnp.zeros_like(out[g, block:, :])
            out[g, block : block + 1, :block] = total[:, g * block : (g + 1) * block]


def chain_sum(local, axis):
    n = lax.axis_size(axis)
    me = lax.axis_index(axis)

    def block(at):
        return lax.dynamic_index_in_dim(local, jnp.clip(at, 0, n - 1), 0, keepdims=False)

    up = down = None
    for step in range(n - 1):
        a, b = block(n - 1 - step + me), block(me - (n - 1) + step)
        up = a if up is None else a + up
        down = b if down is None else b + down
        up = lax.ppermute(up, axis, [(i, i + 1) for i in range(step + 1)])
        down = lax.ppermute(down, axis, [(n - 1 - i, n - 2 - i) for i in range(step + 1)])
    return block(me) + up + down


def shape(*dims, dtype=bf16):
    return jax.ShapeDtypeStruct(dims, dtype)


def body(tokens, d_out, lengths, gain, w_qkv, w_out):
    groups, n = lax.axis_size("ulysses"), lax.axis_size("dp")
    u, d = lax.axis_index("ulysses"), lax.axis_index("dp")
    me = jnp.stack([u, d]).astype(jnp.int32)
    token_rows, grad_rows = tokens[0], d_out[0]
    rows, width = token_rows.shape
    length = rows * groups
    part = width // n
    heads = HEADS // groups
    qw = heads * HEAD_DIM
    columns = w_qkv.shape[1]
    factor = 1.0 / math.sqrt(length * n)
    block = width // (groups * n)
    kept = block * groups

    gain_rows = jnp.pad(gain[None, :], ((0, 15), (0, columns - part)))
    qkv_slots = gather_slots(jnp.concatenate([w_qkv, gain_rows], axis=0), "dp", part // 2)
    out_slots = gather_slots(w_out, "dp", part // 2)
    qkv_flat, qkv_counts = flat(qkv_slots)
    out_flat, out_counts = flat(out_slots)

    bounds = jnp.cumsum(lengths[0]) - lengths[0]
    places = jnp.arange(length, dtype=jnp.int32)
    begins = jnp.max(jnp.where(bounds[None, :] <= places[:, None], bounds[None, :], 0), axis=1)
    places = places - begins
    inverse = ROPE_BASE ** (-jnp.arange(0, HEAD_DIM, 2).astype(f32) / HEAD_DIM)
    angles = places.astype(f32)[:, None] * jnp.tile(inverse, 4)[None, :]
    signs = jnp.where(jnp.arange(128) % HEAD_DIM < HEAD_DIM // 2, -1.0, 1.0).astype(f32)
    cos, sin = jnp.cos(angles), jnp.sin(angles) * signs[None, :]
    cos_here = lax.dynamic_slice_in_dim(cos, u * rows, rows)
    sin_here = lax.dynamic_slice_in_dim(sin, u * rows, rows)

    *pieces, normed = pl.pallas_call(
        functools.partial(proj_kernel, qkv_counts, groups),
        out_shape=[shape(rows, qw + 128)] * groups + [shape(rows, width)],
        in_specs=[SMEM] + [VMEM] * (3 + len(qkv_flat)),
        out_specs=[VMEM] * (groups + 1),
        scratch_shapes=[pltpu.VMEM((rows, columns), f32)],
        compiler_params=params(32),
        name="proj",
    )(me, token_rows, cos_here, sin_here, *qkv_flat)
    qkv_here = [pieces[0]] + [swap(pieces[j], "ulysses", j) for j in range(1, groups)]

    pieces = pl.pallas_call(
        functools.partial(d_attn_kernel, out_counts, groups),
        out_shape=[shape(rows, qw)] * groups,
        in_specs=[SMEM] + [VMEM] * (1 + len(out_flat)),
        out_specs=[VMEM] * groups,
        scratch_shapes=[pltpu.VMEM((rows, QW), f32)],
        compiler_params=params(32),
        name="d_attn",
    )(me, grad_rows, *out_flat)
    grads_here = [pieces[0]] + [swap(pieces[j], "ulysses", j) for j in range(1, groups)]

    slices = pl.pallas_call(
        functools.partial(slices_kernel, n, groups),
        out_shape=[shape(2 * kept, rows)] * n,
        in_specs=[SMEM] + [VMEM] * 2,
        out_specs=[VMEM] * n,
        scratch_shapes=[pltpu.VMEM((width, rows), bf16)],
        compiler_params=params(32),
        name="slices",
    )(me, normed, grad_rows)
    slices = [slices[0]] + [swap(slices[j], "dp", j) for j in range(1, n)]

    outs = pl.pallas_call(
        functools.partial(attend_kernel, groups),
        out_shape=[shape(rows, qw)] * groups + [shape(rows, qw + 128)] * groups,
        in_specs=[SMEM] + [VMEM] * (3 + 2 * groups),
        out_specs=[VMEM] * (2 * groups),
        scratch_shapes=[
            pltpu.VMEM((length, qw), bf16),
            pltpu.VMEM((length, 128), bf16),
            pltpu.VMEM((length, qw), bf16),
            pltpu.VMEM((length, qw), bf16),
            pltpu.VMEM((length, qw), f32),
            pltpu.VMEM((length, 128), f32),
            pltpu.VMEM((128, length), f32),
            pltpu.VMEM((heads * Q_BLOCK, DOC_MOST + Q_BLOCK), bf16),
            pltpu.VMEM((heads * Q_BLOCK, DOC_MOST + Q_BLOCK), bf16),
        ],
        compiler_params=params(40),
        name="attend",
    )(me, begins[:, None], cos, sin, *qkv_here, *grads_here)
    mixed, back = outs[:groups], outs[groups:]
    mixed = [mixed[0]] + [swap(mixed[j], "ulysses", j) for j in range(1, groups)]
    back = [back[0]] + [swap(back[j], "ulysses", j) for j in range(1, groups)]

    attn = pl.pallas_call(
        functools.partial(join_attn_kernel, groups),
        out_shape=shape(rows, QW),
        in_specs=[SMEM] + [VMEM] * groups,
        out_specs=VMEM,
        name="join_attn",
    )(me, *mixed)
    attn_flat, attn_counts = flat(gather_slots(attn, "dp", rows // 2))

    d_proj = pl.pallas_call(
        functools.partial(join_proj_kernel, groups),
        out_shape=shape(rows, columns),
        in_specs=[SMEM] + [VMEM] * groups,
        out_specs=VMEM,
        scratch_shapes=[pltpu.VMEM((rows, 128 * KV_HEADS), f32)],
        name="join_proj",
    )(me, *back)
    proj_flat, proj_counts = flat(gather_slots(d_proj, "dp", rows // 2))

    d_tokens, d_gain = pl.pallas_call(
        functools.partial(tokens_kernel, qkv_counts, groups, factor),
        out_shape=[shape(rows, width), shape(n, 1, kept, dtype=f32)],
        in_specs=[SMEM] + [VMEM] * (3 + len(qkv_flat)),
        out_specs=[VMEM] * 2,
        scratch_shapes=[pltpu.VMEM((rows, width), f32), pltpu.VMEM((1, width), f32)],
        compiler_params=params(40),
        name="d_tokens",
    )(me, token_rows, grad_rows, d_proj, *qkv_flat)
    gains = [d_gain[:1]] + [swap(d_gain[j : j + 1], "dp", j) for j in range(1, n)]

    d_w_out = pl.pallas_call(
        functools.partial(grads_kernel, attn_counts, 1, groups, factor, False),
        out_shape=shape(groups, block, QW, dtype=f32),
        in_specs=[VMEM] * (n + len(attn_flat)),
        out_specs=VMEM,
        scratch_shapes=[pltpu.VMEM((kept, QW), f32)],
        compiler_params=params(32),
        name="d_w_out",
    )(*slices, *attn_flat)
    d_w_out = chain_sum(d_w_out, "ulysses")

    d_w_qkv = pl.pallas_call(
        functools.partial(grads_kernel, proj_counts, 0, groups, factor, True),
        out_shape=shape(groups, block + 8, columns, dtype=f32),
        in_specs=[VMEM] * (n + len(proj_flat) + n),
        out_specs=VMEM,
        scratch_shapes=[pltpu.VMEM((kept, columns), f32)],
        compiler_params=params(32),
        name="d_w_qkv",
    )(*slices, *proj_flat, *gains)
    summed = chain_sum(d_w_qkv, "ulysses")
    return (d_tokens[None], summed[:block], d_w_out, summed[block, :block])


def solution(mesh):
    in_specs = (
        P("dp", "ulysses", None),
        P("dp", "ulysses", None),
        P("dp", None),
        P("dp"),
        P("dp", None),
        P("dp", None),
    )
    out_specs = (
        P("dp", "ulysses", None),
        P(("ulysses", "dp"), None),
        P(("ulysses", "dp"), None),
        P(("ulysses", "dp")),
    )
    return jax.shard_map(body, mesh=mesh, in_specs=in_specs, out_specs=out_specs, check_vma=False)
```

time: 598 us -> 358 us (0.60)
  waiting for transfers between devices: 350 us -> 142 us
  blocking collectives: 84.5 us -> 0 us
  starting transfers between devices: 4.96 us -> 81.3 us
  Pallas kernels: 0 us -> 53.9 us
  matrix products: 40.2 us -> 0 us
  between operations: 14.7 us -> 1.19 us
  local copies, waits for them, and re-layouts: 64.4 us -> 54.8 us
  other arithmetic: 29.8 us -> 23.3 us
    reduce_scatter x1 -> x0, waiting for transfers between devices: 158 us -> none  [body(): lax.psum_scatter(grad_qkv, ('ulysses', 'dp'), scatter_dimension=0, tiled=...]
    ppermute x0 -> x74, waiting for transfers between devices: none -> 142 us  [the longest x62 123 us: swap(): return lax.ppermute(a, axis, [(i, i ^ bit) for i in range(n)])]
    unnamed x5 -> x0, waiting for transfers between devices: 90.1 us -> none
    ppermute x0 -> x74, starting transfers between devices: none -> 81.3 us  [the longest x62 51.7 us: swap(): return lax.ppermute(a, axis, [(i, i ^ bit) for i in range(n)])]
    all_gather x2 -> x0, waiting for transfers between devices: 71.2 us -> none  [the longest x1 43.8 us: body(): lax.all_gather(w_qkv, 'dp', axis=0, tiled=True)]
    pallas_call x0 -> x9, Pallas kernels: none -> 53.9 us  [the longest x1 23.9 us: body(): pl.pallas_call(functools.partial(attend_kernel, groups), out_shape=[shape...]
    dot_general x17 -> x0, matrix products: 40.2 us -> none  [the longest x1 6.48 us: body(): jnp.einsum('td,tc->dc', normed, d_proj, preferred_element_type=jnp.float32)]
    unnamed x1 -> x0, blocking collectives: 40.1 us -> none
  transfers between devices with their start and end apart: 5 -> 74, of which waited for: 5 -> 25; matrix products, arithmetic and copies ran while one was open for 4% -> 10% of each run, Pallas kernels for 0% -> 8%
where the time goes in v1:
time: 358 us; the launch traced here: 356 us
  waiting for transfers between devices  142 us (40%)
  starting transfers between devices  81.3 us (23%)
  local copies, waits for them, and re-layouts  54.8 us (15%)
  Pallas kernels  53.9 us (15%)
  other arithmetic  23.3 us (7%)
    ppermute x62, waiting for transfers between devices, swap(): return lax.ppermute(a, axis, [(i, i ^ bit) for i in range(n)])  123 us
    ppermute x62, starting transfers between devices, swap(): return lax.ppermute(a, axis, [(i, i ^ bit) for i in range(n)])  51.7 us
    unnamed x142, local copies, waits for them, and re-layouts  38.6 us
    pallas_call x1, Pallas kernels, body(): pl.pallas_call(functools.partial(attend_kernel, groups), out_shape=[shape...  23.9 us
    ppermute x6, starting transfers between devices, chain_sum(): up = lax.ppermute(up, axis, [(i, i + 1) for i in range(step + 1)])  21.5 us
    ppermute x6, waiting for transfers between devices, chain_sum(): up = lax.ppermute(up, axis, [(i, i + 1) for i in range(step + 1)])  11.5 us
    ppermute x6, starting transfers between devices, chain_sum(): lax.ppermute(down, axis, [(n - 1 - i, n - 2 - i) for i in range(step + 1)])  8.13 us
    add x4, other arithmetic, chain_sum(): up = a if up is None else a + up  7.31 us
  transfers between devices with their start and end apart: 74, of which 25 were waited for; matrix products, arithmetic and copies ran while one was open for 10% of the time, Pallas kernels for 8%

profile of v1, /device:TPU:0, one launch (start us, length us, event | category | flops | bytes accessed | tf_op | source)
XLA Modules:
  0.0 356.3 jit_solution(2135439852135227327)
XLA Ops:
  0.6 3.0 collective-permute-start.13
  5.6 2.0 collective-permute-start.15
  7.7 9.0 %collective-permute-done.13.refs_2_ = bf16[256,1024]{1,0:T(8,128)(2,1)} collective-permute-done((bf16[256,1024]{1,0:T(8,128)(2,1)}, bf16[256,1024]{1,0:T(8,128)(2,1)}, u32[]{:S(2)}, u32[]{:S(2)}) %collective-permute-start.13) | collective-permute-done | bytes 524320 | tf_op jit(solution)/shard_map/ppermute | solution.py:49
  17.7 2.1 collective-permute-start.17
  22.5 2.0 collective-permute-start.18
  25.2 17.6 %collective-permute-done.17.refs_6_ = bf16[128,1024]{1,0:T(8,128)(2,1)} collective-permute-done((bf16[128,1024]{1,0:T(8,128)(2,1)S(1)}, bf16[128,1024]{1,0:T(8,128)(2,1)}, u32[]{:S(2)}, u32[]{:S(2)}) %collective-permute-start.17) | collective-permute-done | bytes 262176 | tf_op jit(solution)/shard_map/ppermute | solution.py:49
  56.3 3.7 %collective-permute-done.5.refs_6_ = bf16[128,1536]{1,0:T(8,128)(2,1)} collective-permute-done((bf16[128,1536]{1,0:T(8,128)(2,1)}, bf16[128,1536]{1,0:T(8,128)(2,1)}, u32[]{:S(2)}, u32[]{:S(2)}) %collective-permute-start.5) | collective-permute-done | bytes 393248 | tf_op jit(solution)/shard_map/ppermute | solution.py:49
  60.0 2.5 collective-permute-done.6.refs_7_
  65.7 2.6 fusion.2
  73.4 3.9 %d_attn.1 = (bf16[256,256]{1,0:T(8,128)(2,1)S(1)}, bf16[256,256]{1,0:T(8,128)(2,1)S(1)}, bf16[256,256]{1,0:T(8,128)(2,1)}, bf16[256,256]{1,0:T(8,128)(2,1)}) custom-call(s32[2]{0:T(128)S(1)} %copy-done.53, bf16[256,2048]{1,0:T(8,128)(2,1)S(1)} %bitcast.42, bf16[256,1024]{1,0:T(8,128)(2,1)S(1)} %copy-done.30, bf16[256,1024]{1,0:T(8,128)(2,1)S(1)} %copy-done.32, ...), custom_call_target="tpu_custom_call" | custom-call | tf_op jit(solution)/shard_map/d_attn/pallas_call | solution.py:404
  79.0 6.1 %proj.1 = (bf16[256,384]{1,0:T(8,128)(2,1)S(1)}, bf16[256,384]{1,0:T(8,128)(2,1)}, bf16[256,384]{1,0:T(8,128)(2,1)}, bf16[256,384]{1,0:T(8,128)(2,1)}, bf16[256,2048]{1,0:T(8,128)(2,1)S(1)}) custom-call(s32[2]{0:T(128)S(1)} %copy-done.54, bf16[256,2048]{1,0:T(8,128)(2,1)S(1)} %bitcast.45, f32[256,128]{1,0:T(8,128)S(1)} %get-tuple-element.77.cos_ref, ...), custom_call_target="tpu_custom_call" | custom-call | tf_op jit(solution)/shard_map/proj/pallas_call | solution.py:393
  87.2 2.6 collective-permute-start.10
  96.1 21.2 %collective-permute-done.22.refs_6_ = bf16[256,256]{1,0:T(8,128)(2,1)} collective-permute-done((bf16[256,256]{1,0:T(8,128)(2,1)}, bf16[256,256]{1,0:T(8,128)(2,1)}, u32[]{:S(2)}, u32[]{:S(2)}) %collective-permute-start.22) | collective-permute-done | bytes 131104 | tf_op jit(solution)/shard_map/ppermute | solution.py:49
  123.8 23.9 %attend.1 = (bf16[256,256]{1,0:T(8,128)(2,1)S(1)}, bf16[256,256]{1,0:T(8,128)(2,1)S(1)}, bf16[256,256]{1,0:T(8,128)(2,1)S(1)}, bf16[256,256]{1,0:T(8,128)(2,1)S(...) custom-call(s32[2]{0:T(128)S(1)} %copy-done.55, ...), custom_call_target="tpu_custom_call" | custom-call | tf_op jit(solution)/shard_map/attend/pallas_call | solution.py:426
  149.1 2.7 collective-permute-start.56
  151.8 1.9 collective-permute-start.57
  155.1 1.9 slices.1
  160.6 4.0 %collective-permute-done.57.refs_2_ = bf16[256,256]{1,0:T(8,128)(2,1)S(1)} collective-permute-done((bf16[256,256]{1,0:T(8,128)(2,1)S(1)}, bf16[256,256]{1,0:T(8,128)(2,1)S(1)}, u32[]{:S(2)}, u32[]{:S(2)}) %collective-permute-start.57) | collective-permute-done | bytes 131104 | tf_op jit(solution)/shard_map/ppermute | solution.py:49
  165.9 2.0 join_attn.1.refs_8_
  174.3 2.6 collective-permute-done.24.refs_1_
  177.5 9.6 %collective-permute-done.25.refs_2_ = bf16[256,384]{1,0:T(8,128)(2,1)} collective-permute-done((bf16[256,384]{1,0:T(8,128)(2,1)}, bf16[256,384]{1,0:T(8,128)(2,1)}, u32[]{:S(2)}, u32[]{:S(2)}) %collective-permute-start.25) | collective-permute-done | bytes 196640 | tf_op jit(solution)/shard_map/ppermute | solution.py:49
  187.7 2.4 join_proj.1.d_proj_ref.refs_8_
  191.7 3.5 collective-permute-done.29.refs_3_
  203.1 18.3 %collective-permute-done.32.refs_6_ = bf16[512,256]{1,0:T(8,128)(2,1)S(1)} collective-permute-done((bf16[512,256]{1,0:T(8,128)(2,1)}, bf16[512,256]{1,0:T(8,128)(2,1)S(1)}, u32[]{:S(2)}, u32[]{:S(2)}) %collective-permute-start.32) | collective-permute-done | bytes 262176 | tf_op jit(solution)/shard_map/ppermute | solution.py:49
  224.3 6.2 %d_tokens.1 = (bf16[256,2048]{1,0:T(8,128)(2,1)}, f32[8,1,256]{2,1,0:T(1,128)S(1)}) custom-call(s32[2]{0:T(128)S(1)} %copy-done.56, bf16[256,2048]{1,0:T(8,128)(2,1)S(1)} %bitcast.46, bf16[256,2048]{1,0:T(8,128)(2,1)S(1)} %bitcast.44, bf16[256,1536]{1,0:T(8,128)(2,1)} %join_proj.1.d_proj_ref.refs_8_, bf16[272,1536]{1,0:T(8,128)(2,1)S(1)} %fusion.1.refs_0_, ...), custom_call_target="tpu_custom_call" | custom-call | tf_op jit(solution)/shard_map/d_tokens/pallas_call | solution.py:468
  232.4 2.9 collective-permute-done.44.refs_20_
  235.4 3.0 collective-permute-done.45.refs_21_
  239.9 2.0 collective-permute-done.46.refs_22_
  241.9 3.0 collective-permute-done.47.refs_23_
  246.5 2.9 collective-permute-done.48.refs_24_
  249.4 3.9 %collective-permute-done.49.refs_25_ = f32[1,1,256]{2,1,0:T(1,128)S(1)} collective-permute-done((f32[1,1,256]{2,1,0:T(1,128)S(1)}, f32[1,1,256]{2,1,0:T(1,128)S(1)}, u32[]{:S(2)}, u32[]{:S(2)}) %collective-permute-start.49) | collective-permute-done | bytes 1056 | tf_op jit(solution)/shard_map/ppermute | solution.py:49
  263.4 6.2 %collective-permute-done.39.refs_14_ = bf16[128,1536]{1,0:T(8,128)(2,1)} collective-permute-done((bf16[128,1536]{1,0:T(8,128)(2,1)S(1)}, bf16[128,1536]{1,0:T(8,128)(2,1)}, u32[]{:S(2)}, u32[]{:S(2)}) %collective-permute-start.39) | collective-permute-done | bytes 393248 | tf_op jit(solution)/shard_map/ppermute | solution.py:49
  269.6 4.3 %collective-permute-done.40.refs_15_ = bf16[128,1536]{1,0:T(8,128)(2,1)} collective-permute-done((bf16[128,1536]{1,0:T(8,128)(2,1)S(1)}, bf16[128,1536]{1,0:T(8,128)(2,1)}, u32[]{:S(2)}, u32[]{:S(2)}) %collective-permute-start.40) | collective-permute-done | bytes 393248 | tf_op jit(solution)/shard_map/ppermute | solution.py:49
  281.8 2.8 d_w_out.1
  286.4 2.0 collective-permute-start.68
  289.6 4.6 %d_w_qkv.1 = f32[4,72,1536]{2,1,0:T(8,128)S(1)} custom-call(bf16[512,256]{1,0:T(8,128)(2,1)S(1)} %copy-done.11, bf16[512,256]{1,0:T(8,128)(2,1)} %collective-permute-done.27.refs_1_, bf16[512,256]{1,0:T(8,128)(2,1)} %collective-permute-done.28.refs_2_, bf16[512,256]{1,0:T(8,128)(2,1)} %collective-permute-done.29.refs_3_, ...), custom_call_target="tpu_custom_call" | custom-call | tf_op jit(solution)/shard_map/d_w_qkv/pallas_call | solution.py:490
  295.1 2.0 collective-permute-start.50
  300.2 2.0 collective-permute-start.69
  303.6 3.6 %collective-permute-done.50 = f32[72,1536]{1,0:T(8,128)} collective-permute-done((f32[72,1536]{1,0:T(8,128)}, f32[72,1536]{1,0:T(8,128)}, u32[]{:S(2)}, u32[]{:S(2)}) %collective-permute-start.50) | collective-permute-done | bytes 442400 | tf_op jit(solution)/shard_map/ppermute | solution.py:352
  307.2 1.8 bitcast_add_fusion.2
  309.1 5.1 %collective-permute-start.51 = (f32[72,1536]{1,0:T(8,128)}, f32[72,1536]{1,0:T(8,128)}, u32[]{:S(2)}, u32[]{:S(2)}) collective-permute-start(f32[72,1536]{1,0:T(8,128)} %bitcast_add_fusion.2), channel_id=1, source_target_pairs={{0,8},{8,16},{1,9},{9,17},{2,10},{10,18},{3,11},{11,19},{4,12},{12... | collective-permute-start | bytes 1327112 | tf_op jit(solution)/shard_map/ppermute | solution.py:352
  317.4 5.7 %collective-permute-done.51 = f32[72,1536]{1,0:T(8,128)} collective-permute-done((f32[72,1536]{1,0:T(8,128)}, f32[72,1536]{1,0:T(8,128)}, u32[]{:S(2)}, u32[]{:S(2)}) %collective-permute-start.51) | collective-permute-done | bytes 442400 | tf_op jit(solution)/shard_map/ppermute | solution.py:352
  323.1 2.0 bitcast_add_fusion.3
  326.5 5.0 %collective-permute-start.70 = (f32[64,1024]{1,0:T(8,128)S(1)}, f32[64,1024]{1,0:T(8,128)}, u32[]{:S(2)}, u32[]{:S(2)}) collective-permute-start(f32[64,1024]{1,0:T(8,128)S(1)} %get-tuple-element.62), channel_id=1, source_target_pairs={{0,8},{8,16},{16,24},{1,9},{9,17},{17,25},{2,10},{10,18},{18,26},{... | collective-permute-start | bytes 786440 | tf_op jit(solution)/shard_map/ppermute | solution.py:352
  334.4 5.3 %collective-permute-start.52 = (f32[72,1536]{1,0:T(8,128)S(1)}, f32[72,1536]{1,0:T(8,128)}, u32[]{:S(2)}, u32[]{:S(2)}) collective-permute-start(f32[72,1536]{1,0:T(8,128)S(1)} %get-tuple-element.58), channel_id=1, source_target_pairs={{0,8},{8,16},{16,24},{1,9},{9,17},{17,25},{2,10},{10,18},{18,26},{... | collective-permute-start | bytes 1327112 | tf_op jit(solution)/shard_map/ppermute | solution.py:352
  339.8 1.8 bitcast_add_fusion.1
  344.7 2.2 collective-permute-done.52
  346.8 7.0 %collective-permute-done.55 = f32[72,1536]{1,0:T(8,128)} collective-permute-done((f32[72,1536]{1,0:T(8,128)}, f32[72,1536]{1,0:T(8,128)}, u32[]{:S(2)}, u32[]{:S(2)}) %collective-permute-start.55) | collective-permute-done | bytes 442400 | tf_op jit(solution)/shard_map/ppermute | solution.py:353
  (286 shorter events, 116.2 us)
Async XLA Ops:
  0.6 16.1 %collective-permute-start.13 = (bf16[256,1024]{1,0:T(8,128)(2,1)}, bf16[256,1024]{1,0:T(8,128)(2,1)}, u32[]{:S(2)}, u32[]{:S(2)}) collective-permute-start(bf16[256,1024]{1,0:T(8,128)(2,1)} %refs_0_.1), channel_id=1, source_target_pairs={{0,2},{1,3},{2,0},{3,1},{4,6},{5,7},{6,4},{7,5},{8,10},{9,11},{10,... | collective-permute-start | bytes 1572872 | tf_op jit(solution)/shard_map/ppermute | solution.py:49
  5.5 39.2 %collective-permute-start.1 = (bf16[272,1536]{1,0:T(8,128)(2,1)S(1)}, bf16[272,1536]{1,0:T(8,128)(2,1)S(1)}, u32[]{:S(2)}, u32[]{:S(2)}) collective-permute-start(bf16[272,1536]{1,0:T(8,128)(2,1)S(1)} %fusion.1.refs_0_), channel_id=1, source_target_pairs={{0,2},{1,3},{2,0},{3,1},{4,6},{5,7},{6,4},{7,5},{8,10},{9,11},{10,... | collective-permute-start | bytes 2506760 | tf_op jit(solution)/shard_map/ppermute | solution.py:49
  5.6 15.2 %collective-permute-start.15 = (bf16[256,1024]{1,0:T(8,128)(2,1)}, bf16[256,1024]{1,0:T(8,128)(2,1)}, u32[]{:S(2)}, u32[]{:S(2)}) collective-permute-start(bf16[256,1024]{1,0:T(8,128)(2,1)} %refs_0_.1), channel_id=1, source_target_pairs={{0,4},{1,5},{2,6},{3,7},{4,0},{5,1},{6,2},{7,3},{8,12},{9,13},{10,... | collective-permute-start | bytes 1572872 | tf_op jit(solution)/shard_map/ppermute | solution.py:49
  7.6 16.8 %collective-permute-start.12 = (bf16[256,1024]{1,0:T(8,128)(2,1)}, bf16[256,1024]{1,0:T(8,128)(2,1)S(1)}, u32[]{:S(2)}, u32[]{:S(2)}) collective-permute-start(bf16[256,1024]{1,0:T(8,128)(2,1)} %refs_0_.1), channel_id=1, source_target_pairs={{0,1},{1,0},{2,3},{3,2},{4,5},{5,4},{6,7},{7,6},{8,9},{9,8},{10,11... | collective-permute-start | bytes 1572872 | tf_op jit(solution)/shard_map/ppermute | solution.py:49
  7.6 38.4 %collective-permute-start.3 = (bf16[272,1536]{1,0:T(8,128)(2,1)S(1)}, bf16[272,1536]{1,0:T(8,128)(2,1)S(1)}, u32[]{:S(2)}, u32[]{:S(2)}) collective-permute-start(bf16[272,1536]{1,0:T(8,128)(2,1)S(1)} %fusion.1.refs_0_), channel_id=1, source_target_pairs={{0,4},{1,5},{2,6},{3,7},{4,0},{5,1},{6,2},{7,3},{8,12},{9,13},{10,... | collective-permute-start | bytes 2506760 | tf_op jit(solution)/shard_map/ppermute | solution.py:49
  17.7 25.2 %collective-permute-start.17 = (bf16[128,1024]{1,0:T(8,128)(2,1)S(1)}, bf16[128,1024]{1,0:T(8,128)(2,1)}, u32[]{:S(2)}, u32[]{:S(2)}) collective-permute-start(bf16[128,1024]{1,0:T(8,128)(2,1)S(1)} %slice.74), channel_id=1, source_target_pairs={{0,4},{1,5},{2,6},{3,7},{4,0},{5,1},{6,2},{7,3},{8,12},{9,13},{10,... | collective-permute-start | bytes 786440 | tf_op jit(solution)/shard_map/ppermute | solution.py:49
  22.5 21.7 %collective-permute-start.18 = (bf16[128,1024]{1,0:T(8,128)(2,1)}, bf16[128,1024]{1,0:T(8,128)(2,1)}, u32[]{:S(2)}, u32[]{:S(2)}) collective-permute-start(bf16[128,1024]{1,0:T(8,128)(2,1)} %slice.75), channel_id=1, source_target_pairs={{0,2},{1,3},{2,0},{3,1},{4,6},{5,7},{6,4},{7,5},{8,10},{9,11},{10,... | collective-permute-start | bytes 786440 | tf_op jit(solution)/shard_map/ppermute | solution.py:49
  25.2 23.4 %collective-permute-start.14 = (bf16[256,1024]{1,0:T(8,128)(2,1)}, bf16[256,1024]{1,0:T(8,128)(2,1)}, u32[]{:S(2)}, u32[]{:S(2)}) collective-permute-start(bf16[256,1024]{1,0:T(8,128)(2,1)} %collective-permute-done.13.refs_2_), channel_id=1, source_target_pairs={{0,1},{1,0},{2,3},{3,2},{4,5},{5,4},{6,7},{7,6},{8,9},{9,8},{10,11... | collective-permute-start | bytes 1572872 | tf_op jit(solution)/shard_map/ppermute | solution.py:49
  46.0 31.2 %collective-permute-start = (bf16[272,1536]{1,0:T(8,128)(2,1)S(1)}, bf16[272,1536]{1,0:T(8,128)(2,1)}, u32[]{:S(2)}, u32[]{:S(2)}) collective-permute-start(bf16[272,1536]{1,0:T(8,128)(2,1)S(1)} %fusion.1.refs_0_), channel_id=1, source_target_pairs={{0,1},{1,0},{2,3},{3,2},{4,5},{5,4},{6,7},{7,6},{8,9},{9,8},{10,11... | collective-permute-start | bytes 2506760 | tf_op jit(solution)/shard_map/ppermute | solution.py:49
  50.3 12.2 %collective-permute-start.6 = (bf16[144,1536]{1,0:T(8,128)(2,1)}, bf16[144,1536]{1,0:T(8,128)(2,1)}, u32[]{:S(2)}, u32[]{:S(2)}) collective-permute-start(bf16[144,1536]{1,0:T(8,128)(2,1)} %slice.73), channel_id=1, source_target_pairs={{0,2},{1,3},{2,0},{3,1},{4,6},{5,7},{6,4},{7,5},{8,10},{9,11},{10,... | collective-permute-start | bytes 1327112 | tf_op jit(solution)/shard_map/ppermute | solution.py:49
  52.5 26.4 %collective-permute-start.2 = (bf16[272,1536]{1,0:T(8,128)(2,1)S(1)}, bf16[272,1536]{1,0:T(8,128)(2,1)}, u32[]{:S(2)}, u32[]{:S(2)}) collective-permute-start(bf16[272,1536]{1,0:T(8,128)(2,1)S(1)} %collective-permute-done.1.refs_2_), channel_id=1, source_target_pairs={{0,1},{1,0},{2,3},{3,2},{4,5},{5,4},{6,7},{7,6},{8,9},{9,8},{10,11... | collective-permute-start | bytes 2506760 | tf_op jit(solution)/shard_map/ppermute | solution.py:49
  53.2 25.7 %collective-permute-start.4 = (bf16[272,1536]{1,0:T(8,128)(2,1)S(1)}, bf16[272,1536]{1,0:T(8,128)(2,1)}, u32[]{:S(2)}, u32[]{:S(2)}) collective-permute-start(bf16[272,1536]{1,0:T(8,128)(2,1)S(1)} %collective-permute-done.3.refs_4_), channel_id=1, source_target_pairs={{0,1},{1,0},{2,3},{3,2},{4,5},{5,4},{6,7},{7,6},{8,9},{9,8},{10,11... | collective-permute-start | bytes 2506760 | tf_op jit(solution)/shard_map/ppermute | solution.py:49
  60.0 18.9 %collective-permute-start.7 = (bf16[128,1536]{1,0:T(8,128)(2,1)}, bf16[128,1536]{1,0:T(8,128)(2,1)}, u32[]{:S(2)}, u32[]{:S(2)}) collective-permute-start(bf16[128,1536]{1,0:T(8,128)(2,1)} %collective-permute-done.5.refs_6_), channel_id=1, source_target_pairs={{0,1},{1,0},{2,3},{3,2},{4,5},{5,4},{6,7},{7,6},{8,9},{9,8},{10,11... | collective-permute-start | bytes 1179656 | tf_op jit(solution)/shard_map/ppermute | solution.py:49
  62.5 16.4 %collective-permute-start.8 = (bf16[144,1536]{1,0:T(8,128)(2,1)}, bf16[144,1536]{1,0:T(8,128)(2,1)}, u32[]{:S(2)}, u32[]{:S(2)}) collective-permute-start(bf16[144,1536]{1,0:T(8,128)(2,1)} %collective-permute-done.6.refs_7_), channel_id=1, source_target_pairs={{0,1},{1,0},{2,3},{3,2},{4,5},{5,4},{6,7},{7,6},{8,9},{9,8},{10,11... | collective-permute-start | bytes 1327112 | tf_op jit(solution)/shard_map/ppermute | solution.py:49
  77.2 15.6 %collective-permute-start.21 = (bf16[256,256]{1,0:T(8,128)(2,1)S(1)}, bf16[256,256]{1,0:T(8,128)(2,1)S(1)}, u32[]{:S(2)}, u32[]{:S(2)}) collective-permute-start(bf16[256,256]{1,0:T(8,128)(2,1)S(1)} %get-tuple-element.36), channel_id=1, source_target_pairs={{0,8},{8,0},{16,24},{24,16},{1,9},{9,1},{17,25},{25,17},{2,10},{10... | collective-permute-start | bytes 393224 | tf_op jit(solution)/shard_map/ppermute | solution.py:49
  86.7 30.5 %collective-permute-start.9 = (bf16[256,384]{1,0:T(8,128)(2,1)}, bf16[256,384]{1,0:T(8,128)(2,1)}, u32[]{:S(2)}, u32[]{:S(2)}) collective-permute-start(bf16[256,384]{1,0:T(8,128)(2,1)} %get-tuple-element.32), channel_id=1, source_target_pairs={{0,8},{8,0},{16,24},{24,16},{1,9},{9,1},{17,25},{25,17},{2,10},{10... | collective-permute-start | bytes 589832 | tf_op jit(solution)/shard_map/ppermute | solution.py:49
  87.2 30.1 %collective-permute-start.10 = (bf16[256,384]{1,0:T(8,128)(2,1)}, bf16[256,384]{1,0:T(8,128)(2,1)}, u32[]{:S(2)}, u32[]{:S(2)}) collective-permute-start(bf16[256,384]{1,0:T(8,128)(2,1)} %get-tuple-element.33), channel_id=1, source_target_pairs={{0,16},{8,24},{16,0},{24,8},{1,17},{9,25},{17,1},{25,9},{2,18},{10... | collective-permute-start | bytes 589832 | tf_op jit(solution)/shard_map/ppermute | solution.py:49
  89.8 27.5 %collective-permute-start.11 = (bf16[256,384]{1,0:T(8,128)(2,1)}, bf16[256,384]{1,0:T(8,128)(2,1)}, u32[]{:S(2)}, u32[]{:S(2)}) collective-permute-start(bf16[256,384]{1,0:T(8,128)(2,1)} %get-tuple-element.34), channel_id=1, source_target_pairs={{0,24},{8,16},{16,8},{24,0},{1,25},{9,17},{17,9},{25,1},{2,26},{10... | collective-permute-start | bytes 589832 | tf_op jit(solution)/shard_map/ppermute | solution.py:49
  91.1 26.1 %collective-permute-start.22 = (bf16[256,256]{1,0:T(8,128)(2,1)}, bf16[256,256]{1,0:T(8,128)(2,1)}, u32[]{:S(2)}, u32[]{:S(2)}) collective-permute-start(bf16[256,256]{1,0:T(8,128)(2,1)} %get-tuple-element.37), channel_id=1, source_target_pairs={{0,16},{8,24},{16,0},{24,8},{1,17},{9,25},{17,1},{25,9},{2,18},{10... | collective-permute-start | bytes 393224 | tf_op jit(solution)/shard_map/ppermute | solution.py:49
  93.5 23.8 %collective-permute-start.23 = (bf16[256,256]{1,0:T(8,128)(2,1)}, bf16[256,256]{1,0:T(8,128)(2,1)}, u32[]{:S(2)}, u32[]{:S(2)}) collective-permute-start(bf16[256,256]{1,0:T(8,128)(2,1)} %get-tuple-element.38), channel_id=1, source_target_pairs={{0,24},{8,16},{16,8},{24,0},{1,25},{9,17},{17,9},{25,1},{2,26},{10... | collective-permute-start | bytes 393224 | tf_op jit(solution)/shard_map/ppermute | solution.py:49
  151.8 12.8 %collective-permute-start.57 = (bf16[256,256]{1,0:T(8,128)(2,1)S(1)}, bf16[256,256]{1,0:T(8,128)(2,1)S(1)}, u32[]{:S(2)}, u32[]{:S(2)}) collective-permute-start(bf16[256,256]{1,0:T(8,128)(2,1)S(1)} %get-tuple-element.56), channel_id=1, source_target_pairs={{0,16},{8,24},{16,0},{24,8},{1,17},{9,25},{17,1},{25,9},{2,18},{10... | collective-permute-start | bytes 393224 | tf_op jit(solution)/shard_map/ppermute | solution.py:49
  159.8 13.9 %collective-permute-start.27 = (bf16[512,256]{1,0:T(8,128)(2,1)}, bf16[512,256]{1,0:T(8,128)(2,1)}, u32[]{:S(2)}, u32[]{:S(2)}) collective-permute-start(bf16[512,256]{1,0:T(8,128)(2,1)} %get-tuple-element.46), channel_id=1, source_target_pairs={{0,1},{1,0},{2,3},{3,2},{4,5},{5,4},{6,7},{7,6},{8,9},{9,8},{10,11... | collective-permute-start | bytes 786440 | tf_op jit(solution)/shard_map/ppermute | solution.py:49
  167.9 29.2 %collective-permute-start.60 = (bf16[256,1024]{1,0:T(8,128)(2,1)}, bf16[256,1024]{1,0:T(8,128)(2,1)}, u32[]{:S(2)}, u32[]{:S(2)}) collective-permute-start(bf16[256,1024]{1,0:T(8,128)(2,1)} %join_attn.1.refs_8_), channel_id=1, source_target_pairs={{0,2},{1,3},{2,0},{3,1},{4,6},{5,7},{6,4},{7,5},{8,10},{9,11},{10,... | collective-permute-start | bytes 1572872 | tf_op jit(solution)/shard_map/ppermute | solution.py:49
  170.7 16.4 %collective-permute-start.25 = (bf16[256,384]{1,0:T(8,128)(2,1)}, bf16[256,384]{1,0:T(8,128)(2,1)}, u32[]{:S(2)}, u32[]{:S(2)}) collective-permute-start(bf16[256,384]{1,0:T(8,128)(2,1)} %copy-done.64), channel_id=1, source_target_pairs={{0,16},{8,24},{16,0},{24,8},{1,17},{9,25},{17,1},{25,9},{2,18},{10... | collective-permute-start | bytes 589832 | tf_op jit(solution)/shard_map/ppermute | solution.py:49
  172.2 14.9 %collective-permute-start.26 = (bf16[256,384]{1,0:T(8,128)(2,1)}, bf16[256,384]{1,0:T(8,128)(2,1)}, u32[]{:S(2)}, u32[]{:S(2)}) collective-permute-start(bf16[256,384]{1,0:T(8,128)(2,1)} %copy-done.63), channel_id=1, source_target_pairs={{0,24},{8,16},{16,8},{24,0},{1,25},{9,17},{17,9},{25,1},{2,26},{10... | collective-permute-start | bytes 589832 | tf_op jit(solution)/shard_map/ppermute | solution.py:49
  173.8 24.9 %collective-permute-start.62 = (bf16[256,1024]{1,0:T(8,128)(2,1)}, bf16[256,1024]{1,0:T(8,128)(2,1)}, u32[]{:S(2)}, u32[]{:S(2)}) collective-permute-start(bf16[256,1024]{1,0:T(8,128)(2,1)} %join_attn.1.refs_8_), channel_id=1, source_target_pairs={{0,4},{1,5},{2,6},{3,7},{4,0},{5,1},{6,2},{7,3},{8,12},{9,13},{10,... | collective-permute-start | bytes 1572872 | tf_op jit(solution)/shard_map/ppermute | solution.py:49
  176.9 13.2 %collective-permute-start.28 = (bf16[512,256]{1,0:T(8,128)(2,1)}, bf16[512,256]{1,0:T(8,128)(2,1)}, u32[]{:S(2)}, u32[]{:S(2)}) collective-permute-start(bf16[512,256]{1,0:T(8,128)(2,1)} %copy-done.62), channel_id=1, source_target_pairs={{0,2},{1,3},{2,0},{3,1},{4,6},{5,7},{6,4},{7,5},{8,10},{9,11},{10,... | collective-permute-start | bytes 786440 | tf_op jit(solution)/shard_map/ppermute | solution.py:49
  195.2 58.7 %collective-permute-start.35 = (bf16[256,1536]{1,0:T(8,128)(2,1)}, bf16[256,1536]{1,0:T(8,128)(2,1)}, u32[]{:S(2)}, u32[]{:S(2)}) collective-permute-start(bf16[256,1536]{1,0:T(8,128)(2,1)} %join_proj.1.d_proj_ref.refs_8_), channel_id=1, source_target_pairs={{0,2},{1,3},{2,0},{3,1},{4,6},{5,7},{6,4},{7,5},{8,10},{9,11},{10,... | collective-permute-start | bytes 2359304 | tf_op jit(solution)/shard_map/ppermute | solution.py:49
  196.6 57.7 %collective-permute-start.37 = (bf16[256,1536]{1,0:T(8,128)(2,1)}, bf16[256,1536]{1,0:T(8,128)(2,1)}, u32[]{:S(2)}, u32[]{:S(2)}) collective-permute-start(bf16[256,1536]{1,0:T(8,128)(2,1)} %join_proj.1.d_proj_ref.refs_8_), channel_id=1, source_target_pairs={{0,4},{1,5},{2,6},{3,7},{4,0},{5,1},{6,2},{7,3},{8,12},{9,13},{10,... | collective-permute-start | bytes 2359304 | tf_op jit(solution)/shard_map/ppermute | solution.py:49
  197.2 24.3 %collective-permute-start.32 = (bf16[512,256]{1,0:T(8,128)(2,1)}, bf16[512,256]{1,0:T(8,128)(2,1)S(1)}, u32[]{:S(2)}, u32[]{:S(2)}) collective-permute-start(bf16[512,256]{1,0:T(8,128)(2,1)} %copy-done.58), channel_id=1, source_target_pairs={{0,6},{1,7},{2,4},{3,5},{4,2},{5,3},{6,0},{7,1},{8,14},{9,15},{10,... | collective-permute-start | bytes 786440 | tf_op jit(solution)/shard_map/ppermute | solution.py:49
  198.7 31.9 %collective-permute-start.33 = (bf16[512,256]{1,0:T(8,128)(2,1)}, bf16[512,256]{1,0:T(8,128)(2,1)S(1)}, u32[]{:S(2)}, u32[]{:S(2)}) collective-permute-start(bf16[512,256]{1,0:T(8,128)(2,1)} %copy-done.57), channel_id=1, source_target_pairs={{0,7},{1,6},{2,5},{3,4},{4,3},{5,2},{6,1},{7,0},{8,15},{9,14},{10,... | collective-permute-start | bytes 786440 | tf_op jit(solution)/shard_map/ppermute | solution.py:49
  202.3 51.0 %collective-permute-start.64 = (bf16[128,1024]{1,0:T(8,128)(2,1)S(1)}, bf16[128,1024]{1,0:T(8,128)(2,1)S(1)}, u32[]{:S(2)}, u32[]{:S(2)}) collective-permute-start(bf16[128,1024]{1,0:T(8,128)(2,1)S(1)} %slice.79), channel_id=1, source_target_pairs={{0,4},{1,5},{2,6},{3,7},{4,0},{5,1},{6,2},{7,3},{8,12},{9,13},{10,... | collective-permute-start | bytes 786440 | tf_op jit(solution)/shard_map/ppermute | solution.py:49
  222.2 31.6 %collective-permute-start.65 = (bf16[128,1024]{1,0:T(8,128)(2,1)S(1)}, bf16[128,1024]{1,0:T(8,128)(2,1)S(1)}, u32[]{:S(2)}, u32[]{:S(2)}) collective-permute-start(bf16[128,1024]{1,0:T(8,128)(2,1)S(1)} %slice.80), channel_id=1, source_target_pairs={{0,2},{1,3},{2,0},{3,1},{4,6},{5,7},{6,4},{7,5},{8,10},{9,11},{10,... | collective-permute-start | bytes 786440 | tf_op jit(solution)/shard_map/ppermute | solution.py:49
  257.3 28.2 %collective-permute-start.34 = (bf16[256,1536]{1,0:T(8,128)(2,1)}, bf16[256,1536]{1,0:T(8,128)(2,1)S(1)}, u32[]{:S(2)}, u32[]{:S(2)}) collective-permute-start(bf16[256,1536]{1,0:T(8,128)(2,1)} %join_proj.1.d_proj_ref.refs_8_), channel_id=1, source_target_pairs={{0,1},{1,0},{2,3},{3,2},{4,5},{5,4},{6,7},{7,6},{8,9},{9,8},{10,11... | collective-permute-start | bytes 2359304 | tf_op jit(solution)/shard_map/ppermute | solution.py:49
  260.6 27.8 %collective-permute-start.36 = (bf16[256,1536]{1,0:T(8,128)(2,1)}, bf16[256,1536]{1,0:T(8,128)(2,1)}, u32[]{:S(2)}, u32[]{:S(2)}) collective-permute-start(bf16[256,1536]{1,0:T(8,128)(2,1)} %collective-permute-done.35.refs_10_), channel_id=1, source_target_pairs={{0,1},{1,0},{2,3},{3,2},{4,5},{5,4},{6,7},{7,6},{8,9},{9,8},{10,11... | collective-permute-start | bytes 2359304 | tf_op jit(solution)/shard_map/ppermute | solution.py:49
  261.4 27.0 %collective-permute-start.38 = (bf16[256,1536]{1,0:T(8,128)(2,1)}, bf16[256,1536]{1,0:T(8,128)(2,1)}, u32[]{:S(2)}, u32[]{:S(2)}) collective-permute-start(bf16[256,1536]{1,0:T(8,128)(2,1)} %collective-permute-done.37.refs_12_), channel_id=1, source_target_pairs={{0,1},{1,0},{2,3},{3,2},{4,5},{5,4},{6,7},{7,6},{8,9},{9,8},{10,11... | collective-permute-start | bytes 2359304 | tf_op jit(solution)/shard_map/ppermute | solution.py:49
  269.6 18.8 %collective-permute-start.41 = (bf16[128,1536]{1,0:T(8,128)(2,1)}, bf16[128,1536]{1,0:T(8,128)(2,1)}, u32[]{:S(2)}, u32[]{:S(2)}) collective-permute-start(bf16[128,1536]{1,0:T(8,128)(2,1)} %collective-permute-done.39.refs_14_), channel_id=1, source_target_pairs={{0,1},{1,0},{2,3},{3,2},{4,5},{5,4},{6,7},{7,6},{8,9},{9,8},{10,11... | collective-permute-start | bytes 1179656 | tf_op jit(solution)/shard_map/ppermute | solution.py:49
  273.9 14.5 %collective-permute-start.42 = (bf16[128,1536]{1,0:T(8,128)(2,1)}, bf16[128,1536]{1,0:T(8,128)(2,1)}, u32[]{:S(2)}, u32[]{:S(2)}) collective-permute-start(bf16[128,1536]{1,0:T(8,128)(2,1)} %collective-permute-done.40.refs_15_), channel_id=1, source_target_pairs={{0,1},{1,0},{2,3},{3,2},{4,5},{5,4},{6,7},{7,6},{8,9},{9,8},{10,11... | collective-permute-start | bytes 1179656 | tf_op jit(solution)/shard_map/ppermute | solution.py:49
  295.1 12.1 %collective-permute-start.50 = (f32[72,1536]{1,0:T(8,128)}, f32[72,1536]{1,0:T(8,128)}, u32[]{:S(2)}, u32[]{:S(2)}) collective-permute-start(f32[72,1536]{1,0:T(8,128)} %get-tuple-element.60), channel_id=1, source_target_pairs={{0,8},{1,9},{2,10},{3,11},{4,12},{5,13},{6,14},{7,15}} | collective-permute-start | bytes 1327112 | tf_op jit(solution)/shard_map/ppermute | solution.py:352
  297.1 17.1 %collective-permute-start.71 = (f32[64,1024]{1,0:T(8,128)S(1)}, f32[64,1024]{1,0:T(8,128)}, u32[]{:S(2)}, u32[]{:S(2)}) collective-permute-start(f32[64,1024]{1,0:T(8,128)S(1)} %copy-done.66), channel_id=1, source_target_pairs={{24,16},{25,17},{26,18},{27,19},{28,20},{29,21},{30,22},{31,23}} | collective-permute-start | bytes 786440 | tf_op jit(solution)/shard_map/ppermute | solution.py:353
  300.2 14.0 %collective-permute-start.69 = (f32[64,1024]{1,0:T(8,128)}, f32[64,1024]{1,0:T(8,128)}, u32[]{:S(2)}, u32[]{:S(2)}) collective-permute-start(f32[64,1024]{1,0:T(8,128)} %bitcast_add_fusion.7), channel_id=1, source_target_pairs={{0,8},{8,16},{1,9},{9,17},{2,10},{10,18},{3,11},{11,19},{4,12},{12... | collective-permute-start | bytes 786440 | tf_op jit(solution)/shard_map/ppermute | solution.py:352
  302.2 15.2 %collective-permute-start.53 = (f32[72,1536]{1,0:T(8,128)S(1)}, f32[72,1536]{1,0:T(8,128)}, u32[]{:S(2)}, u32[]{:S(2)}) collective-permute-start(f32[72,1536]{1,0:T(8,128)S(1)} %get-tuple-element.61), channel_id=1, source_target_pairs={{24,16},{25,17},{26,18},{27,19},{28,20},{29,21},{30,22},{31,23}} | collective-permute-start | bytes 1327112 | tf_op jit(solution)/shard_map/ppermute | solution.py:353
  309.1 14.0 %collective-permute-start.51 = (f32[72,1536]{1,0:T(8,128)}, f32[72,1536]{1,0:T(8,128)}, u32[]{:S(2)}, u32[]{:S(2)}) collective-permute-start(f32[72,1536]{1,0:T(8,128)} %bitcast_add_fusion.2), channel_id=1, source_target_pairs={{0,8},{8,16},{1,9},{9,17},{2,10},{10,18},{3,11},{11,19},{4,12},{12... | collective-permute-start | bytes 1327112 | tf_op jit(solution)/shard_map/ppermute | solution.py:352
  316.0 15.5 %collective-permute-start.72 = (f32[64,1024]{1,0:T(8,128)}, f32[64,1024]{1,0:T(8,128)}, u32[]{:S(2)}, u32[]{:S(2)}) collective-permute-start(f32[64,1024]{1,0:T(8,128)} %get-tuple-element.63), channel_id=1, source_target_pairs={{24,16},{16,8},{25,17},{17,9},{26,18},{18,10},{27,19},{19,11},{28,... | collective-permute-start | bytes 786440 | tf_op jit(solution)/shard_map/ppermute | solution.py:353
  325.1 14.7 %collective-permute-start.54 = (f32[72,1536]{1,0:T(8,128)}, f32[72,1536]{1,0:T(8,128)}, u32[]{:S(2)}, u32[]{:S(2)}) collective-permute-start(f32[72,1536]{1,0:T(8,128)} %get-tuple-element.59), channel_id=1, source_target_pairs={{24,16},{16,8},{25,17},{17,9},{26,18},{18,10},{27,19},{19,11},{28,... | collective-permute-start | bytes 1327112 | tf_op jit(solution)/shard_map/ppermute | solution.py:353
  326.5 16.4 %collective-permute-start.70 = (f32[64,1024]{1,0:T(8,128)S(1)}, f32[64,1024]{1,0:T(8,128)}, u32[]{:S(2)}, u32[]{:S(2)}) collective-permute-start(f32[64,1024]{1,0:T(8,128)S(1)} %get-tuple-element.62), channel_id=1, source_target_pairs={{0,8},{8,16},{16,24},{1,9},{9,17},{17,25},{2,10},{10,18},{18,26},{... | collective-permute-start | bytes 786440 | tf_op jit(solution)/shard_map/ppermute | solution.py:352
  334.4 12.4 %collective-permute-start.52 = (f32[72,1536]{1,0:T(8,128)S(1)}, f32[72,1536]{1,0:T(8,128)}, u32[]{:S(2)}, u32[]{:S(2)}) collective-permute-start(f32[72,1536]{1,0:T(8,128)S(1)} %get-tuple-element.58), channel_id=1, source_target_pairs={{0,8},{8,16},{16,24},{1,9},{9,17},{17,25},{2,10},{10,18},{18,26},{... | collective-permute-start | bytes 1327112 | tf_op jit(solution)/shard_map/ppermute | solution.py:352
  341.6 12.3 %collective-permute-start.55 = (f32[72,1536]{1,0:T(8,128)}, f32[72,1536]{1,0:T(8,128)}, u32[]{:S(2)}, u32[]{:S(2)}) collective-permute-start(f32[72,1536]{1,0:T(8,128)} %bitcast_add_fusion.1), channel_id=1, source_target_pairs={{24,16},{16,8},{8,0},{25,17},{17,9},{9,1},{26,18},{18,10},{10,2},{... | collective-permute-start | bytes 1327112 | tf_op jit(solution)/shard_map/ppermute | solution.py:353
  (97 other events, 706.4 us)

commit v2 on v1

v2 whole, which is shorter than its diff:
```python
import functools
import math

import jax
import jax.numpy as jnp
from jax import lax
from jax.experimental import pallas as pl
from jax.experimental.pallas import tpu as pltpu
from jax.sharding import PartitionSpec as P

HEADS = 16
KV_HEADS = 4
HEAD_DIM = 64
QW = 1024
KW = 256
DOC_MOST = 384
Q_BLOCK = 128

EPS = 1e-05
ROPE_BASE = 500000.0
SCALE = HEAD_DIM ** (-0.5)

bf16 = jnp.bfloat16
f32 = jnp.float32


def params(mib):
    return pltpu.CompilerParams(vmem_limit_bytes=mib << 20)


def about(us):
    return pl.CostEstimate(flops=int(us * 1e9), bytes_accessed=int(us * 3e6), transcendentals=0)


SMEM = pl.BlockSpec(memory_space=pltpu.SMEM)
VMEM = pl.BlockSpec(memory_space=pltpu.VMEM)
ANY = pl.BlockSpec(memory_space=pl.ANY)


def nt(a, b):
    return lax.dot_general(a, b, (((1,), (1,)), ((), ())), preferred_element_type=f32)


def tn(a, b):
    return lax.dot_general(a, b, (((0,), (0,)), ((), ())), preferred_element_type=f32)


def nn(a, b):
    return jnp.dot(a, b, preferred_element_type=f32)


def swap(a, axis, bit):
    n = lax.axis_size(axis)
    return lax.ppermute(a, axis, [(i, i ^ bit) for i in range(n)])


def neighbours(a, axis):
    n = lax.axis_size(axis)
    return swap(a, axis, n // 4), swap(a, axis, n // 2)


def relay(own, first, second, *earlier):
    rows, columns = own.shape
    half = rows // 32 * 16

    def kernel(own_ref, first_ref, second_ref, *refs):
        upper, lower, trio = refs[-3:]
        upper[...] = first_ref[:half, :]
        lower[...] = second_ref[half:, :]
        trio[:rows, :] = own_ref[...]
        trio[rows : 2 * rows, :] = first_ref[...]
        trio[2 * rows :, :] = second_ref[...]

    return pl.pallas_call(
        kernel,
        out_shape=[shape(half, columns), shape(rows - half, columns), shape(3 * rows, columns)],
        in_specs=[VMEM] * 3 + [ANY] * len(earlier),
        out_specs=[VMEM] * 3,
        compiler_params=params(56),
        cost_estimate=about(2),
        name="relay",
    )(own, first, second, *earlier)


def complete(upper, lower, trio, axis):
    n = lax.axis_size(axis)
    rows, half = trio.shape[0] // 3, upper.shape[0]
    upper, lower = swap(upper, axis, n // 2), swap(lower, axis, n // 4)
    arrays = [trio, upper, lower]
    slots = {
        0: [(0, 0, rows)],
        n // 4: [(0, rows, rows)],
        n // 2: [(0, 2 * rows, rows)],
        n // 4 | n // 2: [(1, 0, half), (2, 0, rows - half)],
    }
    bit = n // 8
    while bit >= 1:
        at = len(arrays)
        arrays += [swap(a, axis, bit) for a in arrays]
        for j in list(slots):
            slots[j ^ bit] = [(i + at, start, size) for i, start, size in slots[j]]
        bit //= 2
    return arrays, [slots[j] for j in range(n)]


def whole_slot(refs, pieces, rows):
    values = [refs[i][start : start + size, :] for i, start, size in pieces]
    value = values[0] if len(values) == 1 else jnp.concatenate(values, axis=0)
    return value[:rows], value


def turn(x, lower):
    return jnp.where(lower, pltpu.roll(x, 96, 1), pltpu.roll(x, 32, 1))


def lower_lanes(rows):
    return lax.broadcasted_iota(jnp.int32, (rows, 128), 1) % HEAD_DIM < HEAD_DIM // 2


def inverse_rms(x):
    return lax.rsqrt(jnp.mean(x * x, axis=1, keepdims=True) + EPS)


def proj_kernel(slots, many, groups, me_ref, tok_ref, cos_ref, sin_ref, *refs):
    n = len(slots)
    outs, (normed_ref, acc) = refs[-groups - 2 : -2], refs[-2:]
    u, d = me_ref[0], me_ref[1]
    rows, width = tok_ref.shape
    part = width // n
    inv = inverse_rms(tok_ref[...].astype(f32))
    for j in range(n):
        at = pl.multiple_of((d ^ j) * part, part)
        w, ext = whole_slot(refs, slots[j], part)
        gain = ext[part : part + 1, :part].astype(f32)
        normed = (tok_ref[:, pl.ds(at, part)].astype(f32) * inv * gain).astype(bf16)
        normed_ref[:, pl.ds(at, part)] = normed
        term = nn(normed, w[:, : acc.shape[1]])
        if j == 0:
            acc[...] = term
        else:
            acc[...] += term
    lower = lower_lanes(rows)
    cos, sin = cos_ref[...], sin_ref[...]
    turned = []
    for c in range((QW + KW) // 128):
        x = acc[:, c * 128 : (c + 1) * 128]
        turned.append((x * cos + turn(x, lower) * sin).astype(bf16))
    heads = HEADS // groups
    repeat = groups // KV_HEADS
    for g in range(groups):
        qw = heads * HEAD_DIM
        q = jnp.concatenate(turned[g * qw // 128 : (g + 1) * qw // 128], axis=1)
        kh = g // repeat
        at = QW // 128 + kh // 2
        half = (kh % 2) * HEAD_DIM
        k = turned[at][:, half : half + HEAD_DIM]
        v = acc[:, QW + KW + kh * HEAD_DIM : QW + KW + (kh + 1) * HEAD_DIM].astype(bf16)
        piece = jnp.concatenate([q, k, v], axis=1)
        for j in range(groups):

            @pl.when((u ^ g) == j)
            def _():
                outs[j][...] = piece


def spread(own, axis):
    n = lax.axis_size(axis)
    slots = {0: own}
    far = 1
    while far < n:
        slots[far] = swap(own, axis, far)
        for j in range(1, (far + 1) // 2):
            slots[far ^ j] = swap(slots[far], axis, j)
        far = 2 * far + 1
    return [slots[j] for j in range(n)]


def d_attn_kernel(slots, groups, columns, me_ref, *refs):
    shards, arrays = refs[: 2 * groups], refs[2 * groups :]
    out, weight = refs[-2:]
    u, d = me_ref[0], me_ref[1]
    n = len(slots)
    rows, width = shards[0].shape
    part = width // n
    for j in range(n):
        at = pl.multiple_of((d ^ j) * part, part)
        weight[pl.ds(at, part), :] = whole_slot(arrays, slots[j], part)[0][:, columns:]
    for side in range(2):
        for j in range(groups):
            at = pl.multiple_of((2 * (u ^ j) + side) * rows, rows)
            out[pl.ds(at, rows), :] = nn(shards[side * groups + j][...], weight[...]).astype(bf16)


def slices_kernel(n, groups, normed_ref, d_out_ref, *refs):
    out, turned = refs[-2:]
    width = normed_ref.shape[1]
    block = width // (groups * n)
    for side, ref in enumerate((normed_ref, d_out_ref)):
        turned[...] = ref[...].T
        for e in range(n):
            for g in range(groups):
                at = g * (width // groups) + e * block
                to = (side * groups + g) * block
                out[e, to : to + block, :] = turned[at : at + block, :]


def collect(u, pieces, *wholes):
    rows = pieces[0].shape[0]
    for j, piece in enumerate(pieces):
        at = pl.ds(pl.multiple_of((u ^ j) * rows, rows), rows)
        lane = 0
        for whole, scale in wholes:
            part = piece[:, lane : lane + whole.shape[1]]
            whole[at, :] = part if scale is None else part * jnp.asarray(scale, bf16)
            lane += whole.shape[1]


def hand_out(u, g, value, outs):
    for j, out in enumerate(outs):

        @pl.when((u ^ g) == j)
        def _():
            out[...] = value


def doc_starts(lengths_ref):
    starts = [jnp.int32(0)]
    for i in range(lengths_ref.shape[0] - 1):
        starts.append(starts[-1] + lengths_ref[i])
    return starts


def window(b, starts):
    q0 = b * Q_BLOCK
    w0, w1 = max(0, q0 - DOC_MOST), q0 + Q_BLOCK
    key_pos = w0 + lax.broadcasted_iota(jnp.int32, (Q_BLOCK, w1 - w0), 1)
    row_pos = q0 + lax.broadcasted_iota(jnp.int32, (Q_BLOCK, w1 - w0), 0)
    row_at = q0 + lax.broadcasted_iota(jnp.int32, (Q_BLOCK, 1), 0)
    begin = jnp.zeros((Q_BLOCK, 1), jnp.int32)
    for start in starts[1:]:
        begin = jnp.where(row_at >= start, start, begin)
    allowed = (key_pos >= begin) & (key_pos <= row_pos)
    return slice(q0, w1), slice(w0, w1), jnp.where(allowed, 0.0, -1e30).astype(f32)


def stacked(whole, rows, heads):
    return jnp.concatenate([whole[rows, h * HEAD_DIM : (h + 1) * HEAD_DIM] for h in range(heads)], axis=0)


def side_by_side(value, heads):
    return jnp.concatenate([value[h * Q_BLOCK : (h + 1) * Q_BLOCK, :] for h in range(heads)], axis=1)


def forward_kernel(groups, me_ref, lengths_ref, *refs):
    pieces, outs = refs[:groups], refs[groups + 1 : 2 * groups + 1]
    o_ref, stats_ref, q_all, kv_all, attn_all = refs[2 * groups + 1 :]
    u = me_ref[0]
    length, qw = q_all.shape
    heads = qw // HEAD_DIM
    collect(u, pieces, (q_all, SCALE), (kv_all, None))
    starts = doc_starts(lengths_ref)
    for b in range(length // Q_BLOCK):
        here, there, bias = window(b, starts)
        keys, values = kv_all[there, :HEAD_DIM], kv_all[there, HEAD_DIM:]
        scores = nt(stacked(q_all, here, heads), keys)
        scores = scores + jnp.concatenate([bias] * heads, axis=0)
        peak = jnp.max(scores, axis=1, keepdims=True)
        weights = jnp.exp(scores - peak)
        inverse = 1.0 / jnp.sum(weights, axis=1, keepdims=True)
        mixed = side_by_side(nn((weights * inverse).astype(bf16), values), heads)
        o_ref[here, :] = mixed
        attn_all[here, :] = mixed.astype(bf16)
        stats_ref[b, :, :1] = peak
        stats_ref[b, :, 1:2] = inverse
    rows = length // groups
    for g in range(groups):
        hand_out(u, g, attn_all[g * rows : (g + 1) * rows, :], outs)


def backward_kernel(groups, me_ref, lengths_ref, cos_ref, sin_ref, o_ref, stats_ref, *refs):
    qkv_pieces, g_all = refs[:groups], refs[groups]
    q_all, kv_all, dq_all, acc = refs[-4:]
    outs = refs[-4 - groups : -4]
    u = me_ref[0]
    length, qw = q_all.shape
    heads = qw // HEAD_DIM
    collect(u, qkv_pieces, (q_all, SCALE), (kv_all, None))
    starts = doc_starts(lengths_ref)
    acc[...] = jnp.zeros_like(acc)
    for b in range(length // Q_BLOCK):
        here, there, bias = window(b, starts)
        keys, values = kv_all[there, :HEAD_DIM], kv_all[there, HEAD_DIM:]
        queries, grads = stacked(q_all, here, heads), stacked(g_all, here, heads)
        scores = nt(queries, keys) + jnp.concatenate([bias] * heads, axis=0)
        shares = jnp.exp(scores - stats_ref[b, :, :1]) * stats_ref[b, :, 1:2]
        row_dot = jnp.sum(grads.astype(f32) * stacked(o_ref, here, heads), axis=1, keepdims=True)
        d_scores = (shares * (nt(grads, values) - row_dot)).astype(bf16)
        dq_all[here, :] = side_by_side(nn(d_scores, keys) * SCALE, heads)
        acc[:HEAD_DIM, there] += tn(queries, d_scores)
        acc[HEAD_DIM:, there] += tn(grads, shares.astype(bf16))
    rows = length // groups
    lower = lower_lanes(rows)
    value_lane = lax.broadcasted_iota(jnp.int32, (rows, 128), 1) >= HEAD_DIM
    for g in range(groups):
        here = slice(g * rows, (g + 1) * rows)
        cos, sin = cos_ref[here, :], sin_ref[here, :]
        parts = []
        for c in range(qw // 128):
            x = dq_all[here, c * 128 : (c + 1) * 128]
            parts.append(x * cos - turn(x, lower) * sin)
        x = acc[:, here].T
        parts.append(jnp.where(value_lane, x, x * cos - turn(x, lower) * sin))
        hand_out(u, g, jnp.concatenate(parts, axis=1).astype(bf16), outs)


def join_attn_kernel(groups, me_ref, *refs):
    u, out = me_ref[0], refs[-1]
    qw = QW // groups
    for j in range(groups):
        at = pl.multiple_of((u ^ j) * qw, qw)
        out[:, pl.ds(at, qw)] = refs[j][...]


def join_proj_kernel(groups, me_ref, *refs):
    u, (out, wide) = me_ref[0], refs[-2:]
    qw = QW // groups
    repeat = groups // KV_HEADS
    wide[...] = jnp.zeros_like(wide)
    for j in range(groups):
        at = pl.multiple_of((u ^ j) * qw, qw)
        out[:, pl.ds(at, qw)] = refs[j][:, :qw]
        back = refs[j][:, qw:].astype(f32)
        for kh in range(KV_HEADS):

            @pl.when((u ^ j) // repeat == kh)
            def _():
                wide[:, kh * 128 : (kh + 1) * 128] += back

    low = wide[...].astype(bf16)
    for at, half in ((QW, 0), (QW + KW, HEAD_DIM)):
        heads = [low[:, kh * 128 + half : kh * 128 + half + HEAD_DIM] for kh in range(KV_HEADS)]
        out[:, at : at + KW] = jnp.concatenate(heads, axis=1)


def tokens_kernel(slots, many, groups, factor, me_ref, tok_ref, d_out_ref, d_proj_ref, *refs):
    n = len(slots)
    d_tok_ref, d_gain_ref, wide, gains = refs[-4:]
    d = me_ref[1]
    width = tok_ref.shape[1]
    part = width // n
    d_proj = d_proj_ref[...]
    for j in range(n):
        at = pl.multiple_of((d ^ j) * part, part)
        w, ext = whole_slot(refs, slots[j], part)
        wide[:, pl.ds(at, part)] = nt(d_proj, w[:, : d_proj.shape[1]])
        gains[:, pl.ds(at, part)] = ext[part : part + 1, :part].astype(f32)
    x = tok_ref[...].astype(f32)
    inv = inverse_rms(x)
    unit = x * inv
    d_normed = wide[...]
    d_gain = jnp.sum(d_normed * unit, axis=0, keepdims=True) * factor
    scaled = d_normed * gains[...]
    mean = jnp.mean(scaled * unit, axis=1, keepdims=True)
    d_tok_ref[...] = (d_out_ref[...].astype(f32) + inv * (scaled - unit * mean)).astype(bf16)
    block = width // (groups * n)
    for e in range(n):
        starts = [g * (width // groups) + e * block for g in range(groups)]
        mine = jnp.concatenate([d_gain[:, s : s + block] for s in starts], axis=1)
        for g in range(groups):
            d_gain_ref[g, e : e + 1, :] = mine[:, g * block : (g + 1) * block]


def grads_kernel(slots, side, groups, factor, me_ref, slices, *refs):
    n = len(slots)
    out, acc = refs[-2:]
    d = me_ref[1]
    kept = acc.shape[0]
    for j in range(n):
        a = slices[d ^ j, side * kept : (side + 1) * kept, :]
        b, _ = whole_slot(refs, slots[j], a.shape[1])
        term = nn(a, b)
        if j == 0:
            acc[...] = term
        else:
            acc[...] += term
    block = kept // groups
    for g in range(groups):
        out[g] = acc[g * block : (g + 1) * block, :] * factor


def grads_and_pass_kernel(slots, side, groups, factor, me_ref, slices, *refs):
    *refs, pass_ref, out, pass_out, acc = refs
    grads_kernel(slots, side, groups, factor, me_ref, slices, *refs, out, acc)
    pass_out[...] = pass_ref[...]


def block_sum(local, axis):
    me = lax.axis_index(axis)
    total = lax.dynamic_index_in_dim(local, me, 0, keepdims=False)
    for j in range(1, lax.axis_size(axis)):
        total = total + swap(lax.dynamic_index_in_dim(local, me ^ j, 0, keepdims=False), axis, j)
    return total


def weights_here(w_qkv, w_out, gain, me, qw, grad_rows):
    part, columns = w_qkv.shape
    rows, width = grad_rows.shape
    half = rows // 2

    def kernel(me_ref, w_qkv_ref, w_out_ref, gain_ref, grad_ref, out, upper, lower):
        at = pl.multiple_of(me_ref[0] * qw, qw)
        out[:part, :columns] = w_qkv_ref[...]
        out[:part, columns:] = w_out_ref[:, pl.ds(at, qw)]
        out[part:, :] = jnp.zeros_like(out[part:, :])
        out[part : part + 1, :part] = gain_ref[...]
        upper[...] = grad_ref[:half, :]
        lower[...] = grad_ref[half:, :]

    return pl.pallas_call(
        kernel,
        out_shape=[shape(part + 16, columns + qw)] + [shape(half, width)] * 2,
        in_specs=[SMEM] + [VMEM] * 4,
        out_specs=[VMEM] * 3,
        cost_estimate=about(2),
        name="weights_here",
    )(me, w_qkv, w_out, gain[None, :], grad_rows)


def shape(*dims, dtype=bf16):
    return jax.ShapeDtypeStruct(dims, dtype)


def body(tokens, d_out, lengths, gain, w_qkv, w_out):
    groups, n = lax.axis_size("ulysses"), lax.axis_size("dp")
    u, d = lax.axis_index("ulysses"), lax.axis_index("dp")
    me = jnp.stack([u, d]).astype(jnp.int32)
    token_rows, grad_rows = tokens[0], d_out[0]
    rows, width = token_rows.shape
    length = rows * groups
    part = width // n
    heads = HEADS // groups
    qw = heads * HEAD_DIM
    columns = w_qkv.shape[1]
    factor = 1.0 / math.sqrt(length * n)
    block = width // (groups * n)
    kept = block * groups

    held, *grad_halves = weights_here(w_qkv, w_out, gain, me, qw, grad_rows)
    held_near = neighbours(held, "dp")
    first, second = (spread(half, "ulysses") for half in grad_halves)
    held_arrays, held_slots = complete(*relay(held, *held_near, first[1], first[groups - 1]), "dp")

    bounds = jnp.cumsum(lengths[0]) - lengths[0]
    places = jnp.arange(length, dtype=jnp.int32)
    begins = jnp.max(jnp.where(bounds[None, :] <= places[:, None], bounds[None, :], 0), axis=1)
    places = places - begins
    inverse = ROPE_BASE ** (-jnp.arange(0, HEAD_DIM, 2).astype(f32) / HEAD_DIM)
    angles = places.astype(f32)[:, None] * jnp.tile(inverse, 4)[None, :]
    signs = jnp.where(jnp.arange(128) % HEAD_DIM < HEAD_DIM // 2, -1.0, 1.0).astype(f32)
    cos, sin = jnp.cos(angles), jnp.sin(angles) * signs[None, :]
    cos_here = lax.dynamic_slice_in_dim(cos, u * rows, rows)
    sin_here = lax.dynamic_slice_in_dim(sin, u * rows, rows)

    *pieces, normed = pl.pallas_call(
        functools.partial(proj_kernel, held_slots, len(held_arrays), groups),
        out_shape=[shape(rows, qw + 128)] * groups + [shape(rows, width)],
        in_specs=[SMEM] + [VMEM] * (3 + len(held_arrays)) + [ANY] * 2,
        out_specs=[VMEM] * (groups + 1),
        scratch_shapes=[pltpu.VMEM((rows, columns), f32)],
        compiler_params=params(56),
        cost_estimate=about(8),
        name="proj",
    )(me, token_rows, cos_here, sin_here, *held_arrays, second[1], second[groups - 1])
    qkv_here = [pieces[0]] + [swap(pieces[j], "ulysses", j) for j in range(1, groups)]

    own_slices = pl.pallas_call(
        functools.partial(slices_kernel, n, groups),
        out_shape=shape(n, 2 * kept, rows),
        in_specs=[VMEM] * 2,
        out_specs=VMEM,
        scratch_shapes=[pltpu.VMEM((width, rows), bf16)],
        compiler_params=params(56),
        cost_estimate=about(3),
        name="slices",
    )(normed, grad_rows)
    slices = lax.all_to_all(own_slices, "dp", 0, 0, tiled=True)
    d_attn = pl.pallas_call(
        functools.partial(d_attn_kernel, held_slots, groups, columns),
        out_shape=shape(length, qw),
        in_specs=[SMEM] + [VMEM] * (2 * groups + len(held_arrays)) + [ANY],
        out_specs=VMEM,
        scratch_shapes=[pltpu.VMEM((width, qw), bf16)],
        compiler_params=params(56),
        cost_estimate=about(6),
        name="d_attn",
    )(me, *first, *second, *held_arrays, own_slices)

    blocks = length // Q_BLOCK
    *mixed, o, stats = pl.pallas_call(
        functools.partial(forward_kernel, groups),
        out_shape=[shape(rows, qw)] * groups
        + [shape(length, qw, dtype=f32), shape(blocks, heads * Q_BLOCK, 2, dtype=f32)],
        in_specs=[SMEM] * 2 + [VMEM] * groups + [ANY],
        out_specs=[VMEM] * (groups + 2),
        scratch_shapes=[
            pltpu.VMEM((length, qw), bf16),
            pltpu.VMEM((length, 128), bf16),
            pltpu.VMEM((length, qw), bf16),
        ],
        compiler_params=params(56),
        cost_estimate=about(10),
        name="forward",
    )(me, lengths[0], *qkv_here, d_attn)
    mixed = [mixed[0]] + [swap(mixed[j], "ulysses", j) for j in range(1, groups)]

    back = pl.pallas_call(
        functools.partial(backward_kernel, groups),
        out_shape=[shape(rows, qw + 128)] * groups,
        in_specs=[SMEM] * 2 + [VMEM] * (5 + groups),
        out_specs=[VMEM] * groups,
        scratch_shapes=[
            pltpu.VMEM((length, qw), bf16),
            pltpu.VMEM((length, 128), bf16),
            pltpu.VMEM((length, qw), f32),
            pltpu.VMEM((128, length), f32),
        ],
        compiler_params=params(56),
        cost_estimate=about(15),
        name="backward",
    )(me, lengths[0], cos, sin, o, stats, *qkv_here, d_attn)
    back = [back[0]] + [swap(back[j], "ulysses", j) for j in range(1, groups)]

    attn = pl.pallas_call(
        functools.partial(join_attn_kernel, groups),
        out_shape=shape(rows, QW),
        in_specs=[SMEM] + [VMEM] * groups + [ANY] * 2,
        out_specs=VMEM,
        cost_estimate=about(2),
        name="join_attn",
    )(me, *mixed, slices, back[0])
    attn_near = neighbours(attn, "dp")

    d_proj = pl.pallas_call(
        functools.partial(join_proj_kernel, groups),
        out_shape=shape(rows, columns),
        in_specs=[SMEM] + [VMEM] * groups + [ANY] * 2,
        out_specs=VMEM,
        scratch_shapes=[pltpu.VMEM((rows, 128 * KV_HEADS), f32)],
        cost_estimate=about(3),
        name="join_proj",
    )(me, *back, *attn_near)
    proj_near = neighbours(d_proj, "dp")
    attn_arrays, attn_slots = complete(*relay(attn, *attn_near, d_proj), "dp")

    d_w_out_terms = pl.pallas_call(
        functools.partial(grads_kernel, attn_slots, 1, groups, factor),
        out_shape=shape(groups, block, QW, dtype=f32),
        in_specs=[SMEM] + [VMEM] * (1 + len(attn_arrays)),
        out_specs=VMEM,
        scratch_shapes=[pltpu.VMEM((kept, QW), f32)],
        compiler_params=params(56),
        cost_estimate=about(5),
        name="d_w_out",
    )(me, slices, *attn_arrays)

    d_w_out = block_sum(d_w_out_terms, "ulysses")
    relayed = relay(d_proj, *proj_near, d_w_out_terms)
    proj_arrays, proj_slots = complete(*relayed, "dp")

    d_tokens, partial_gain = pl.pallas_call(
        functools.partial(tokens_kernel, held_slots, len(held_arrays), groups, factor),
        out_shape=[shape(rows, width), shape(groups, n, block, dtype=f32)],
        in_specs=[SMEM] + [VMEM] * (3 + len(held_arrays)) + [ANY],
        out_specs=[VMEM] * 2,
        scratch_shapes=[pltpu.VMEM((rows, width), f32), pltpu.VMEM((1, width), f32)],
        compiler_params=params(56),
        cost_estimate=about(8),
        name="d_tokens",
    )(me, token_rows, grad_rows, d_proj, *held_arrays, relayed[0])

    d_w_qkv, gain_terms = pl.pallas_call(
        functools.partial(grads_and_pass_kernel, proj_slots, 0, groups, factor),
        out_shape=[shape(groups, block, columns, dtype=f32), shape(groups, n, block, dtype=f32)],
        in_specs=[SMEM] + [VMEM] * (2 + len(proj_arrays)),
        out_specs=[VMEM] * 2,
        scratch_shapes=[pltpu.VMEM((kept, columns), f32)],
        compiler_params=params(56),
        cost_estimate=about(6),
        name="d_w_qkv",
    )(me, slices, *proj_arrays, partial_gain)
    d_w_qkv = block_sum(d_w_qkv, "ulysses")
    d_gain = gain_terms.reshape(groups * n, block)
    d_gain = lax.all_to_all(d_gain, ("ulysses", "dp"), 0, 0, tiled=True).sum(axis=0)
    return (d_tokens[None], d_w_qkv, d_w_out, d_gain)


def solution(mesh):
    in_specs = (
        P("dp", "ulysses", None),
        P("dp", "ulysses", None),
        P("dp", None),
        P("dp"),
        P("dp", None),
        P("dp", None),
    )
    out_specs = (
        P("dp", "ulysses", None),
        P(("ulysses", "dp"), None),
        P(("ulysses", "dp"), None),
        P(("ulysses", "dp")),
    )
    return jax.shard_map(body, mesh=mesh, in_specs=in_specs, out_specs=out_specs, check_vma=False)
```

time: 358 us -> 265 us (0.74)
  local copies, waits for them, and re-layouts: 54.8 us -> 18.7 us
  waiting for transfers between devices: 142 us -> 109 us
  starting transfers between devices: 81.3 us -> 52.8 us
  Pallas kernels: 53.9 us -> 76.3 us
  other arithmetic: 23.3 us -> 7.1 us
    ppermute x62 -> x42, waiting for transfers between devices: 123 us -> 80.9 us  [swap(): return lax.ppermute(a, axis, [(i, i ^ bit) for i in range(n)])]
    ppermute x12 -> x0, starting transfers between devices: 29.6 us -> none  [the longest x6 21.5 us: chain_sum(): up = lax.ppermute(up, axis, [(i, i + 1) for i in range(step + 1)])]
    all_to_all x0 -> x2, waiting for transfers between devices: none -> 27.9 us  [the longest x1 27.8 us: body(): lax.all_to_all(d_gain, ('ulysses', 'dp'), 0, 0, tiled=True).sum(axis=0)]
    unnamed x142 -> x78, local copies, waits for them, and re-layouts: 38.6 us -> 14.4 us
    pallas_call x7 -> x12, Pallas kernels: 49.5 us -> 71.6 us  [the longest x1 12.9 us: body(): pl.pallas_call(functools.partial(backward_kernel, groups), out_shape=[sha...]
    ppermute x12 -> x0, waiting for transfers between devices: 18.5 us -> none  [the longest x6 11.5 us: chain_sum(): up = lax.ppermute(up, axis, [(i, i + 1) for i in range(step + 1)])]
    add x8 -> x2, other arithmetic: 13.8 us -> 3.7 us  [block_sum(): total + swap(lax.dynamic_index_in_dim(local, me ^ j, 0, keepdims=False),...]
    slice x10 -> x0, local copies, waits for them, and re-layouts: 8.99 us -> none  [the longest x4 4.49 us: gather_slots(): lower = swap(over_second[split:], axis, first)]
  transfers between devices with their start and end apart: 74 -> 44, of which waited for: 25 -> 15; matrix products, arithmetic and copies ran while one was open for 10% -> 3% of each run, Pallas kernels for 8% -> 22%
where the time goes in v2:
time: 265 us
  waiting for transfers between devices  109 us (41%)
  Pallas kernels  76.3 us (29%)
  starting transfers between devices  52.8 us (20%)
  local copies, waits for them, and re-layouts  18.7 us (7%)
  other arithmetic  7.1 us (3%)
    ppermute x42, waiting for transfers between devices, swap(): return lax.ppermute(a, axis, [(i, i ^ bit) for i in range(n)])  80.9 us
    ppermute x42, starting transfers between devices, swap(): return lax.ppermute(a, axis, [(i, i ^ bit) for i in range(n)])  45.7 us
    all_to_all x1, waiting for transfers between devices, body(): lax.all_to_all(d_gain, ('ulysses', 'dp'), 0, 0, tiled=True).sum(axis=0)  27.8 us
    unnamed x78, local copies, waits for them, and re-layouts  14.4 us
    pallas_call x1, Pallas kernels, body(): pl.pallas_call(functools.partial(backward_kernel, groups), out_shape=[sha...  12.9 us
    pallas_call x3, Pallas kernels, relay(): pl.pallas_call(kernel, out_shape=[shape(half, columns), shape(rows - half...  9.94 us
    pallas_call x1, Pallas kernels, body(): pl.pallas_call(functools.partial(forward_kernel, groups), out_shape=[shap...  8.76 us
    pallas_call x1, Pallas kernels, body(): pl.pallas_call(functools.partial(tokens_kernel, held_slots, len(held_arra...  7.89 us
  transfers between devices with their start and end apart: 44, of which 15 were waited for; matrix products, arithmetic and copies ran while one was open for 3% of the time, Pallas kernels for 22%

profile of v2, /device:TPU:0, one launch (start us, length us, event | category | flops | bytes accessed | tf_op | source)
XLA Modules:
  0.0 264.6 jit_solution(17414337767090558824)
XLA Ops:
  2.5 3.0 %weights_here.1 = (bf16[272,1792]{1,0:T(8,128)(2,1)}, bf16[128,2048]{1,0:T(8,128)(2,1)}, bf16[128,2048]{1,0:T(8,128)(2,1)}) custom-call(s32[2]{0:T(128)} %pad_add_fusion.me_ref, bf16[256,1536]{1,0:T(8,128)(2,1)} %w_qkv_ref.1, bf16[256,1024]{1,0:T(8,128)(2,1)} %w_out_ref.1, bf16[1,256]{1,0:T(2,128)(2,1)} %broadcast_in_dim.32.gain_ref, bf16[256,2048]{1,0:T(8,128)(2,1)} %bitcast.37), custom_call_target="tpu_custom_call" | custom-call | flops 2000000000 | bytes 6000000 | tf_op jit(solution)/shard_map/weights_here/pallas_call | solution.py:419
  5.5 2.9 %collective-permute-start = (bf16[272,1792]{1,0:T(8,128)(2,1)}, bf16[272,1792]{1,0:T(8,128)(2,1)S(1)}, u32[]{:S(2)}, u32[]{:S(2)}) collective-permute-start(bf16[272,1792]{1,0:T(8,128)(2,1)} %get-tuple-element.35.own_ref), channel_id=1, source_target_pairs={{0,2},{1,3},{2,0},{3,1},{4,6},{5,7},{6,4},{7,5},{8,10},{9,11},{10,... | collective-permute-start | bytes 2924552 | tf_op jit(solution)/shard_map/ppermute | solution.py:54
  8.4 1.5 collective-permute-start.1
  9.9 1.6 collective-permute-start.2
  11.5 2.5 collective-permute-start.3
  14.0 10.2 %collective-permute-done.2.refs_0_.refs_1_ = bf16[128,2048]{1,0:T(8,128)(2,1)S(1)} collective-permute-done((bf16[128,2048]{1,0:T(8,128)(2,1)}, bf16[128,2048]{1,0:T(8,128)(2,1)S(1)}, u32[]{:S(2)}, u32[]{:S(2)}) %collective-permute-start.2) | collective-permute-done | bytes 524320 | tf_op jit(solution)/shard_map/ppermute | solution.py:54
  24.2 12.4 %collective-permute-done.3.refs_1_.refs_3_ = bf16[128,2048]{1,0:T(8,128)(2,1)S(1)} collective-permute-done((bf16[128,2048]{1,0:T(8,128)(2,1)}, bf16[128,2048]{1,0:T(8,128)(2,1)S(1)}, u32[]{:S(2)}, u32[]{:S(2)}) %collective-permute-start.3) | collective-permute-done | bytes 524320 | tf_op jit(solution)/shard_map/ppermute | solution.py:54
  38.8 3.7 %relay.3 = (bf16[128,1792]{1,0:T(8,128)(2,1)}, bf16[144,1792]{1,0:T(8,128)(2,1)}, bf16[816,1792]{1,0:T(8,128)(2,1)}) custom-call(bf16[272,1792]{1,0:T(8,128)(2,1)} %get-tuple-element.35.own_ref, bf16[272,1792]{1,0:T(8,128)(2,1)} %copy-done.8, bf16[272,1792]{1,0:T(8,128)(2,1)} %copy-done.9, bf16[128,2048]{1,0:T(8,128)(2,1)} %copy-done.14, ...), custom_call_target="tpu_custom_call" | custom-call | flops 2000000000 | bytes 6000000 | tf_op jit(solution)/shard_map/relay/pallas_call | solution.py:74
  43.1 2.6 collective-permute-start.10
  47.1 13.0 %collective-permute-done.5.refs_2_.refs_10_ = bf16[144,1792]{1,0:T(8,128)(2,1)} collective-permute-done((bf16[144,1792]{1,0:T(8,128)(2,1)}, bf16[144,1792]{1,0:T(8,128)(2,1)}, u32[]{:S(2)}, u32[]{:S(2)}) %collective-permute-start.5) | collective-permute-done | bytes 516128 | tf_op jit(solution)/shard_map/ppermute | solution.py:54
  60.7 1.9 fusion
  63.4 6.4 %collective-permute-done.10.refs_7_ = bf16[128,2048]{1,0:T(8,128)(2,1)} collective-permute-done((bf16[128,2048]{1,0:T(8,128)(2,1)S(1)}, bf16[128,2048]{1,0:T(8,128)(2,1)}, u32[]{:S(2)}, u32[]{:S(2)}) %collective-permute-start.10) | collective-permute-done | bytes 524320 | tf_op jit(solution)/shard_map/ppermute | solution.py:54
  71.5 7.8 %proj.1 = (bf16[256,384]{1,0:T(8,128)(2,1)}, bf16[256,384]{1,0:T(8,128)(2,1)}, bf16[256,384]{1,0:T(8,128)(2,1)}, bf16[256,384]{1,0:T(8,128)(2,1)}, bf16[256,2048]{1,0:T(8,128)(2,1)}) custom-call(s32[2]{0:T(128)} %pad_add_fusion.me_ref, bf16[256,2048]{1,0:T(8,128)(2,1)} %bitcast.35, f32[256,128]{1,0:T(8,128)} %get-tuple-element.75.cos_ref, ...), custom_call_target="tpu_custom_call" | custom-call | flops 8000000000 | bytes 24000000 | tf_op jit(solution)/shard_map/proj/pallas_call | solution.py:464
  79.3 2.1 collective-permute-start.11
  81.7 2.2 collective-permute-start.13
  83.9 3.5 %slices.1.refs_14_ = bf16[8,512,256]{2,1,0:T(8,128)(2,1)} custom-call(bf16[256,2048]{1,0:T(8,128)(2,1)} %get-tuple-element.45.normed_ref, bf16[256,2048]{1,0:T(8,128)(2,1)} %bitcast.38), custom_call_target="tpu_custom_call" | custom-call | flops 3000000000 | bytes 9000000 | tf_op jit(solution)/shard_map/slices/pallas_call | solution.py:476
  87.4 3.8 %all-to-all-start = ((bf16[8,512,256]{2,1,0:T(8,128)(2,1)}), bf16[8,512,256]{2,1,0:T(8,128)(2,1)S(1)}, u32[]{:S(2)}, u32[]{:S(2)}) async-start(bf16[8,512,256]{2,1,0:T(8,128)(2,1)} %slices.1.refs_14_), calls=%async_computation | async-start | bytes 4194304 | tf_op jit(solution)/shard_map/all_to_all | solution.py:486
  91.2 4.8 %collective-permute-done.15.refs_6_ = bf16[128,2048]{1,0:T(8,128)(2,1)S(1)} collective-permute-done((bf16[128,2048]{1,0:T(8,128)(2,1)}, bf16[128,2048]{1,0:T(8,128)(2,1)S(1)}, u32[]{:S(2)}, u32[]{:S(2)}) %collective-permute-start.15) | collective-permute-done | bytes 524320 | tf_op jit(solution)/shard_map/ppermute | solution.py:54
  96.8 6.5 %d_attn.1.refs_4_ = bf16[1024,256]{1,0:T(8,128)(2,1)} custom-call(s32[2]{0:T(128)} %pad_add_fusion.me_ref, bf16[128,2048]{1,0:T(8,128)(2,1)} %get-tuple-element.36.refs_0_, bf16[128,2048]{1,0:T(8,128)(2,1)} %copy-done.14, bf16[128,2048]{1,0:T(8,128)(2,1)} %collective-permute-done.14.refs_2_, bf16[128,2048]{1,0:T(8,128)(2,1)} %copy-done.15, ...), custom_call_target="tpu_custom_call" | custom-call | flops 6000000000 | bytes 18000000 | tf_op jit(solution)/shard_map/d_attn/pallas_call | solution.py:487
  105.1 8.8 %forward.1 = (bf16[256,256]{1,0:T(8,128)(2,1)}, bf16[256,256]{1,0:T(8,128)(2,1)}, bf16[256,256]{1,0:T(8,128)(2,1)}, bf16[256,256]{1,0:T(8,128)(2,1)}, f32[1024,256]{1,0:T(8,128)}, /*index=5*/f32[8,512,2]{2,1,0:T(8,128)}) custom-call(s32[2]{0:T(128)} %pad_add_fusion.me_ref, s32[10]{0:T(128)} %bitcast.40, bf16[256,384]{1,0:T(8,128)(2,1)} %get-tuple-element.41.refs_0_, ...), custom_call_target="tpu_custom_call" | custom-call | flops 10000000000 | bytes 30000000 | tf_op jit(solution)/shard_map/forward/pallas_call | solution.py:499
  113.8 1.9 collective-permute-start.20
  115.7 2.5 collective-permute-start.21
  118.2 12.9 %backward.1 = (bf16[256,384]{1,0:T(8,128)(2,1)}, bf16[256,384]{1,0:T(8,128)(2,1)}, bf16[256,384]{1,0:T(8,128)(2,1)}, bf16[256,384]{1,0:T(8,128)(2,1)}) custom-call(s32[2]{0:T(128)} %pad_add_fusion.me_ref, s32[10]{0:T(128)} %bitcast.41, f32[1024,128]{1,0:T(8,128)} %copy-done.3, f32[1024,128]{1,0:T(8,128)} %copy-done.2, f32[1024,256]{1,0:T(8,128)} %get-tuple-element.46.o_ref, ...), custom_call_target="tpu_custom_call" | custom-call | flops 15000000512 | bytes 45000000 | tf_op jit(solution)/shard_map/backward/pallas_call | solution.py:516
  132.6 2.0 join_attn.1.own_ref
  135.6 1.9 collective-permute-start.17
  137.5 2.5 collective-permute-start.18
  140.0 4.0 %collective-permute-done.16.refs_1_ = bf16[256,384]{1,0:T(8,128)(2,1)S(1)} collective-permute-done((bf16[256,384]{1,0:T(8,128)(2,1)S(1)}, bf16[256,384]{1,0:T(8,128)(2,1)S(1)}, u32[]{:S(2)}, u32[]{:S(2)}) %collective-permute-start.16) | collective-permute-done | bytes 196640 | tf_op jit(solution)/shard_map/ppermute | solution.py:54
  144.0 8.1 %collective-permute-done.17.refs_2_ = bf16[256,384]{1,0:T(8,128)(2,1)S(1)} collective-permute-done((bf16[256,384]{1,0:T(8,128)(2,1)S(1)}, bf16[256,384]{1,0:T(8,128)(2,1)S(1)}, u32[]{:S(2)}, u32[]{:S(2)}) %collective-permute-start.17) | collective-permute-done | bytes 196640 | tf_op jit(solution)/shard_map/ppermute | solution.py:54
  153.9 2.7 %join_proj.1.refs_0_.own_ref.d_proj_ref = bf16[256,1536]{1,0:T(8,128)(2,1)} custom-call(s32[2]{0:T(128)} %pad_add_fusion.me_ref, bf16[256,384]{1,0:T(8,128)(2,1)} %get-tuple-element.48.refs_5_.refs_0_, bf16[256,384]{1,0:T(8,128)(2,1)} %copy-done.32, bf16[256,384]{1,0:T(8,128)(2,1)} %copy-done.33, bf16[256,384]{1,0:T(8,128)(2,1)} %copy-done.34, ...), custom_call_target="tpu_custom_call" | custom-call | flops 3000000000 | bytes 9000000 | tf_op jit(solution)/shard_map/join_proj/pallas_call | solution.py:543
  156.6 2.9 %relay.4 = (bf16[128,1024]{1,0:T(8,128)(2,1)}, bf16[128,1024]{1,0:T(8,128)(2,1)}, bf16[768,1024]{1,0:T(8,128)(2,1)}) custom-call(bf16[256,1024]{1,0:T(8,128)(2,1)} %join_attn.1.own_ref, bf16[256,1024]{1,0:T(8,128)(2,1)} %copy-done.17, bf16[256,1024]{1,0:T(8,128)(2,1)} %copy-done.18, bf16[256,1536]{1,0:T(8,128)(2,1)} %join_proj.1.refs_0_.own_ref.d_proj_ref), custom_call_target="tpu_custom_call" | custom-call | flops 2000000000 | bytes 6000000 | tf_op jit(solution)/shard_map/relay/pallas_call | solution.py:74
  159.5 1.5 collective-permute-start.26
  163.5 5.3 %collective-permute-done.26.refs_1_ = bf16[128,1024]{1,0:T(8,128)(2,1)S(1)} collective-permute-done((bf16[128,1024]{1,0:T(8,128)(2,1)}, bf16[128,1024]{1,0:T(8,128)(2,1)S(1)}, u32[]{:S(2)}, u32[]{:S(2)}) %collective-permute-start.26) | collective-permute-done | bytes 262176 | tf_op jit(solution)/shard_map/ppermute | solution.py:54
  168.8 1.6 collective-permute-done.27.refs_2_
  170.4 1.5 collective-permute-done.30.refs_5_
  173.8 5.0 %d_w_out.1.refs_0_ = f32[4,64,1024]{2,1,0:T(8,128)} custom-call(s32[2]{0:T(128)} %pad_add_fusion.me_ref, bf16[8,512,256]{2,1,0:T(8,128)(2,1)} %copy-done, bf16[768,1024]{1,0:T(8,128)(2,1)} %get-tuple-element.56.refs_0_, bf16[128,1024]{1,0:T(8,128)(2,1)} %copy-done.22, bf16[128,1024]{1,0:T(8,128)(2,1)} %copy-done.23, bf16[768,1024]{1,0:T(8,128)(2,1)} %copy-done.7, ...), custom_call_target="tpu_custom_call" | custom-call | flops 5000000000 | bytes 15000000 | tf_op jit(solution)/shard_map/d_w_out/pallas_call | solution.py:555
  178.8 7.7 %collective-permute-done.24.first_ref = bf16[256,1536]{1,0:T(8,128)(2,1)S(1)} collective-permute-done((bf16[256,1536]{1,0:T(8,128)(2,1)S(1)}, bf16[256,1536]{1,0:T(8,128)(2,1)S(1)}, u32[]{:S(2)}, u32[]{:S(2)}) %collective-permute-start.24) | collective-permute-done | bytes 786464 | tf_op jit(solution)/shard_map/ppermute | solution.py:54
  188.3 3.4 %relay.5 = (bf16[128,1536]{1,0:T(8,128)(2,1)}, bf16[128,1536]{1,0:T(8,128)(2,1)}, bf16[768,1536]{1,0:T(8,128)(2,1)}) custom-call(bf16[256,1536]{1,0:T(8,128)(2,1)} %join_proj.1.refs_0_.own_ref.d_proj_ref, bf16[256,1536]{1,0:T(8,128)(2,1)} %copy-done.11, bf16[256,1536]{1,0:T(8,128)(2,1)} %copy-done.12, f32[4,64,1024]{2,1,0:T(8,128)} %d_w_out.1.refs_0_), custom_call_target="tpu_custom_call" | custom-call | flops 2000000000 | bytes 6000000 | tf_op jit(solution)/shard_map/relay/pallas_call | solution.py:74
  194.5 1.6 collective-permute-start.41
  196.1 2.7 %collective-permute-start.40 = (f32[64,1024]{1,0:T(8,128)}, f32[64,1024]{1,0:T(8,128)}, u32[]{:S(2)}, u32[]{:S(2)}) collective-permute-start(f32[64,1024]{1,0:T(8,128)} %get-tuple-element.71), channel_id=1, source_target_pairs={{0,16},{8,24},{16,0},{24,8},{1,17},{9,25},{17,1},{25,9},{2,18},{10... | collective-permute-start | bytes 786440 | tf_op jit(solution)/shard_map/ppermute | solution.py:54
  198.8 4.7 %collective-permute-done.31.refs_1_ = bf16[128,1536]{1,0:T(8,128)(2,1)} collective-permute-done((bf16[128,1536]{1,0:T(8,128)(2,1)}, bf16[128,1536]{1,0:T(8,128)(2,1)}, u32[]{:S(2)}, u32[]{:S(2)}) %collective-permute-start.31) | collective-permute-done | bytes 393248 | tf_op jit(solution)/shard_map/ppermute | solution.py:54
  204.0 7.9 %d_tokens.1 = (bf16[256,2048]{1,0:T(8,128)(2,1)}, f32[4,8,64]{2,1,0:T(8,128)}) custom-call(s32[2]{0:T(128)} %pad_add_fusion.me_ref, bf16[256,2048]{1,0:T(8,128)(2,1)} %bitcast.36, bf16[256,2048]{1,0:T(8,128)(2,1)} %bitcast.39, bf16[256,1536]{1,0:T(8,128)(2,1)} %join_proj.1.refs_0_.own_ref.d_proj_ref, bf16[816,1792]{1,0:T(8,128)(2,1)} %get-tuple-element.37.refs_0_.refs_8_, ...), custom_call_target="tpu_custom_call" | custom-call | flops 8000000000 | bytes 24000000 | tf_op jit(solution)/shard_map/d_tokens/pallas_call | solution.py:570
  211.9 2.9 %collective-permute-start.39 = (f32[64,1024]{1,0:T(8,128)}, f32[64,1024]{1,0:T(8,128)}, u32[]{:S(2)}, u32[]{:S(2)}) collective-permute-start(f32[64,1024]{1,0:T(8,128)} %get-tuple-element.69), channel_id=1, source_target_pairs={{0,8},{8,0},{16,24},{24,16},{1,9},{9,1},{17,25},{25,17},{2,10},{10... | collective-permute-start | bytes 786440 | tf_op jit(solution)/shard_map/ppermute | solution.py:54
  216.4 6.3 %d_w_qkv.1 = (f32[4,64,1536]{2,1,0:T(8,128)}, f32[4,8,64]{2,1,0:T(8,128)}) custom-call(s32[2]{0:T(128)} %pad_add_fusion.me_ref, bf16[8,512,256]{2,1,0:T(8,128)(2,1)} %copy-done, bf16[768,1536]{1,0:T(8,128)(2,1)} %get-tuple-element.61.refs_0_, bf16[128,1536]{1,0:T(8,128)(2,1)} %collective-permute-done.31.refs_1_, ...), custom_call_target="tpu_custom_call" | custom-call | flops 6000000000 | bytes 18000000 | tf_op jit(solution)/shard_map/d_w_qkv/pallas_call | solution.py:581
  226.3 2.9 %collective-permute-start.36 = (f32[64,1536]{1,0:T(8,128)S(1)}, f32[64,1536]{1,0:T(8,128)S(1)}, u32[]{:S(2)}, u32[]{:S(2)}) collective-permute-start(f32[64,1536]{1,0:T(8,128)S(1)} %get-tuple-element.66), channel_id=1, source_target_pairs={{0,8},{8,0},{16,24},{24,16},{1,9},{9,1},{17,25},{25,17},{2,10},{10... | collective-permute-start | bytes 1179656 | tf_op jit(solution)/shard_map/ppermute | solution.py:54
  229.1 3.3 %all-to-all-start.1 = ((f32[32,1,64]{2,1,0:T(1,128)}), f32[32,1,64]{2,1,0:T(1,128)S(1)}, u32[]{:S(2)}, u32[]{:S(2)}) async-start(f32[32,1,64]{2,1,0:T(1,128)} %bitcast.16), calls=%async_computation.1 | async-start | bytes 32768 | tf_op jit(solution)/shard_map/all_to_all | solution.py:593
  232.5 1.9 fusion.4
  234.4 27.8 %all-to-all-done.1 = f32[32,1,64]{2,1,0:T(1,128)S(1)} async-done(((f32[32,1,64]{2,1,0:T(1,128)}), f32[32,1,64]{2,1,0:T(1,128)S(1)}, u32[]{:S(2)}, u32[]{:S(2)}) %all-to-all-start.1) | async-done | bytes 8224 | tf_op jit(solution)/shard_map/all_to_all | solution.py:593
  262.8 1.8 fusion.2
  (149 shorter events, 31.4 us)
Async XLA Ops:
  5.5 31.1 %collective-permute-start = (bf16[272,1792]{1,0:T(8,128)(2,1)}, bf16[272,1792]{1,0:T(8,128)(2,1)S(1)}, u32[]{:S(2)}, u32[]{:S(2)}) collective-permute-start(bf16[272,1792]{1,0:T(8,128)(2,1)} %get-tuple-element.35.own_ref), channel_id=1, source_target_pairs={{0,2},{1,3},{2,0},{3,1},{4,6},{5,7},{6,4},{7,5},{8,10},{9,11},{10,... | collective-permute-start | bytes 2924552 | tf_op jit(solution)/shard_map/ppermute | solution.py:54
  8.4 28.2 %collective-permute-start.1 = (bf16[272,1792]{1,0:T(8,128)(2,1)}, bf16[272,1792]{1,0:T(8,128)(2,1)S(1)}, u32[]{:S(2)}, u32[]{:S(2)}) collective-permute-start(bf16[272,1792]{1,0:T(8,128)(2,1)} %get-tuple-element.35.own_ref), channel_id=1, source_target_pairs={{0,4},{1,5},{2,6},{3,7},{4,0},{5,1},{6,2},{7,3},{8,12},{9,13},{10,... | collective-permute-start | bytes 2924552 | tf_op jit(solution)/shard_map/ppermute | solution.py:54
  9.9 32.6 %copy-start.13 = (bf16[128,2048]{1,0:T(8,128)(2,1)S(1)}, bf16[128,2048]{1,0:T(8,128)(2,1)}, u32[]{:S(2)}) copy-start(bf16[128,2048]{1,0:T(8,128)(2,1)} %get-tuple-element.40.refs_4_) | copy-start | bytes 1572868
  9.9 35.8 %copy-start.38 = (s32[1,10]{1,0:T(1,128)S(1)}, s32[1,10]{1,0:T(1,128)}, u32[]{:S(2)}) copy-start(s32[1,10]{1,0:T(1,128)} %param.8) | copy-start | bytes 124
  9.9 14.3 %collective-permute-start.2 = (bf16[128,2048]{1,0:T(8,128)(2,1)}, bf16[128,2048]{1,0:T(8,128)(2,1)S(1)}, u32[]{:S(2)}, u32[]{:S(2)}) collective-permute-start(bf16[128,2048]{1,0:T(8,128)(2,1)} %get-tuple-element.36.refs_0_), channel_id=1, source_target_pairs={{0,8},{8,0},{16,24},{24,16},{1,9},{9,1},{17,25},{25,17},{2,10},{10... | collective-permute-start | bytes 1572872 | tf_op jit(solution)/shard_map/ppermute | solution.py:54
  11.5 25.1 %collective-permute-start.3 = (bf16[128,2048]{1,0:T(8,128)(2,1)}, bf16[128,2048]{1,0:T(8,128)(2,1)S(1)}, u32[]{:S(2)}, u32[]{:S(2)}) collective-permute-start(bf16[128,2048]{1,0:T(8,128)(2,1)} %get-tuple-element.36.refs_0_), channel_id=1, source_target_pairs={{0,24},{8,16},{16,8},{24,0},{1,25},{9,17},{17,9},{25,1},{2,26},{10... | collective-permute-start | bytes 1572872 | tf_op jit(solution)/shard_map/ppermute | solution.py:54
  42.5 27.3 %collective-permute-start.6 = (bf16[816,1792]{1,0:T(8,128)(2,1)}, bf16[816,1792]{1,0:T(8,128)(2,1)S(1)}, u32[]{:S(2)}, u32[]{:S(2)}) collective-permute-start(bf16[816,1792]{1,0:T(8,128)(2,1)} %get-tuple-element.37.refs_0_.refs_8_), channel_id=1, source_target_pairs={{0,1},{1,0},{2,3},{3,2},{4,5},{5,4},{6,7},{7,6},{8,9},{9,8},{10,11... | collective-permute-start | bytes 8773640 | tf_op jit(solution)/shard_map/ppermute | solution.py:54
  42.5 20.9 %collective-permute-start.9 = (bf16[128,2048]{1,0:T(8,128)(2,1)S(1)}, bf16[128,2048]{1,0:T(8,128)(2,1)}, u32[]{:S(2)}, u32[]{:S(2)}) collective-permute-start(bf16[128,2048]{1,0:T(8,128)(2,1)S(1)} %copy-done.13), channel_id=1, source_target_pairs={{0,8},{8,0},{16,24},{24,16},{1,9},{9,1},{17,25},{25,17},{2,10},{10... | collective-permute-start | bytes 1572872 | tf_op jit(solution)/shard_map/ppermute | solution.py:54
  43.1 26.6 %collective-permute-start.10 = (bf16[128,2048]{1,0:T(8,128)(2,1)S(1)}, bf16[128,2048]{1,0:T(8,128)(2,1)}, u32[]{:S(2)}, u32[]{:S(2)}) collective-permute-start(bf16[128,2048]{1,0:T(8,128)(2,1)S(1)} %copy-done.13), channel_id=1, source_target_pairs={{0,24},{8,16},{16,8},{24,0},{1,25},{9,17},{17,9},{25,1},{2,26},{10... | collective-permute-start | bytes 1572872 | tf_op jit(solution)/shard_map/ppermute | solution.py:54
  45.9 14.3 %collective-permute-start.4 = (bf16[128,1792]{1,0:T(8,128)(2,1)}, bf16[128,1792]{1,0:T(8,128)(2,1)}, u32[]{:S(2)}, u32[]{:S(2)}) collective-permute-start(bf16[128,1792]{1,0:T(8,128)(2,1)} %get-tuple-element.38), channel_id=1, source_target_pairs={{0,4},{1,5},{2,6},{3,7},{4,0},{5,1},{6,2},{7,3},{8,12},{9,13},{10,... | collective-permute-start | bytes 1376264 | tf_op jit(solution)/shard_map/ppermute | solution.py:54
  46.4 13.6 %collective-permute-start.5 = (bf16[144,1792]{1,0:T(8,128)(2,1)}, bf16[144,1792]{1,0:T(8,128)(2,1)}, u32[]{:S(2)}, u32[]{:S(2)}) collective-permute-start(bf16[144,1792]{1,0:T(8,128)(2,1)} %get-tuple-element.39), channel_id=1, source_target_pairs={{0,2},{1,3},{2,0},{3,1},{4,6},{5,7},{6,4},{7,5},{8,10},{9,11},{10,... | collective-permute-start | bytes 1548296 | tf_op jit(solution)/shard_map/ppermute | solution.py:54
  60.0 9.7 %collective-permute-start.8 = (bf16[144,1792]{1,0:T(8,128)(2,1)}, bf16[144,1792]{1,0:T(8,128)(2,1)}, u32[]{:S(2)}, u32[]{:S(2)}) collective-permute-start(bf16[144,1792]{1,0:T(8,128)(2,1)} %collective-permute-done.5.refs_2_.refs_10_), channel_id=1, source_target_pairs={{0,1},{1,0},{2,3},{3,2},{4,5},{5,4},{6,7},{7,6},{8,9},{9,8},{10,11... | collective-permute-start | bytes 1548296 | tf_op jit(solution)/shard_map/ppermute | solution.py:54
  60.1 9.6 %collective-permute-start.7 = (bf16[128,1792]{1,0:T(8,128)(2,1)}, bf16[128,1792]{1,0:T(8,128)(2,1)S(1)}, u32[]{:S(2)}, u32[]{:S(2)}) collective-permute-start(bf16[128,1792]{1,0:T(8,128)(2,1)} %collective-permute-done.4.refs_1_.refs_9_), channel_id=1, source_target_pairs={{0,1},{1,0},{2,3},{3,2},{4,5},{5,4},{6,7},{7,6},{8,9},{9,8},{10,11... | collective-permute-start | bytes 1376264 | tf_op jit(solution)/shard_map/ppermute | solution.py:54
  62.6 16.8 %copy-start.2 = (f32[1024,128]{1,0:T(8,128)}, f32[1024,128]{1,0:T(8,128)S(1)}, u32[]{:S(2)}) copy-start(f32[1024,128]{1,0:T(8,128)S(1)} %get-tuple-element.72.sin_ref) | copy-start | bytes 1572868
  62.6 16.8 %copy-start.3 = (f32[1024,128]{1,0:T(8,128)}, f32[1024,128]{1,0:T(8,128)S(1)}, u32[]{:S(2)}) copy-start(f32[1024,128]{1,0:T(8,128)S(1)} %get-tuple-element.73.cos_ref) | copy-start | bytes 1572868
  63.4 27.8 %collective-permute-start.14 = (bf16[128,2048]{1,0:T(8,128)(2,1)}, bf16[128,2048]{1,0:T(8,128)(2,1)}, u32[]{:S(2)}, u32[]{:S(2)}) collective-permute-start(bf16[128,2048]{1,0:T(8,128)(2,1)} %copy-done.15), channel_id=1, source_target_pairs={{0,8},{8,0},{16,24},{24,16},{1,9},{9,1},{17,25},{25,17},{2,10},{10... | collective-permute-start | bytes 1572872 | tf_op jit(solution)/shard_map/ppermute | solution.py:54
  69.7 26.3 %collective-permute-start.15 = (bf16[128,2048]{1,0:T(8,128)(2,1)}, bf16[128,2048]{1,0:T(8,128)(2,1)S(1)}, u32[]{:S(2)}, u32[]{:S(2)}) collective-permute-start(bf16[128,2048]{1,0:T(8,128)(2,1)} %collective-permute-done.10.refs_7_), channel_id=1, source_target_pairs={{0,8},{8,0},{16,24},{24,16},{1,9},{9,1},{17,25},{25,17},{2,10},{10... | collective-permute-start | bytes 1572872 | tf_op jit(solution)/shard_map/ppermute | solution.py:54
  79.3 24.0 %collective-permute-start.11 = (bf16[256,384]{1,0:T(8,128)(2,1)}, bf16[256,384]{1,0:T(8,128)(2,1)S(1)}, u32[]{:S(2)}, u32[]{:S(2)}) collective-permute-start(bf16[256,384]{1,0:T(8,128)(2,1)} %get-tuple-element.42), channel_id=1, source_target_pairs={{0,8},{8,0},{16,24},{24,16},{1,9},{9,1},{17,25},{25,17},{2,10},{10... | collective-permute-start | bytes 589832 | tf_op jit(solution)/shard_map/ppermute | solution.py:54
  81.4 21.9 %collective-permute-start.12 = (bf16[256,384]{1,0:T(8,128)(2,1)}, bf16[256,384]{1,0:T(8,128)(2,1)S(1)}, u32[]{:S(2)}, u32[]{:S(2)}) collective-permute-start(bf16[256,384]{1,0:T(8,128)(2,1)} %get-tuple-element.43), channel_id=1, source_target_pairs={{0,16},{8,24},{16,0},{24,8},{1,17},{9,25},{17,1},{25,9},{2,18},{10... | collective-permute-start | bytes 589832 | tf_op jit(solution)/shard_map/ppermute | solution.py:54
  81.7 22.7 %collective-permute-start.13 = (bf16[256,384]{1,0:T(8,128)(2,1)}, bf16[256,384]{1,0:T(8,128)(2,1)S(1)}, u32[]{:S(2)}, u32[]{:S(2)}) collective-permute-start(bf16[256,384]{1,0:T(8,128)(2,1)} %get-tuple-element.44), channel_id=1, source_target_pairs={{0,24},{8,16},{16,8},{24,0},{1,25},{9,17},{17,9},{25,1},{2,26},{10... | collective-permute-start | bytes 589832 | tf_op jit(solution)/shard_map/ppermute | solution.py:54
  87.4 43.8 %all-to-all-start = ((bf16[8,512,256]{2,1,0:T(8,128)(2,1)}), bf16[8,512,256]{2,1,0:T(8,128)(2,1)S(1)}, u32[]{:S(2)}, u32[]{:S(2)}) async-start(bf16[8,512,256]{2,1,0:T(8,128)(2,1)} %slices.1.refs_14_), calls=%async_computation | async-start | bytes 4194304 | tf_op jit(solution)/shard_map/all_to_all | solution.py:486
  113.8 17.3 %collective-permute-start.19 = (bf16[256,256]{1,0:T(8,128)(2,1)}, bf16[256,256]{1,0:T(8,128)(2,1)S(1)}, u32[]{:S(2)}, u32[]{:S(2)}) collective-permute-start(bf16[256,256]{1,0:T(8,128)(2,1)} %get-tuple-element.53), channel_id=1, source_target_pairs={{0,8},{8,0},{16,24},{24,16},{1,9},{9,1},{17,25},{25,17},{2,10},{10... | collective-permute-start | bytes 393224 | tf_op jit(solution)/shard_map/ppermute | solution.py:54
  113.8 17.3 %collective-permute-start.20 = (bf16[256,256]{1,0:T(8,128)(2,1)}, bf16[256,256]{1,0:T(8,128)(2,1)S(1)}, u32[]{:S(2)}, u32[]{:S(2)}) collective-permute-start(bf16[256,256]{1,0:T(8,128)(2,1)} %get-tuple-element.54), channel_id=1, source_target_pairs={{0,16},{8,24},{16,0},{24,8},{1,17},{9,25},{17,1},{25,9},{2,18},{10... | collective-permute-start | bytes 393224 | tf_op jit(solution)/shard_map/ppermute | solution.py:54
  115.7 15.4 %collective-permute-start.21 = (bf16[256,256]{1,0:T(8,128)(2,1)}, bf16[256,256]{1,0:T(8,128)(2,1)S(1)}, u32[]{:S(2)}, u32[]{:S(2)}) collective-permute-start(bf16[256,256]{1,0:T(8,128)(2,1)} %get-tuple-element.55), channel_id=1, source_target_pairs={{0,24},{8,16},{16,8},{24,0},{1,25},{9,17},{17,9},{25,1},{2,26},{10... | collective-permute-start | bytes 393224 | tf_op jit(solution)/shard_map/ppermute | solution.py:54
  134.6 17.5 %collective-permute-start.22 = (bf16[256,1024]{1,0:T(8,128)(2,1)}, bf16[256,1024]{1,0:T(8,128)(2,1)S(1)}, u32[]{:S(2)}, u32[]{:S(2)}) collective-permute-start(bf16[256,1024]{1,0:T(8,128)(2,1)} %join_attn.1.own_ref), channel_id=1, source_target_pairs={{0,2},{1,3},{2,0},{3,1},{4,6},{5,7},{6,4},{7,5},{8,10},{9,11},{10,... | collective-permute-start | bytes 1572872 | tf_op jit(solution)/shard_map/ppermute | solution.py:54
  135.1 17.0 %collective-permute-start.23 = (bf16[256,1024]{1,0:T(8,128)(2,1)}, bf16[256,1024]{1,0:T(8,128)(2,1)S(1)}, u32[]{:S(2)}, u32[]{:S(2)}) collective-permute-start(bf16[256,1024]{1,0:T(8,128)(2,1)} %join_attn.1.own_ref), channel_id=1, source_target_pairs={{0,4},{1,5},{2,6},{3,7},{4,0},{5,1},{6,2},{7,3},{8,12},{9,13},{10,... | collective-permute-start | bytes 1572872 | tf_op jit(solution)/shard_map/ppermute | solution.py:54
  135.6 8.4 %collective-permute-start.16 = (bf16[256,384]{1,0:T(8,128)(2,1)S(1)}, bf16[256,384]{1,0:T(8,128)(2,1)S(1)}, u32[]{:S(2)}, u32[]{:S(2)}) collective-permute-start(bf16[256,384]{1,0:T(8,128)(2,1)S(1)} %copy-done.31), channel_id=1, source_target_pairs={{0,8},{8,0},{16,24},{24,16},{1,9},{9,1},{17,25},{25,17},{2,10},{10... | collective-permute-start | bytes 589832 | tf_op jit(solution)/shard_map/ppermute | solution.py:54
  135.6 16.5 %collective-permute-start.17 = (bf16[256,384]{1,0:T(8,128)(2,1)S(1)}, bf16[256,384]{1,0:T(8,128)(2,1)S(1)}, u32[]{:S(2)}, u32[]{:S(2)}) collective-permute-start(bf16[256,384]{1,0:T(8,128)(2,1)S(1)} %copy-done.30), channel_id=1, source_target_pairs={{0,16},{8,24},{16,0},{24,8},{1,17},{9,25},{17,1},{25,9},{2,18},{10... | collective-permute-start | bytes 589832 | tf_op jit(solution)/shard_map/ppermute | solution.py:54
  137.5 14.6 %collective-permute-start.18 = (bf16[256,384]{1,0:T(8,128)(2,1)S(1)}, bf16[256,384]{1,0:T(8,128)(2,1)S(1)}, u32[]{:S(2)}, u32[]{:S(2)}) collective-permute-start(bf16[256,384]{1,0:T(8,128)(2,1)S(1)} %copy-done.29), channel_id=1, source_target_pairs={{0,24},{8,16},{16,8},{24,0},{1,25},{9,17},{17,9},{25,1},{2,26},{10... | collective-permute-start | bytes 589832 | tf_op jit(solution)/shard_map/ppermute | solution.py:54
  159.5 12.4 %collective-permute-start.28 = (bf16[768,1024]{1,0:T(8,128)(2,1)}, bf16[768,1024]{1,0:T(8,128)(2,1)S(1)}, u32[]{:S(2)}, u32[]{:S(2)}) collective-permute-start(bf16[768,1024]{1,0:T(8,128)(2,1)} %get-tuple-element.56.refs_0_), channel_id=1, source_target_pairs={{0,1},{1,0},{2,3},{3,2},{4,5},{5,4},{6,7},{7,6},{8,9},{9,8},{10,11... | collective-permute-start | bytes 4718600 | tf_op jit(solution)/shard_map/ppermute | solution.py:54
  159.5 9.3 %collective-permute-start.26 = (bf16[128,1024]{1,0:T(8,128)(2,1)}, bf16[128,1024]{1,0:T(8,128)(2,1)S(1)}, u32[]{:S(2)}, u32[]{:S(2)}) collective-permute-start(bf16[128,1024]{1,0:T(8,128)(2,1)} %get-tuple-element.57), channel_id=1, source_target_pairs={{0,4},{1,5},{2,6},{3,7},{4,0},{5,1},{6,2},{7,3},{8,12},{9,13},{10,... | collective-permute-start | bytes 786440 | tf_op jit(solution)/shard_map/ppermute | solution.py:54
  161.0 9.4 %collective-permute-start.27 = (bf16[128,1024]{1,0:T(8,128)(2,1)}, bf16[128,1024]{1,0:T(8,128)(2,1)S(1)}, u32[]{:S(2)}, u32[]{:S(2)}) collective-permute-start(bf16[128,1024]{1,0:T(8,128)(2,1)} %get-tuple-element.58), channel_id=1, source_target_pairs={{0,2},{1,3},{2,0},{3,1},{4,6},{5,7},{6,4},{7,5},{8,10},{9,11},{10,... | collective-permute-start | bytes 786440 | tf_op jit(solution)/shard_map/ppermute | solution.py:54
  162.5 24.0 %collective-permute-start.24 = (bf16[256,1536]{1,0:T(8,128)(2,1)S(1)}, bf16[256,1536]{1,0:T(8,128)(2,1)S(1)}, u32[]{:S(2)}, u32[]{:S(2)}) collective-permute-start(bf16[256,1536]{1,0:T(8,128)(2,1)S(1)} %copy-done.10), channel_id=1, source_target_pairs={{0,2},{1,3},{2,0},{3,1},{4,6},{5,7},{6,4},{7,5},{8,10},{9,11},{10,... | collective-permute-start | bytes 2359304 | tf_op jit(solution)/shard_map/ppermute | solution.py:54
  163.0 23.5 %collective-permute-start.25 = (bf16[256,1536]{1,0:T(8,128)(2,1)S(1)}, bf16[256,1536]{1,0:T(8,128)(2,1)S(1)}, u32[]{:S(2)}, u32[]{:S(2)}) collective-permute-start(bf16[256,1536]{1,0:T(8,128)(2,1)S(1)} %copy-done.10), channel_id=1, source_target_pairs={{0,4},{1,5},{2,6},{3,7},{4,0},{5,1},{6,2},{7,3},{8,12},{9,13},{10,... | collective-permute-start | bytes 2359304 | tf_op jit(solution)/shard_map/ppermute | solution.py:54
  168.8 1.6 collective-permute-start.29
  170.4 1.5 collective-permute-start.30
  191.7 23.2 %collective-permute-start.33 = (bf16[768,1536]{1,0:T(8,128)(2,1)}, bf16[768,1536]{1,0:T(8,128)(2,1)S(1)}, u32[]{:S(2)}, u32[]{:S(2)}) collective-permute-start(bf16[768,1536]{1,0:T(8,128)(2,1)} %get-tuple-element.61.refs_0_), channel_id=1, source_target_pairs={{0,1},{1,0},{2,3},{3,2},{4,5},{5,4},{6,7},{7,6},{8,9},{9,8},{10,11... | collective-permute-start | bytes 7077896 | tf_op jit(solution)/shard_map/ppermute | solution.py:54
  191.7 11.8 %collective-permute-start.31 = (bf16[128,1536]{1,0:T(8,128)(2,1)}, bf16[128,1536]{1,0:T(8,128)(2,1)}, u32[]{:S(2)}, u32[]{:S(2)}) collective-permute-start(bf16[128,1536]{1,0:T(8,128)(2,1)} %get-tuple-element.59.refs_6_), channel_id=1, source_target_pairs={{0,4},{1,5},{2,6},{3,7},{4,0},{5,1},{6,2},{7,3},{8,12},{9,13},{10,... | collective-permute-start | bytes 1179656 | tf_op jit(solution)/shard_map/ppermute | solution.py:54
  192.2 11.6 %collective-permute-start.32 = (bf16[128,1536]{1,0:T(8,128)(2,1)}, bf16[128,1536]{1,0:T(8,128)(2,1)}, u32[]{:S(2)}, u32[]{:S(2)}) collective-permute-start(bf16[128,1536]{1,0:T(8,128)(2,1)} %get-tuple-element.62), channel_id=1, source_target_pairs={{0,2},{1,3},{2,0},{3,1},{4,6},{5,7},{6,4},{7,5},{8,10},{9,11},{10,... | collective-permute-start | bytes 1179656 | tf_op jit(solution)/shard_map/ppermute | solution.py:54
  194.5 31.1 %collective-permute-start.41 = (f32[64,1024]{1,0:T(8,128)S(1)}, f32[64,1024]{1,0:T(8,128)S(1)}, u32[]{:S(2)}, u32[]{:S(2)}) collective-permute-start(f32[64,1024]{1,0:T(8,128)S(1)} %get-tuple-element.70), channel_id=1, source_target_pairs={{0,24},{8,16},{16,8},{24,0},{1,25},{9,17},{17,9},{25,1},{2,26},{10... | collective-permute-start | bytes 786440 | tf_op jit(solution)/shard_map/ppermute | solution.py:54
  196.1 36.4 %collective-permute-start.40 = (f32[64,1024]{1,0:T(8,128)}, f32[64,1024]{1,0:T(8,128)}, u32[]{:S(2)}, u32[]{:S(2)}) collective-permute-start(f32[64,1024]{1,0:T(8,128)} %get-tuple-element.71), channel_id=1, source_target_pairs={{0,16},{8,24},{16,0},{24,8},{1,17},{9,25},{17,1},{25,9},{2,18},{10... | collective-permute-start | bytes 786440 | tf_op jit(solution)/shard_map/ppermute | solution.py:54
  203.5 8.4 %collective-permute-start.34 = (bf16[128,1536]{1,0:T(8,128)(2,1)}, bf16[128,1536]{1,0:T(8,128)(2,1)S(1)}, u32[]{:S(2)}, u32[]{:S(2)}) collective-permute-start(bf16[128,1536]{1,0:T(8,128)(2,1)} %collective-permute-done.31.refs_1_), channel_id=1, source_target_pairs={{0,1},{1,0},{2,3},{3,2},{4,5},{5,4},{6,7},{7,6},{8,9},{9,8},{10,11... | collective-permute-start | bytes 1179656 | tf_op jit(solution)/shard_map/ppermute | solution.py:54
  203.8 11.1 %collective-permute-start.35 = (bf16[128,1536]{1,0:T(8,128)(2,1)}, bf16[128,1536]{1,0:T(8,128)(2,1)S(1)}, u32[]{:S(2)}, u32[]{:S(2)}) collective-permute-start(bf16[128,1536]{1,0:T(8,128)(2,1)} %collective-permute-done.32.refs_2_), channel_id=1, source_target_pairs={{0,1},{1,0},{2,3},{3,2},{4,5},{5,4},{6,7},{7,6},{8,9},{9,8},{10,11... | collective-permute-start | bytes 1179656 | tf_op jit(solution)/shard_map/ppermute | solution.py:54
  211.9 20.6 %collective-permute-start.39 = (f32[64,1024]{1,0:T(8,128)}, f32[64,1024]{1,0:T(8,128)}, u32[]{:S(2)}, u32[]{:S(2)}) collective-permute-start(f32[64,1024]{1,0:T(8,128)} %get-tuple-element.69), channel_id=1, source_target_pairs={{0,8},{8,0},{16,24},{24,16},{1,9},{9,1},{17,25},{25,17},{2,10},{10... | collective-permute-start | bytes 786440 | tf_op jit(solution)/shard_map/ppermute | solution.py:54
  224.0 38.8 %collective-permute-start.38 = (f32[64,1536]{1,0:T(8,128)S(1)}, f32[64,1536]{1,0:T(8,128)S(1)}, u32[]{:S(2)}, u32[]{:S(2)}) collective-permute-start(f32[64,1536]{1,0:T(8,128)S(1)} %get-tuple-element.67), channel_id=1, source_target_pairs={{0,24},{8,16},{16,8},{24,0},{1,25},{9,17},{17,9},{25,1},{2,26},{10... | collective-permute-start | bytes 1179656 | tf_op jit(solution)/shard_map/ppermute | solution.py:54
  225.4 37.4 %collective-permute-start.37 = (f32[64,1536]{1,0:T(8,128)S(1)}, f32[64,1536]{1,0:T(8,128)S(1)}, u32[]{:S(2)}, u32[]{:S(2)}) collective-permute-start(f32[64,1536]{1,0:T(8,128)S(1)} %get-tuple-element.68), channel_id=1, source_target_pairs={{0,16},{8,24},{16,0},{24,8},{1,17},{9,25},{17,1},{25,9},{2,18},{10... | collective-permute-start | bytes 1179656 | tf_op jit(solution)/shard_map/ppermute | solution.py:54
  226.3 36.5 %collective-permute-start.36 = (f32[64,1536]{1,0:T(8,128)S(1)}, f32[64,1536]{1,0:T(8,128)S(1)}, u32[]{:S(2)}, u32[]{:S(2)}) collective-permute-start(f32[64,1536]{1,0:T(8,128)S(1)} %get-tuple-element.66), channel_id=1, source_target_pairs={{0,8},{8,0},{16,24},{24,16},{1,9},{9,1},{17,25},{25,17},{2,10},{10... | collective-permute-start | bytes 1179656 | tf_op jit(solution)/shard_map/ppermute | solution.py:54
  229.1 33.1 %all-to-all-start.1 = ((f32[32,1,64]{2,1,0:T(1,128)}), f32[32,1,64]{2,1,0:T(1,128)S(1)}, u32[]{:S(2)}, u32[]{:S(2)}) async-start(f32[32,1,64]{2,1,0:T(1,128)} %bitcast.16), calls=%async_computation.1 | async-start | bytes 32768 | tf_op jit(solution)/shard_map/all_to_all | solution.py:593
  (35 other events, 83.9 us)

commit v3 on v2

--- a/solution.py
+++ b/solution.py
@@ -59,39 +59,16 @@
     return swap(a, axis, n // 4), swap(a, axis, n // 2)
 
 
-def relay(own, first, second, *earlier):
-    rows, columns = own.shape
+def complete(own, first, second, axis):
+    n = lax.axis_size(axis)
+    rows = own.shape[0]
     half = rows // 32 * 16
-
-    def kernel(own_ref, first_ref, second_ref, *refs):
-        upper, lower, trio = refs[-3:]
-        upper[...] = first_ref[:half, :]
-        lower[...] = second_ref[half:, :]
-        trio[:rows, :] = own_ref[...]
-        trio[rows : 2 * rows, :] = first_ref[...]
-        trio[2 * rows :, :] = second_ref[...]
-
-    return pl.pallas_call(
-        kernel,
-        out_shape=[shape(half, columns), shape(rows - half, columns), shape(3 * rows, columns)],
-        in_specs=[VMEM] * 3 + [ANY] * len(earlier),
-        out_specs=[VMEM] * 3,
-        compiler_params=params(56),
-        cost_estimate=about(2),
-        name="relay",
-    )(own, first, second, *earlier)
-
-
-def complete(upper, lower, trio, axis):
-    n = lax.axis_size(axis)
-    rows, half = trio.shape[0] // 3, upper.shape[0]
-    upper, lower = swap(upper, axis, n // 2), swap(lower, axis, n // 4)
-    arrays = [trio, upper, lower]
+    arrays = [own, first, second, swap(first[:half], axis, n // 2), swap(second[half:], axis, n // 4)]
     slots = {
         0: [(0, 0, rows)],
-        n // 4: [(0, rows, rows)],
-        n // 2: [(0, 2 * rows, rows)],
-        n // 4 | n // 2: [(1, 0, half), (2, 0, rows - half)],
+        n // 4: [(1, 0, rows)],
+        n // 2: [(2, 0, rows)],
+        n // 4 | n // 2: [(3, 0, half), (4, 0, rows - half)],
     }
     bit = n // 8
     while bit >= 1:
@@ -163,32 +140,21 @@
                 outs[j][...] = piece
 
 
-def spread(own, axis):
-    n = lax.axis_size(axis)
-    slots = {0: own}
-    far = 1
-    while far < n:
-        slots[far] = swap(own, axis, far)
-        for j in range(1, (far + 1) // 2):
-            slots[far ^ j] = swap(slots[far], axis, j)
-        far = 2 * far + 1
-    return [slots[j] for j in range(n)]
-
-
-def d_attn_kernel(slots, groups, columns, me_ref, *refs):
-    shards, arrays = refs[: 2 * groups], refs[2 * groups :]
-    out, weight = refs[-2:]
+def d_attn_kernel(slots, sets, columns, me_ref, own_ref, pair_ref, *refs):
+    outs, weight = refs[-1 - sets : -1], refs[-1]
     u, d = me_ref[0], me_ref[1]
     n = len(slots)
-    rows, width = shards[0].shape
+    rows, width = own_ref.shape
     part = width // n
     for j in range(n):
         at = pl.multiple_of((d ^ j) * part, part)
-        weight[pl.ds(at, part), :] = whole_slot(arrays, slots[j], part)[0][:, columns:]
-    for side in range(2):
-        for j in range(groups):
-            at = pl.multiple_of((2 * (u ^ j) + side) * rows, rows)
-            out[pl.ds(at, rows), :] = nn(shards[side * groups + j][...], weight[...]).astype(bf16)
+        weight[pl.ds(at, part), :] = whole_slot(refs, slots[j], part)[0][:, columns:]
+    for side, ref in enumerate((own_ref, pair_ref)):
+        at = pl.ds(pl.multiple_of((u % 2 ^ side) * rows, rows), rows)
+        value = nn(ref[...], weight[...]).astype(bf16)
+        qw = value.shape[1] // sets
+        for i in range(sets):
+            outs[i][at, :] = value[:, i * qw : (i + 1) * qw]
 
 
 def slices_kernel(n, groups, normed_ref, d_out_ref, *refs):
@@ -220,7 +186,7 @@
 
         @pl.when((u ^ g) == j)
         def _():
-            out[...] = value
+            out[...] = value.astype(out.dtype)
 
 
 def doc_starts(lengths_ref):
@@ -278,13 +244,14 @@
 
 
 def backward_kernel(groups, me_ref, lengths_ref, cos_ref, sin_ref, o_ref, stats_ref, *refs):
-    qkv_pieces, g_all = refs[:groups], refs[groups]
-    q_all, kv_all, dq_all, acc = refs[-4:]
-    outs = refs[-4 - groups : -4]
+    qkv_pieces, grad_pieces = refs[:groups], refs[groups : groups + groups // 2]
+    q_all, kv_all, g_all, dq_all, acc = refs[-5:]
+    outs = refs[-5 - groups : -5]
     u = me_ref[0]
     length, qw = q_all.shape
     heads = qw // HEAD_DIM
     collect(u, qkv_pieces, (q_all, SCALE), (kv_all, None))
+    collect(u // 2, grad_pieces, (g_all, None))
     starts = doc_starts(lengths_ref)
     acc[...] = jnp.zeros_like(acc)
     for b in range(length // Q_BLOCK):
@@ -372,8 +339,8 @@
 
 def grads_kernel(slots, side, groups, factor, me_ref, slices, *refs):
     n = len(slots)
-    out, acc = refs[-2:]
-    d = me_ref[1]
+    outs, acc = refs[-1 - groups : -1], refs[-1]
+    u, d = me_ref[0], me_ref[1]
     kept = acc.shape[0]
     for j in range(n):
         a = slices[d ^ j, side * kept : (side + 1) * kept, :]
@@ -385,45 +352,50 @@
             acc[...] += term
     block = kept // groups
     for g in range(groups):
-        out[g] = acc[g * block : (g + 1) * block, :] * factor
+        hand_out(u, g, acc[g * block : (g + 1) * block, :] * factor, outs)
 
 
 def grads_and_pass_kernel(slots, side, groups, factor, me_ref, slices, *refs):
-    *refs, pass_ref, out, pass_out, acc = refs
-    grads_kernel(slots, side, groups, factor, me_ref, slices, *refs, out, acc)
+    refs, (pass_ref, *outs, pass_out, acc) = refs[: -3 - groups], refs[-3 - groups :]
+    grads_kernel(slots, side, groups, factor, me_ref, slices, *refs, *outs, acc)
     pass_out[...] = pass_ref[...]
 
 
-def block_sum(local, axis):
-    me = lax.axis_index(axis)
-    total = lax.dynamic_index_in_dim(local, me, 0, keepdims=False)
-    for j in range(1, lax.axis_size(axis)):
-        total = total + swap(lax.dynamic_index_in_dim(local, me ^ j, 0, keepdims=False), axis, j)
-    return total
-
-
-def weights_here(w_qkv, w_out, gain, me, qw, grad_rows):
+def weights_here(w_qkv, w_out, gain, me, qw):
     part, columns = w_qkv.shape
-    rows, width = grad_rows.shape
-    half = rows // 2
-
-    def kernel(me_ref, w_qkv_ref, w_out_ref, gain_ref, grad_ref, out, upper, lower):
-        at = pl.multiple_of(me_ref[0] * qw, qw)
+    sets = QW // qw // 2
+
+    def kernel(me_ref, w_qkv_ref, w_out_ref, gain_ref, out):
         out[:part, :columns] = w_qkv_ref[...]
-        out[:part, columns:] = w_out_ref[:, pl.ds(at, qw)]
+        for i in range(sets):
+            at = pl.multiple_of((me_ref[0] ^ (2 * i)) * qw, qw)
+            out[:part, columns + i * qw : columns + (i + 1) * qw] = w_out_ref[:, pl.ds(at, qw)]
         out[part:, :] = jnp.zeros_like(out[part:, :])
         out[part : part + 1, :part] = gain_ref[...]
-        upper[...] = grad_ref[:half, :]
-        lower[...] = grad_ref[half:, :]
 
     return pl.pallas_call(
         kernel,
-        out_shape=[shape(part + 16, columns + qw)] + [shape(half, width)] * 2,
-        in_specs=[SMEM] + [VMEM] * 4,
-        out_specs=[VMEM] * 3,
+        out_shape=shape(part + 16, columns + sets * qw),
+        in_specs=[SMEM] + [VMEM] * 3,
+        out_specs=VMEM,
         cost_estimate=about(2),
         name="weights_here",
-    )(me, w_qkv, w_out, gain[None, :], grad_rows)
+    )(me, w_qkv, w_out, gain[None, :])
+
+
+def after(value, *earlier):
+    def kernel(*refs):
+        del refs
+
+    return pl.pallas_call(
+        kernel,
+        out_shape=shape(*value.shape),
+        in_specs=[ANY] * (1 + len(earlier)),
+        out_specs=ANY,
+        input_output_aliases={0: 0},
+        cost_estimate=about(0.1),
+        name="after",
+    )(value, *earlier)
 
 
 def shape(*dims, dtype=bf16):
@@ -445,10 +417,10 @@
     block = width // (groups * n)
     kept = block * groups
 
-    held, *grad_halves = weights_here(w_qkv, w_out, gain, me, qw, grad_rows)
+    held = weights_here(w_qkv, w_out, gain, me, qw)
     held_near = neighbours(held, "dp")
-    first, second = (spread(half, "ulysses") for half in grad_halves)
-    held_arrays, held_slots = complete(*relay(held, *held_near, first[1], first[groups - 1]), "dp")
+    grad_pair = swap(grad_rows, "ulysses", 1)
+    held_arrays, held_slots = complete(held, after(held_near[0], grad_pair), held_near[1], "dp")
 
     bounds = jnp.cumsum(lengths[0]) - lengths[0]
     places = jnp.arange(length, dtype=jnp.int32)
@@ -464,13 +436,13 @@
     *pieces, normed = pl.pallas_call(
         functools.partial(proj_kernel, held_slots, len(held_arrays), groups),
         out_shape=[shape(rows, qw + 128)] * groups + [shape(rows, width)],
-        in_specs=[SMEM] + [VMEM] * (3 + len(held_arrays)) + [ANY] * 2,
+        in_specs=[SMEM] + [VMEM] * (3 + len(held_arrays)),
         out_specs=[VMEM] * (groups + 1),
         scratch_shapes=[pltpu.VMEM((rows, columns), f32)],
         compiler_params=params(56),
         cost_estimate=about(8),
         name="proj",
-    )(me, token_rows, cos_here, sin_here, *held_arrays, second[1], second[groups - 1])
+    )(me, token_rows, cos_here, sin_here, *held_arrays)
     qkv_here = [pieces[0]] + [swap(pieces[j], "ulysses", j) for j in range(1, groups)]
 
     own_slices = pl.pallas_call(
@@ -484,16 +456,18 @@
         name="slices",
     )(normed, grad_rows)
     slices = lax.all_to_all(own_slices, "dp", 0, 0, tiled=True)
-    d_attn = pl.pallas_call(
-        functools.partial(d_attn_kernel, held_slots, groups, columns),
-        out_shape=shape(length, qw),
-        in_specs=[SMEM] + [VMEM] * (2 * groups + len(held_arrays)) + [ANY],
-        out_specs=VMEM,
-        scratch_shapes=[pltpu.VMEM((width, qw), bf16)],
+    sets = groups // 2
+    pieces = pl.pallas_call(
+        functools.partial(d_attn_kernel, held_slots, sets, columns),
+        out_shape=[shape(2 * rows, qw)] * sets,
+        in_specs=[SMEM] + [VMEM] * (2 + len(held_arrays)) + [ANY],
+        out_specs=[VMEM] * sets,
+        scratch_shapes=[pltpu.VMEM((width, sets * qw), bf16)],
         compiler_params=params(56),
         cost_estimate=about(6),
         name="d_attn",
-    )(me, *first, *second, *held_arrays, own_slices)
+    )(me, grad_rows, grad_pair, *held_arrays, qkv_here[1])
+    grads_here = [pieces[0]] + [swap(after(pieces[i], *qkv_here[1:]), "ulysses", 2 * i) for i in range(1, sets)]
 
     blocks = length // Q_BLOCK
     *mixed, o, stats = pl.pallas_call(
@@ -510,24 +484,25 @@
         compiler_params=params(56),
         cost_estimate=about(10),
         name="forward",
-    )(me, lengths[0], *qkv_here, d_attn)
+    )(me, lengths[0], *qkv_here, own_slices)
     mixed = [mixed[0]] + [swap(mixed[j], "ulysses", j) for j in range(1, groups)]
 
     back = pl.pallas_call(
         functools.partial(backward_kernel, groups),
         out_shape=[shape(rows, qw + 128)] * groups,
-        in_specs=[SMEM] * 2 + [VMEM] * (5 + groups),
+        in_specs=[SMEM] * 2 + [VMEM] * (4 + groups + sets),
         out_specs=[VMEM] * groups,
         scratch_shapes=[
             pltpu.VMEM((length, qw), bf16),
             pltpu.VMEM((length, 128), bf16),
+            pltpu.VMEM((length, qw), bf16),
             pltpu.VMEM((length, qw), f32),
             pltpu.VMEM((128, length), f32),
         ],
         compiler_params=params(56),
         cost_estimate=about(15),
         name="backward",
-    )(me, lengths[0], cos, sin, o, stats, *qkv_here, d_attn)
+    )(me, lengths[0], cos, sin, o, stats, *qkv_here, *grads_here)
     back = [back[0]] + [swap(back[j], "ulysses", j) for j in range(1, groups)]
 
     attn = pl.pallas_call(
@@ -550,22 +525,20 @@
         name="join_proj",
     )(me, *back, *attn_near)
     proj_near = neighbours(d_proj, "dp")
-    attn_arrays, attn_slots = complete(*relay(attn, *attn_near, d_proj), "dp")
-
-    d_w_out_terms = pl.pallas_call(
+    attn_arrays, attn_slots = complete(attn, *(after(a, d_proj) for a in attn_near), "dp")
+
+    d_w_out, *terms = pl.pallas_call(
         functools.partial(grads_kernel, attn_slots, 1, groups, factor),
-        out_shape=shape(groups, block, QW, dtype=f32),
+        out_shape=[shape(block, QW, dtype=f32)] * 2 + [shape(block, QW)] * (groups - 2),
         in_specs=[SMEM] + [VMEM] * (1 + len(attn_arrays)),
-        out_specs=VMEM,
+        out_specs=[VMEM] * groups,
         scratch_shapes=[pltpu.VMEM((kept, QW), f32)],
         compiler_params=params(56),
         cost_estimate=about(5),
         name="d_w_out",
     )(me, slices, *attn_arrays)
 
-    d_w_out = block_sum(d_w_out_terms, "ulysses")
-    relayed = relay(d_proj, *proj_near, d_w_out_terms)
-    proj_arrays, proj_slots = complete(*relayed, "dp")
+    out_terms = [swap(term, "ulysses", j) for j, term in enumerate(terms, 1)]
 
     d_tokens, partial_gain = pl.pallas_call(
         functools.partial(tokens_kernel, held_slots, len(held_arrays), groups, factor),
@@ -576,19 +549,23 @@
         compiler_params=params(56),
         cost_estimate=about(8),
         name="d_tokens",
-    )(me, token_rows, grad_rows, d_proj, *held_arrays, relayed[0])
-
-    d_w_qkv, gain_terms = pl.pallas_call(
+    )(me, token_rows, grad_rows, d_proj, *held_arrays, d_w_out)
+
+    proj_arrays, proj_slots = complete(d_proj, after(proj_near[0], partial_gain), after(proj_near[1], out_terms[0]), "dp")
+    d_w_qkv, *terms, gain_terms = pl.pallas_call(
         functools.partial(grads_and_pass_kernel, proj_slots, 0, groups, factor),
-        out_shape=[shape(groups, block, columns, dtype=f32), shape(groups, n, block, dtype=f32)],
-        in_specs=[SMEM] + [VMEM] * (2 + len(proj_arrays)),
-        out_specs=[VMEM] * 2,
+        out_shape=[shape(block, columns, dtype=f32)] * 2 + [shape(block, columns)] * (groups - 2) + [shape(groups, n, block, dtype=f32)],
+        in_specs=[SMEM] + [VMEM] * (1 + len(proj_arrays)) + [ANY] * (groups - 1) + [VMEM],
+        out_specs=[VMEM] * (groups + 1),
         scratch_shapes=[pltpu.VMEM((kept, columns), f32)],
         compiler_params=params(56),
         cost_estimate=about(6),
         name="d_w_qkv",
-    )(me, slices, *proj_arrays, partial_gain)
-    d_w_qkv = block_sum(d_w_qkv, "ulysses")
+    )(me, slices, *proj_arrays, *out_terms, partial_gain)
+    for j, term in enumerate(terms, 1):
+        d_w_qkv = d_w_qkv + swap(term, "ulysses", j).astype(f32)
+    for term in out_terms:
+        d_w_out = d_w_out + term.astype(f32)
     d_gain = gain_terms.reshape(groups * n, block)
     d_gain = lax.all_to_all(d_gain, ("ulysses", "dp"), 0, 0, tiled=True).sum(axis=0)
     return (d_tokens[None], d_w_qkv, d_w_out, d_gain)

time: 265 us -> 226 us (0.85)
  waiting for transfers between devices: 109 us -> 81.1 us
  Pallas kernels: 76.3 us -> 66.5 us
    all_to_all x1, waiting for transfers between devices: 27.8 us -> 13.4 us  [body(): lax.all_to_all(d_gain, ('ulysses', 'dp'), 0, 0, tiled=True).sum(axis=0)]
    ppermute x42 -> x44, waiting for transfers between devices: 80.9 us -> 67.8 us  [swap(): return lax.ppermute(a, axis, [(i, i ^ bit) for i in range(n)])]
    pallas_call x5 -> x8, Pallas kernels: 19.4 us -> 8.74 us  [the longest x1 6.33 us: body(): pl.pallas_call(functools.partial(d_attn_kernel, held_slots, sets, columns...]
    slice x0 -> x6, local copies, waits for them, and re-layouts: none -> 5.09 us  [the longest x3 3.06 us: complete(): first[:half]]
    unnamed x78 -> x88, local copies, waits for them, and re-layouts: 14.4 us -> 11.2 us
    ppermute x42 -> x44, starting transfers between devices: 45.7 us -> 45.8 us  [swap(): return lax.ppermute(a, axis, [(i, i ^ bit) for i in range(n)])]
  transfers between devices with their start and end apart: 44 -> 46, of which waited for: 15 -> 11; matrix products, arithmetic and copies ran while one was open for 3% -> 5% of each run, Pallas kernels for 22% -> 21%
where the time goes in v3:
time: 226 us
  waiting for transfers between devices  81.1 us (36%)
  Pallas kernels  66.5 us (29%)
  starting transfers between devices  52.6 us (23%)
  local copies, waits for them, and re-layouts  18.4 us (8%)
  other arithmetic  5.96 us (3%)
    ppermute x44, waiting for transfers between devices, swap(): return lax.ppermute(a, axis, [(i, i ^ bit) for i in range(n)])  67.8 us
    ppermute x44, starting transfers between devices, swap(): return lax.ppermute(a, axis, [(i, i ^ bit) for i in range(n)])  45.8 us
    all_to_all x1, waiting for transfers between devices, body(): lax.all_to_all(d_gain, ('ulysses', 'dp'), 0, 0, tiled=True).sum(axis=0)  13.4 us
    pallas_call x1, Pallas kernels, body(): pl.pallas_call(functools.partial(backward_kernel, groups), out_shape=[sha...  12.9 us
    unnamed x88, local copies, waits for them, and re-layouts  11.2 us
    pallas_call x1, Pallas kernels, body(): pl.pallas_call(functools.partial(forward_kernel, groups), out_shape=[shap...  8.81 us
    pallas_call x1, Pallas kernels, body(): pl.pallas_call(functools.partial(tokens_kernel, held_slots, len(held_arra...  8.21 us
    pallas_call x1, Pallas kernels, body(): pl.pallas_call(functools.partial(proj_kernel, held_slots, len(held_arrays...  8.08 us
  transfers between devices with their start and end apart: 46, of which 11 were waited for; matrix products, arithmetic and copies ran while one was open for 5% of the time, Pallas kernels for 21%

profile of v3, /device:TPU:0, one launch (start us, length us, event | category | flops | bytes accessed | tf_op | source)
XLA Modules:
  0.0 225.8 jit_solution(1505755132799663247)
XLA Ops:
  0.6 1.2 broadcast_in_dim.32.gain_ref
  2.5 2.4 %weights_here.1.refs_0_ = bf16[272,2048]{1,0:T(8,128)(2,1)} custom-call(s32[2]{0:T(128)} %pad_add_fusion.me_ref, bf16[256,1536]{1,0:T(8,128)(2,1)} %w_qkv_ref.1, bf16[256,1024]{1,0:T(8,128)(2,1)} %w_out_ref.1, bf16[1,256]{1,0:T(2,128)(2,1)} %broadcast_in_dim.32.gain_ref), custom_call_target="tpu_custom_call" | custom-call | flops 2000000000 | bytes 6000000 | tf_op jit(solution)/shard_map/weights_here/pallas_call | solution.py:376
  4.9 3.0 %collective-permute-start.2 = (bf16[272,2048]{1,0:T(8,128)(2,1)}, bf16[272,2048]{1,0:T(8,128)(2,1)S(1)}, u32[]{:S(2)}, u32[]{:S(2)}) collective-permute-start(bf16[272,2048]{1,0:T(8,128)(2,1)} %weights_here.1.refs_0_), channel_id=1, source_target_pairs={{0,4},{1,5},{2,6},{3,7},{4,0},{5,1},{6,2},{7,3},{8,12},{9,13},{10,... | collective-permute-start | bytes 3342344 | tf_op jit(solution)/shard_map/ppermute | solution.py:54
  7.9 1.5 collective-permute-start
  9.4 1.6 collective-permute-start.1
  11.0 21.7 %collective-permute-done.2.refs_2_ = bf16[272,2048]{1,0:T(8,128)(2,1)S(1)} collective-permute-done((bf16[272,2048]{1,0:T(8,128)(2,1)}, bf16[272,2048]{1,0:T(8,128)(2,1)S(1)}, u32[]{:S(2)}, u32[]{:S(2)}) %collective-permute-start.2) | collective-permute-done | bytes 1114144 | tf_op jit(solution)/shard_map/ppermute | solution.py:54
  32.7 1.8 collective-permute-start.4
  36.6 1.1 slice.24
  38.3 1.5 collective-permute-start.3
  39.9 12.4 %collective-permute-done.3.refs_3_ = bf16[128,2048]{1,0:T(8,128)(2,1)} collective-permute-done((bf16[128,2048]{1,0:T(8,128)(2,1)S(1)}, bf16[128,2048]{1,0:T(8,128)(2,1)}, u32[]{:S(2)}, u32[]{:S(2)}) %collective-permute-start.3) | collective-permute-done | bytes 524320 | tf_op jit(solution)/shard_map/ppermute | solution.py:54
  52.9 1.9 fusion
  56.6 8.1 %proj.1 = (bf16[256,384]{1,0:T(8,128)(2,1)}, bf16[256,384]{1,0:T(8,128)(2,1)}, bf16[256,384]{1,0:T(8,128)(2,1)}, bf16[256,384]{1,0:T(8,128)(2,1)}, bf16[256,2048]{1,0:T(8,128)(2,1)}) custom-call(s32[2]{0:T(128)} %pad_add_fusion.me_ref, bf16[256,2048]{1,0:T(8,128)(2,1)} %bitcast.12, f32[256,128]{1,0:T(8,128)} %get-tuple-element.63.cos_ref, ...), custom_call_target="tpu_custom_call" | custom-call | flops 8000000000 | bytes 24000000 | tf_op jit(solution)/shard_map/proj/pallas_call | solution.py:436
  64.7 1.6 collective-permute-start.10
  66.3 2.6 %collective-permute-start.11 = (bf16[256,384]{1,0:T(8,128)(2,1)}, bf16[256,384]{1,0:T(8,128)(2,1)S(1)}, u32[]{:S(2)}, u32[]{:S(2)}) collective-permute-start(bf16[256,384]{1,0:T(8,128)(2,1)} %get-tuple-element.34), channel_id=1, source_target_pairs={{0,16},{8,24},{16,0},{24,8},{1,17},{9,25},{17,1},{25,9},{2,18},{10... | collective-permute-start | bytes 589832 | tf_op jit(solution)/shard_map/ppermute | solution.py:54
  69.1 3.4 %slices.1.refs_4_ = bf16[8,512,256]{2,1,0:T(8,128)(2,1)} custom-call(bf16[256,2048]{1,0:T(8,128)(2,1)} %get-tuple-element.36.normed_ref, bf16[256,2048]{1,0:T(8,128)(2,1)} %bitcast.15), custom_call_target="tpu_custom_call" | custom-call | flops 3000000000 | bytes 9000000 | tf_op jit(solution)/shard_map/slices/pallas_call | solution.py:448
  72.6 3.8 %all-to-all-start = ((bf16[8,512,256]{2,1,0:T(8,128)(2,1)}), bf16[8,512,256]{2,1,0:T(8,128)(2,1)S(1)}, u32[]{:S(2)}, u32[]{:S(2)}) async-start(bf16[8,512,256]{2,1,0:T(8,128)(2,1)} %slices.1.refs_4_), calls=%async_computation | async-start | bytes 4194304 | tf_op jit(solution)/shard_map/all_to_all | solution.py:458
  77.0 6.3 %d_attn.1 = (bf16[512,256]{1,0:T(8,128)(2,1)}, bf16[512,256]{1,0:T(8,128)(2,1)}) custom-call(s32[2]{0:T(128)} %pad_add_fusion.me_ref, bf16[256,2048]{1,0:T(8,128)(2,1)} %bitcast.16, bf16[256,2048]{1,0:T(8,128)(2,1)} %copy-done.6, bf16[272,2048]{1,0:T(8,128)(2,1)} %weights_here.1.refs_0_, bf16[272,2048]{1,0:T(8,128)(2,1)} %after.6.refs_1_, ...), custom_call_target="tpu_custom_call" | custom-call | flops 6000000000 | bytes 18000000 | tf_op jit(solution)/shard_map/d_attn/pallas_call | solution.py:460
  84.4 4.5 %collective-permute-start.13 = (bf16[512,256]{1,0:T(8,128)(2,1)}, bf16[512,256]{1,0:T(8,128)(2,1)S(1)}, u32[]{:S(2)}, u32[]{:S(2)}) collective-permute-start(bf16[512,256]{1,0:T(8,128)(2,1)} %after.7), channel_id=1, source_target_pairs={{0,16},{8,24},{16,0},{24,8},{1,17},{9,25},{17,1},{25,9},{2,18},{10... | collective-permute-start | bytes 786440 | tf_op jit(solution)/shard_map/ppermute | solution.py:54
  88.9 8.8 %forward.1 = (bf16[256,256]{1,0:T(8,128)(2,1)}, bf16[256,256]{1,0:T(8,128)(2,1)}, bf16[256,256]{1,0:T(8,128)(2,1)}, bf16[256,256]{1,0:T(8,128)(2,1)}, f32[1024,256]{1,0:T(8,128)}, /*index=5*/f32[8,512,2]{2,1,0:T(8,128)}) custom-call(s32[2]{0:T(128)} %pad_add_fusion.me_ref, s32[10]{0:T(128)} %bitcast.18, bf16[256,384]{1,0:T(8,128)(2,1)} %get-tuple-element.32.refs_0_, ...), custom_call_target="tpu_custom_call" | custom-call | flops 10000000000 | bytes 30000000 | tf_op jit(solution)/shard_map/forward/pallas_call | solution.py:473
  97.7 1.9 collective-permute-start.18
  99.6 2.5 %collective-permute-start.19 = (bf16[256,256]{1,0:T(8,128)(2,1)}, bf16[256,256]{1,0:T(8,128)(2,1)S(1)}, u32[]{:S(2)}, u32[]{:S(2)}) collective-permute-start(bf16[256,256]{1,0:T(8,128)(2,1)} %get-tuple-element.48), channel_id=1, source_target_pairs={{0,24},{8,16},{16,8},{24,0},{1,25},{9,17},{17,9},{25,1},{2,26},{10... | collective-permute-start | bytes 393224 | tf_op jit(solution)/shard_map/ppermute | solution.py:54
  102.8 12.9 %backward.1 = (bf16[256,384]{1,0:T(8,128)(2,1)}, bf16[256,384]{1,0:T(8,128)(2,1)}, bf16[256,384]{1,0:T(8,128)(2,1)}, bf16[256,384]{1,0:T(8,128)(2,1)}) custom-call(s32[2]{0:T(128)} %pad_add_fusion.me_ref, s32[10]{0:T(128)} %bitcast.19, f32[1024,128]{1,0:T(8,128)} %copy-done.10, f32[1024,128]{1,0:T(8,128)} %copy-done.9, f32[1024,256]{1,0:T(8,128)} %get-tuple-element.37.o_ref, ...), custom_call_target="tpu_custom_call" | custom-call | flops 15000000512 | bytes 45000000 | tf_op jit(solution)/shard_map/backward/pallas_call | solution.py:490
  117.2 2.0 join_attn.1.refs_0_
  120.1 1.5 collective-permute-start.21
  121.6 2.3 collective-permute-start.15
  123.9 2.1 collective-permute-start.16
  126.0 2.6 %collective-permute-done.14.refs_1_ = bf16[256,384]{1,0:T(8,128)(2,1)S(1)} collective-permute-done((bf16[256,384]{1,0:T(8,128)(2,1)S(1)}, bf16[256,384]{1,0:T(8,128)(2,1)S(1)}, u32[]{:S(2)}, u32[]{:S(2)}) %collective-permute-start.14) | collective-permute-done | bytes 196640 | tf_op jit(solution)/shard_map/ppermute | solution.py:54
  128.6 9.9 %collective-permute-done.15.refs_2_ = bf16[256,384]{1,0:T(8,128)(2,1)S(1)} collective-permute-done((bf16[256,384]{1,0:T(8,128)(2,1)S(1)}, bf16[256,384]{1,0:T(8,128)(2,1)S(1)}, u32[]{:S(2)}, u32[]{:S(2)}) %collective-permute-start.15) | collective-permute-done | bytes 196640 | tf_op jit(solution)/shard_map/ppermute | solution.py:54
  140.3 2.4 %join_proj.1.refs_1_.d_proj_ref.refs_0_ = bf16[256,1536]{1,0:T(8,128)(2,1)} custom-call(s32[2]{0:T(128)} %pad_add_fusion.me_ref, bf16[256,384]{1,0:T(8,128)(2,1)} %get-tuple-element.41.refs_5_.refs_0_, bf16[256,384]{1,0:T(8,128)(2,1)} %copy-done.37, bf16[256,384]{1,0:T(8,128)(2,1)} %copy-done.38, bf16[256,384]{1,0:T(8,128)(2,1)} %copy-done.39, ...), custom_call_target="tpu_custom_call" | custom-call | flops 3000000000 | bytes 9000000 | tf_op jit(solution)/shard_map/join_proj/pallas_call | solution.py:518
  145.9 6.6 %collective-permute-done.23.refs_4_ = bf16[128,1024]{1,0:T(8,128)(2,1)S(1)} collective-permute-done((bf16[128,1024]{1,0:T(8,128)(2,1)S(1)}, bf16[128,1024]{1,0:T(8,128)(2,1)S(1)}, u32[]{:S(2)}, u32[]{:S(2)}) %collective-permute-start.23) | collective-permute-done | bytes 262176 | tf_op jit(solution)/shard_map/ppermute | solution.py:54
  152.5 1.4 collective-permute-done.22.refs_3_
  154.5 1.7 collective-permute-start.29
  157.8 5.4 %d_w_out.1 = (f32[64,1024]{1,0:T(8,128)}, f32[64,1024]{1,0:T(8,128)}, bf16[64,1024]{1,0:T(8,128)(2,1)}, bf16[64,1024]{1,0:T(8,128)(2,1)}) custom-call(s32[2]{0:T(128)} %pad_add_fusion.me_ref, bf16[8,512,256]{2,1,0:T(8,128)(2,1)} %copy-done.1, bf16[256,1024]{1,0:T(8,128)(2,1)} %join_attn.1.refs_0_, bf16[256,1024]{1,0:T(8,128)(2,1)} %after.8.refs_1_, ...), custom_call_target="tpu_custom_call" | custom-call | flops 5000000000 | bytes 15000000 | tf_op jit(solution)/shard_map/d_w_out/pallas_call | solution.py:530
  163.2 2.6 %collective-permute-start.31 = (f32[64,1024]{1,0:T(8,128)}, f32[64,1024]{1,0:T(8,128)S(1)}, u32[]{:S(2)}, u32[]{:S(2)}) collective-permute-start(f32[64,1024]{1,0:T(8,128)} %get-tuple-element.52), channel_id=1, source_target_pairs={{0,8},{8,0},{16,24},{24,16},{1,9},{9,1},{17,25},{25,17},{2,10},{10... | collective-permute-start | bytes 786440 | tf_op jit(solution)/shard_map/ppermute | solution.py:54
  165.8 1.1 collective-permute-start.39
  166.9 1.4 collective-permute-start.40
  168.3 8.2 %d_tokens.1 = (bf16[256,2048]{1,0:T(8,128)(2,1)}, f32[4,8,64]{2,1,0:T(8,128)}) custom-call(s32[2]{0:T(128)} %pad_add_fusion.me_ref, bf16[256,2048]{1,0:T(8,128)(2,1)} %bitcast.13, bf16[256,2048]{1,0:T(8,128)(2,1)} %bitcast.17, bf16[256,1536]{1,0:T(8,128)(2,1)} %join_proj.1.refs_1_.d_proj_ref.refs_0_, bf16[272,2048]{1,0:T(8,128)(2,1)} %weights_here.1.refs_0_, ...), custom_call_target="tpu_custom_call" | custom-call | flops 8000000000 | bytes 24000000 | tf_op jit(solution)/shard_map/d_tokens/pallas_call | solution.py:543
  178.6 1.6 collective-permute-start.32
  181.8 8.4 %collective-permute-done.32.refs_3_ = bf16[128,1536]{1,0:T(8,128)(2,1)S(1)} collective-permute-done((bf16[128,1536]{1,0:T(8,128)(2,1)S(1)}, bf16[128,1536]{1,0:T(8,128)(2,1)S(1)}, u32[]{:S(2)}, u32[]{:S(2)}) %collective-permute-start.32) | collective-permute-done | bytes 393248 | tf_op jit(solution)/shard_map/ppermute | solution.py:54
  190.1 2.7 %collective-permute-done.33.refs_4_ = bf16[128,1536]{1,0:T(8,128)(2,1)S(1)} collective-permute-done((bf16[128,1536]{1,0:T(8,128)(2,1)S(1)}, bf16[128,1536]{1,0:T(8,128)(2,1)S(1)}, u32[]{:S(2)}, u32[]{:S(2)}) %collective-permute-start.33) | collective-permute-done | bytes 393248 | tf_op jit(solution)/shard_map/ppermute | solution.py:54
  192.9 1.7 collective-permute-done.38.refs_9_
  195.4 6.4 %d_w_qkv.1 = (f32[64,1536]{1,0:T(8,128)}, f32[64,1536]{1,0:T(8,128)}, bf16[64,1536]{1,0:T(8,128)(2,1)}, bf16[64,1536]{1,0:T(8,128)(2,1)}, f32[4,8,64]{2,1,0:T(8,128)}) custom-call(s32[2]{0:T(128)} %pad_add_fusion.me_ref, bf16[8,512,256]{2,1,0:T(8,128)(2,1)} %copy-done.1, bf16[256,1536]{1,0:T(8,128)(2,1)} %join_proj.1.refs_1_.d_proj_ref.refs_0_, ...), custom_call_target="tpu_custom_call" | custom-call | flops 6000000000 | bytes 18000000 | tf_op jit(solution)/shard_map/d_w_qkv/pallas_call | solution.py:555
  201.8 1.1 collective-permute-start.41
  202.9 2.0 collective-permute-start.42
  204.8 1.4 collective-permute-start.43
  206.2 3.0 %all-to-all-start.1 = ((f32[32,1,64]{2,1,0:T(1,128)}), f32[32,1,64]{2,1,0:T(1,128)S(1)}, u32[]{:S(2)}, u32[]{:S(2)}) async-start(f32[32,1,64]{2,1,0:T(1,128)} %bitcast.11), calls=%async_computation.1 | async-start | bytes 32768 | tf_op jit(solution)/shard_map/all_to_all | solution.py:570
  209.3 1.7 convert_add_fusion.1
  211.0 13.4 %all-to-all-done.1 = f32[32,1,64]{2,1,0:T(1,128)S(1)} async-done(((f32[32,1,64]{2,1,0:T(1,128)}), f32[32,1,64]{2,1,0:T(1,128)S(1)}, u32[]{:S(2)}, u32[]{:S(2)}) %all-to-all-start.1) | async-done | bytes 8224 | tf_op jit(solution)/shard_map/all_to_all | solution.py:570
  (170 shorter events, 23.4 us)
Async XLA Ops:
  4.9 29.6 %copy-start.43 = (s32[1,10]{1,0:T(1,128)S(1)}, s32[1,10]{1,0:T(1,128)}, u32[]{:S(2)}) copy-start(s32[1,10]{1,0:T(1,128)} %param.8) | copy-start | bytes 124
  4.9 27.7 %collective-permute-start.2 = (bf16[272,2048]{1,0:T(8,128)(2,1)}, bf16[272,2048]{1,0:T(8,128)(2,1)S(1)}, u32[]{:S(2)}, u32[]{:S(2)}) collective-permute-start(bf16[272,2048]{1,0:T(8,128)(2,1)} %weights_here.1.refs_0_), channel_id=1, source_target_pairs={{0,4},{1,5},{2,6},{3,7},{4,0},{5,1},{6,2},{7,3},{8,12},{9,13},{10,... | collective-permute-start | bytes 3342344 | tf_op jit(solution)/shard_map/ppermute | solution.py:54
  7.9 26.8 %collective-permute-start = (bf16[272,2048]{1,0:T(8,128)(2,1)}, bf16[272,2048]{1,0:T(8,128)(2,1)S(1)}, u32[]{:S(2)}, u32[]{:S(2)}) collective-permute-start(bf16[272,2048]{1,0:T(8,128)(2,1)} %weights_here.1.refs_0_), channel_id=1, source_target_pairs={{0,2},{1,3},{2,0},{3,1},{4,6},{5,7},{6,4},{7,5},{8,10},{9,11},{10,... | collective-permute-start | bytes 3342344 | tf_op jit(solution)/shard_map/ppermute | solution.py:54
  9.4 25.3 %collective-permute-start.1 = (bf16[256,2048]{1,0:T(8,128)(2,1)}, bf16[256,2048]{1,0:T(8,128)(2,1)S(1)}, u32[]{:S(2)}, u32[]{:S(2)}) collective-permute-start(bf16[256,2048]{1,0:T(8,128)(2,1)} %bitcast.14), channel_id=1, source_target_pairs={{0,8},{8,0},{16,24},{24,16},{1,9},{9,1},{17,25},{25,17},{2,10},{10... | collective-permute-start | bytes 3145736 | tf_op jit(solution)/shard_map/ppermute | solution.py:54
  32.7 19.6 %collective-permute-start.4 = (bf16[144,2048]{1,0:T(8,128)(2,1)S(1)}, bf16[144,2048]{1,0:T(8,128)(2,1)}, u32[]{:S(2)}, u32[]{:S(2)}) collective-permute-start(bf16[144,2048]{1,0:T(8,128)(2,1)S(1)} %slice.25), channel_id=1, source_target_pairs={{0,2},{1,3},{2,0},{3,1},{4,6},{5,7},{6,4},{7,5},{8,10},{9,11},{10,... | collective-permute-start | bytes 1769480 | tf_op jit(solution)/shard_map/ppermute | solution.py:54
  34.5 21.2 %collective-permute-start.5 = (bf16[272,2048]{1,0:T(8,128)(2,1)}, bf16[272,2048]{1,0:T(8,128)(2,1)}, u32[]{:S(2)}, u32[]{:S(2)}) collective-permute-start(bf16[272,2048]{1,0:T(8,128)(2,1)} %weights_here.1.refs_0_), channel_id=1, source_target_pairs={{0,1},{1,0},{2,3},{3,2},{4,5},{5,4},{6,7},{7,6},{8,9},{9,8},{10,11... | collective-permute-start | bytes 3342344 | tf_op jit(solution)/shard_map/ppermute | solution.py:54
  37.7 17.9 %collective-permute-start.6 = (bf16[272,2048]{1,0:T(8,128)(2,1)}, bf16[272,2048]{1,0:T(8,128)(2,1)}, u32[]{:S(2)}, u32[]{:S(2)}) collective-permute-start(bf16[272,2048]{1,0:T(8,128)(2,1)} %after.6.refs_1_), channel_id=1, source_target_pairs={{0,1},{1,0},{2,3},{3,2},{4,5},{5,4},{6,7},{7,6},{8,9},{9,8},{10,11... | collective-permute-start | bytes 3342344 | tf_op jit(solution)/shard_map/ppermute | solution.py:54
  38.3 14.0 %collective-permute-start.3 = (bf16[128,2048]{1,0:T(8,128)(2,1)S(1)}, bf16[128,2048]{1,0:T(8,128)(2,1)}, u32[]{:S(2)}, u32[]{:S(2)}) collective-permute-start(bf16[128,2048]{1,0:T(8,128)(2,1)S(1)} %slice.24), channel_id=1, source_target_pairs={{0,4},{1,5},{2,6},{3,7},{4,0},{5,1},{6,2},{7,3},{8,12},{9,13},{10,... | collective-permute-start | bytes 1572872 | tf_op jit(solution)/shard_map/ppermute | solution.py:54
  39.8 15.9 %collective-permute-start.7 = (bf16[272,2048]{1,0:T(8,128)(2,1)}, bf16[272,2048]{1,0:T(8,128)(2,1)}, u32[]{:S(2)}, u32[]{:S(2)}) collective-permute-start(bf16[272,2048]{1,0:T(8,128)(2,1)} %copy-done.12), channel_id=1, source_target_pairs={{0,1},{1,0},{2,3},{3,2},{4,5},{5,4},{6,7},{7,6},{8,9},{9,8},{10,11... | collective-permute-start | bytes 3342344 | tf_op jit(solution)/shard_map/ppermute | solution.py:54
  52.3 3.4 %collective-permute-start.8 = (bf16[128,2048]{1,0:T(8,128)(2,1)}, bf16[128,2048]{1,0:T(8,128)(2,1)}, u32[]{:S(2)}, u32[]{:S(2)}) collective-permute-start(bf16[128,2048]{1,0:T(8,128)(2,1)} %collective-permute-done.3.refs_3_), channel_id=1, source_target_pairs={{0,1},{1,0},{2,3},{3,2},{4,5},{5,4},{6,7},{7,6},{8,9},{9,8},{10,11... | collective-permute-start | bytes 1572872 | tf_op jit(solution)/shard_map/ppermute | solution.py:54
  52.3 3.4 %collective-permute-start.9 = (bf16[144,2048]{1,0:T(8,128)(2,1)}, bf16[144,2048]{1,0:T(8,128)(2,1)S(1)}, u32[]{:S(2)}, u32[]{:S(2)}) collective-permute-start(bf16[144,2048]{1,0:T(8,128)(2,1)} %collective-permute-done.4.refs_4_), channel_id=1, source_target_pairs={{0,1},{1,0},{2,3},{3,2},{4,5},{5,4},{6,7},{7,6},{8,9},{9,8},{10,11... | collective-permute-start | bytes 1769480 | tf_op jit(solution)/shard_map/ppermute | solution.py:54
  64.7 11.7 %collective-permute-start.10 = (bf16[256,384]{1,0:T(8,128)(2,1)}, bf16[256,384]{1,0:T(8,128)(2,1)S(1)}, u32[]{:S(2)}, u32[]{:S(2)}) collective-permute-start(bf16[256,384]{1,0:T(8,128)(2,1)} %get-tuple-element.33), channel_id=1, source_target_pairs={{0,8},{8,0},{16,24},{24,16},{1,9},{9,1},{17,25},{25,17},{2,10},{10... | collective-permute-start | bytes 589832 | tf_op jit(solution)/shard_map/ppermute | solution.py:54
  66.3 17.3 %collective-permute-start.11 = (bf16[256,384]{1,0:T(8,128)(2,1)}, bf16[256,384]{1,0:T(8,128)(2,1)S(1)}, u32[]{:S(2)}, u32[]{:S(2)}) collective-permute-start(bf16[256,384]{1,0:T(8,128)(2,1)} %get-tuple-element.34), channel_id=1, source_target_pairs={{0,16},{8,24},{16,0},{24,8},{1,17},{9,25},{17,1},{25,9},{2,18},{10... | collective-permute-start | bytes 589832 | tf_op jit(solution)/shard_map/ppermute | solution.py:54
  68.9 14.8 %collective-permute-start.12 = (bf16[256,384]{1,0:T(8,128)(2,1)}, bf16[256,384]{1,0:T(8,128)(2,1)S(1)}, u32[]{:S(2)}, u32[]{:S(2)}) collective-permute-start(bf16[256,384]{1,0:T(8,128)(2,1)} %get-tuple-element.35), channel_id=1, source_target_pairs={{0,24},{8,16},{16,8},{24,0},{1,25},{9,17},{17,9},{25,1},{2,26},{10... | collective-permute-start | bytes 589832 | tf_op jit(solution)/shard_map/ppermute | solution.py:54
  72.6 43.2 %all-to-all-start = ((bf16[8,512,256]{2,1,0:T(8,128)(2,1)}), bf16[8,512,256]{2,1,0:T(8,128)(2,1)S(1)}, u32[]{:S(2)}, u32[]{:S(2)}) async-start(bf16[8,512,256]{2,1,0:T(8,128)(2,1)} %slices.1.refs_4_), calls=%async_computation | async-start | bytes 4194304 | tf_op jit(solution)/shard_map/all_to_all | solution.py:458
  84.4 17.7 %collective-permute-start.13 = (bf16[512,256]{1,0:T(8,128)(2,1)}, bf16[512,256]{1,0:T(8,128)(2,1)S(1)}, u32[]{:S(2)}, u32[]{:S(2)}) collective-permute-start(bf16[512,256]{1,0:T(8,128)(2,1)} %after.7), channel_id=1, source_target_pairs={{0,16},{8,24},{16,0},{24,8},{1,17},{9,25},{17,1},{25,9},{2,18},{10... | collective-permute-start | bytes 786440 | tf_op jit(solution)/shard_map/ppermute | solution.py:54
  97.7 18.0 %collective-permute-start.17 = (bf16[256,256]{1,0:T(8,128)(2,1)}, bf16[256,256]{1,0:T(8,128)(2,1)S(1)}, u32[]{:S(2)}, u32[]{:S(2)}) collective-permute-start(bf16[256,256]{1,0:T(8,128)(2,1)} %get-tuple-element.46), channel_id=1, source_target_pairs={{0,8},{8,0},{16,24},{24,16},{1,9},{9,1},{17,25},{25,17},{2,10},{10... | collective-permute-start | bytes 393224 | tf_op jit(solution)/shard_map/ppermute | solution.py:54
  97.7 18.0 %collective-permute-start.18 = (bf16[256,256]{1,0:T(8,128)(2,1)}, bf16[256,256]{1,0:T(8,128)(2,1)S(1)}, u32[]{:S(2)}, u32[]{:S(2)}) collective-permute-start(bf16[256,256]{1,0:T(8,128)(2,1)} %get-tuple-element.47), channel_id=1, source_target_pairs={{0,16},{8,24},{16,0},{24,8},{1,17},{9,25},{17,1},{25,9},{2,18},{10... | collective-permute-start | bytes 393224 | tf_op jit(solution)/shard_map/ppermute | solution.py:54
  99.6 16.1 %collective-permute-start.19 = (bf16[256,256]{1,0:T(8,128)(2,1)}, bf16[256,256]{1,0:T(8,128)(2,1)S(1)}, u32[]{:S(2)}, u32[]{:S(2)}) collective-permute-start(bf16[256,256]{1,0:T(8,128)(2,1)} %get-tuple-element.48), channel_id=1, source_target_pairs={{0,24},{8,16},{16,8},{24,0},{1,25},{9,17},{17,9},{25,1},{2,26},{10... | collective-permute-start | bytes 393224 | tf_op jit(solution)/shard_map/ppermute | solution.py:54
  119.2 19.3 %collective-permute-start.20 = (bf16[256,1024]{1,0:T(8,128)(2,1)}, bf16[256,1024]{1,0:T(8,128)(2,1)S(1)}, u32[]{:S(2)}, u32[]{:S(2)}) collective-permute-start(bf16[256,1024]{1,0:T(8,128)(2,1)} %join_attn.1.refs_0_), channel_id=1, source_target_pairs={{0,2},{1,3},{2,0},{3,1},{4,6},{5,7},{6,4},{7,5},{8,10},{9,11},{10,... | collective-permute-start | bytes 1572872 | tf_op jit(solution)/shard_map/ppermute | solution.py:54
  120.1 18.5 %collective-permute-start.21 = (bf16[256,1024]{1,0:T(8,128)(2,1)}, bf16[256,1024]{1,0:T(8,128)(2,1)S(1)}, u32[]{:S(2)}, u32[]{:S(2)}) collective-permute-start(bf16[256,1024]{1,0:T(8,128)(2,1)} %join_attn.1.refs_0_), channel_id=1, source_target_pairs={{0,4},{1,5},{2,6},{3,7},{4,0},{5,1},{6,2},{7,3},{8,12},{9,13},{10,... | collective-permute-start | bytes 1572872 | tf_op jit(solution)/shard_map/ppermute | solution.py:54
  121.6 7.0 %collective-permute-start.14 = (bf16[256,384]{1,0:T(8,128)(2,1)S(1)}, bf16[256,384]{1,0:T(8,128)(2,1)S(1)}, u32[]{:S(2)}, u32[]{:S(2)}) collective-permute-start(bf16[256,384]{1,0:T(8,128)(2,1)S(1)} %copy-done.36), channel_id=1, source_target_pairs={{0,8},{8,0},{16,24},{24,16},{1,9},{9,1},{17,25},{25,17},{2,10},{10... | collective-permute-start | bytes 589832 | tf_op jit(solution)/shard_map/ppermute | solution.py:54
  121.6 16.9 %collective-permute-start.15 = (bf16[256,384]{1,0:T(8,128)(2,1)S(1)}, bf16[256,384]{1,0:T(8,128)(2,1)S(1)}, u32[]{:S(2)}, u32[]{:S(2)}) collective-permute-start(bf16[256,384]{1,0:T(8,128)(2,1)S(1)} %copy-done.35), channel_id=1, source_target_pairs={{0,16},{8,24},{16,0},{24,8},{1,17},{9,25},{17,1},{25,9},{2,18},{10... | collective-permute-start | bytes 589832 | tf_op jit(solution)/shard_map/ppermute | solution.py:54
  123.9 14.7 %collective-permute-start.16 = (bf16[256,384]{1,0:T(8,128)(2,1)S(1)}, bf16[256,384]{1,0:T(8,128)(2,1)S(1)}, u32[]{:S(2)}, u32[]{:S(2)}) collective-permute-start(bf16[256,384]{1,0:T(8,128)(2,1)S(1)} %copy-done.34), channel_id=1, source_target_pairs={{0,24},{8,16},{16,8},{24,0},{1,25},{9,17},{17,9},{25,1},{2,26},{10... | collective-permute-start | bytes 589832 | tf_op jit(solution)/shard_map/ppermute | solution.py:54
  128.6 25.3 %collective-permute-start.24 = (bf16[256,1024]{1,0:T(8,128)(2,1)}, bf16[256,1024]{1,0:T(8,128)(2,1)S(1)}, u32[]{:S(2)}, u32[]{:S(2)}) collective-permute-start(bf16[256,1024]{1,0:T(8,128)(2,1)} %join_attn.1.refs_0_), channel_id=1, source_target_pairs={{0,1},{1,0},{2,3},{3,2},{4,5},{5,4},{6,7},{7,6},{8,9},{9,8},{10,11... | collective-permute-start | bytes 1572872 | tf_op jit(solution)/shard_map/ppermute | solution.py:54
  143.7 10.8 %collective-permute-start.26 = (bf16[256,1024]{1,0:T(8,128)(2,1)}, bf16[256,1024]{1,0:T(8,128)(2,1)S(1)}, u32[]{:S(2)}, u32[]{:S(2)}) collective-permute-start(bf16[256,1024]{1,0:T(8,128)(2,1)} %after.9.refs_2_), channel_id=1, source_target_pairs={{0,1},{1,0},{2,3},{3,2},{4,5},{5,4},{6,7},{7,6},{8,9},{9,8},{10,11... | collective-permute-start | bytes 1572872 | tf_op jit(solution)/shard_map/ppermute | solution.py:54
  143.8 8.7 %collective-permute-start.23 = (bf16[128,1024]{1,0:T(8,128)(2,1)S(1)}, bf16[128,1024]{1,0:T(8,128)(2,1)S(1)}, u32[]{:S(2)}, u32[]{:S(2)}) collective-permute-start(bf16[128,1024]{1,0:T(8,128)(2,1)S(1)} %slice.27), channel_id=1, source_target_pairs={{0,2},{1,3},{2,0},{3,1},{4,6},{5,7},{6,4},{7,5},{8,10},{9,11},{10,... | collective-permute-start | bytes 786440 | tf_op jit(solution)/shard_map/ppermute | solution.py:54
  145.1 11.1 %collective-permute-start.25 = (bf16[256,1024]{1,0:T(8,128)(2,1)}, bf16[256,1024]{1,0:T(8,128)(2,1)S(1)}, u32[]{:S(2)}, u32[]{:S(2)}) collective-permute-start(bf16[256,1024]{1,0:T(8,128)(2,1)} %after.8.refs_1_), channel_id=1, source_target_pairs={{0,1},{1,0},{2,3},{3,2},{4,5},{5,4},{6,7},{7,6},{8,9},{9,8},{10,11... | collective-permute-start | bytes 1572872 | tf_op jit(solution)/shard_map/ppermute | solution.py:54
  145.4 8.6 %collective-permute-start.22 = (bf16[128,1024]{1,0:T(8,128)(2,1)S(1)}, bf16[128,1024]{1,0:T(8,128)(2,1)S(1)}, u32[]{:S(2)}, u32[]{:S(2)}) collective-permute-start(bf16[128,1024]{1,0:T(8,128)(2,1)S(1)} %slice.26), channel_id=1, source_target_pairs={{0,4},{1,5},{2,6},{3,7},{4,0},{5,1},{6,2},{7,3},{8,12},{9,13},{10,... | collective-permute-start | bytes 786440 | tf_op jit(solution)/shard_map/ppermute | solution.py:54
  152.5 3.8 %collective-permute-start.28 = (bf16[128,1024]{1,0:T(8,128)(2,1)S(1)}, bf16[128,1024]{1,0:T(8,128)(2,1)S(1)}, u32[]{:S(2)}, u32[]{:S(2)}) collective-permute-start(bf16[128,1024]{1,0:T(8,128)(2,1)S(1)} %collective-permute-done.23.refs_4_), channel_id=1, source_target_pairs={{0,1},{1,0},{2,3},{3,2},{4,5},{5,4},{6,7},{7,6},{8,9},{9,8},{10,11... | collective-permute-start | bytes 786440 | tf_op jit(solution)/shard_map/ppermute | solution.py:54
  153.9 2.3 %collective-permute-start.27 = (bf16[128,1024]{1,0:T(8,128)(2,1)S(1)}, bf16[128,1024]{1,0:T(8,128)(2,1)S(1)}, u32[]{:S(2)}, u32[]{:S(2)}) collective-permute-start(bf16[128,1024]{1,0:T(8,128)(2,1)S(1)} %collective-permute-done.22.refs_3_), channel_id=1, source_target_pairs={{0,1},{1,0},{2,3},{3,2},{4,5},{5,4},{6,7},{7,6},{8,9},{9,8},{10,11... | collective-permute-start | bytes 786440 | tf_op jit(solution)/shard_map/ppermute | solution.py:54
  153.9 24.5 %collective-permute-start.30 = (bf16[256,1536]{1,0:T(8,128)(2,1)}, bf16[256,1536]{1,0:T(8,128)(2,1)S(1)}, u32[]{:S(2)}, u32[]{:S(2)}) collective-permute-start(bf16[256,1536]{1,0:T(8,128)(2,1)} %join_proj.1.refs_1_.d_proj_ref.refs_0_), channel_id=1, source_target_pairs={{0,4},{1,5},{2,6},{3,7},{4,0},{5,1},{6,2},{7,3},{8,12},{9,13},{10,... | collective-permute-start | bytes 2359304 | tf_op jit(solution)/shard_map/ppermute | solution.py:54
  154.5 22.0 %collective-permute-start.29 = (bf16[256,1536]{1,0:T(8,128)(2,1)}, bf16[256,1536]{1,0:T(8,128)(2,1)S(1)}, u32[]{:S(2)}, u32[]{:S(2)}) collective-permute-start(bf16[256,1536]{1,0:T(8,128)(2,1)} %join_proj.1.refs_1_.d_proj_ref.refs_0_), channel_id=1, source_target_pairs={{0,2},{1,3},{2,0},{3,1},{4,6},{5,7},{6,4},{7,5},{8,10},{9,11},{10,... | collective-permute-start | bytes 2359304 | tf_op jit(solution)/shard_map/ppermute | solution.py:54
  163.2 15.3 %collective-permute-start.31 = (f32[64,1024]{1,0:T(8,128)}, f32[64,1024]{1,0:T(8,128)S(1)}, u32[]{:S(2)}, u32[]{:S(2)}) collective-permute-start(f32[64,1024]{1,0:T(8,128)} %get-tuple-element.52), channel_id=1, source_target_pairs={{0,8},{8,0},{16,24},{24,16},{1,9},{9,1},{17,25},{25,17},{2,10},{10... | collective-permute-start | bytes 786440 | tf_op jit(solution)/shard_map/ppermute | solution.py:54
  165.8 15.4 %collective-permute-start.39 = (bf16[64,1024]{1,0:T(8,128)(2,1)}, bf16[64,1024]{1,0:T(8,128)(2,1)S(1)}, u32[]{:S(2)}, u32[]{:S(2)}) collective-permute-start(bf16[64,1024]{1,0:T(8,128)(2,1)} %get-tuple-element.53), channel_id=1, source_target_pairs={{0,16},{8,24},{16,0},{24,8},{1,17},{9,25},{17,1},{25,9},{2,18},{10... | collective-permute-start | bytes 393224 | tf_op jit(solution)/shard_map/ppermute | solution.py:54
  166.9 14.5 %collective-permute-start.40 = (bf16[64,1024]{1,0:T(8,128)(2,1)}, bf16[64,1024]{1,0:T(8,128)(2,1)S(1)}, u32[]{:S(2)}, u32[]{:S(2)}) collective-permute-start(bf16[64,1024]{1,0:T(8,128)(2,1)} %get-tuple-element.54), channel_id=1, source_target_pairs={{0,24},{8,16},{16,8},{24,0},{1,25},{9,17},{17,9},{25,1},{2,26},{10... | collective-permute-start | bytes 393224 | tf_op jit(solution)/shard_map/ppermute | solution.py:54
  176.6 16.3 %collective-permute-start.34 = (bf16[256,1536]{1,0:T(8,128)(2,1)}, bf16[256,1536]{1,0:T(8,128)(2,1)S(1)}, u32[]{:S(2)}, u32[]{:S(2)}) collective-permute-start(bf16[256,1536]{1,0:T(8,128)(2,1)} %join_proj.1.refs_1_.d_proj_ref.refs_0_), channel_id=1, source_target_pairs={{0,1},{1,0},{2,3},{3,2},{4,5},{5,4},{6,7},{7,6},{8,9},{9,8},{10,11... | collective-permute-start | bytes 2359304 | tf_op jit(solution)/shard_map/ppermute | solution.py:54
  178.5 14.4 %collective-permute-start.35 = (bf16[256,1536]{1,0:T(8,128)(2,1)}, bf16[256,1536]{1,0:T(8,128)(2,1)}, u32[]{:S(2)}, u32[]{:S(2)}) collective-permute-start(bf16[256,1536]{1,0:T(8,128)(2,1)} %after.10.refs_1_), channel_id=1, source_target_pairs={{0,1},{1,0},{2,3},{3,2},{4,5},{5,4},{6,7},{7,6},{8,9},{9,8},{10,11... | collective-permute-start | bytes 2359304 | tf_op jit(solution)/shard_map/ppermute | solution.py:54
  178.6 11.5 %collective-permute-start.32 = (bf16[128,1536]{1,0:T(8,128)(2,1)S(1)}, bf16[128,1536]{1,0:T(8,128)(2,1)S(1)}, u32[]{:S(2)}, u32[]{:S(2)}) collective-permute-start(bf16[128,1536]{1,0:T(8,128)(2,1)S(1)} %slice.28), channel_id=1, source_target_pairs={{0,4},{1,5},{2,6},{3,7},{4,0},{5,1},{6,2},{7,3},{8,12},{9,13},{10,... | collective-permute-start | bytes 1179656 | tf_op jit(solution)/shard_map/ppermute | solution.py:54
  181.2 28.1 %copy-start.8 = (f32[64,1024]{1,0:T(8,128)S(1)}, f32[64,1024]{1,0:T(8,128)}, u32[]{:S(2)}) copy-start(f32[64,1024]{1,0:T(8,128)} %copy-done.7) | copy-start | bytes 786436
  181.2 11.6 %collective-permute-start.36 = (bf16[256,1536]{1,0:T(8,128)(2,1)}, bf16[256,1536]{1,0:T(8,128)(2,1)S(1)}, u32[]{:S(2)}, u32[]{:S(2)}) collective-permute-start(bf16[256,1536]{1,0:T(8,128)(2,1)} %after.11.refs_2_), channel_id=1, source_target_pairs={{0,1},{1,0},{2,3},{3,2},{4,5},{5,4},{6,7},{7,6},{8,9},{9,8},{10,11... | collective-permute-start | bytes 2359304 | tf_op jit(solution)/shard_map/ppermute | solution.py:54
  181.5 11.4 %collective-permute-start.33 = (bf16[128,1536]{1,0:T(8,128)(2,1)S(1)}, bf16[128,1536]{1,0:T(8,128)(2,1)S(1)}, u32[]{:S(2)}, u32[]{:S(2)}) collective-permute-start(bf16[128,1536]{1,0:T(8,128)(2,1)S(1)} %slice.29), channel_id=1, source_target_pairs={{0,2},{1,3},{2,0},{3,1},{4,6},{5,7},{6,4},{7,5},{8,10},{9,11},{10,... | collective-permute-start | bytes 1179656 | tf_op jit(solution)/shard_map/ppermute | solution.py:54
  190.1 2.8 %collective-permute-start.37 = (bf16[128,1536]{1,0:T(8,128)(2,1)S(1)}, bf16[128,1536]{1,0:T(8,128)(2,1)S(1)}, u32[]{:S(2)}, u32[]{:S(2)}) collective-permute-start(bf16[128,1536]{1,0:T(8,128)(2,1)S(1)} %collective-permute-done.32.refs_3_), channel_id=1, source_target_pairs={{0,1},{1,0},{2,3},{3,2},{4,5},{5,4},{6,7},{7,6},{8,9},{9,8},{10,11... | collective-permute-start | bytes 1179656 | tf_op jit(solution)/shard_map/ppermute | solution.py:54
  192.8 1.7 collective-permute-start.38
  201.8 23.1 %collective-permute-start.41 = (f32[64,1536]{1,0:T(8,128)}, f32[64,1536]{1,0:T(8,128)S(1)}, u32[]{:S(2)}, u32[]{:S(2)}) collective-permute-start(f32[64,1536]{1,0:T(8,128)} %get-tuple-element.56), channel_id=1, source_target_pairs={{0,8},{8,0},{16,24},{24,16},{1,9},{9,1},{17,25},{25,17},{2,10},{10... | collective-permute-start | bytes 1179656 | tf_op jit(solution)/shard_map/ppermute | solution.py:54
  202.9 22.1 %collective-permute-start.42 = (bf16[64,1536]{1,0:T(8,128)(2,1)}, bf16[64,1536]{1,0:T(8,128)(2,1)S(1)}, u32[]{:S(2)}, u32[]{:S(2)}) collective-permute-start(bf16[64,1536]{1,0:T(8,128)(2,1)} %get-tuple-element.57), channel_id=1, source_target_pairs={{0,16},{8,24},{16,0},{24,8},{1,17},{9,25},{17,1},{25,9},{2,18},{10... | collective-permute-start | bytes 589832 | tf_op jit(solution)/shard_map/ppermute | solution.py:54
  204.8 20.1 %collective-permute-start.43 = (bf16[64,1536]{1,0:T(8,128)(2,1)}, bf16[64,1536]{1,0:T(8,128)(2,1)S(1)}, u32[]{:S(2)}, u32[]{:S(2)}) collective-permute-start(bf16[64,1536]{1,0:T(8,128)(2,1)} %get-tuple-element.58), channel_id=1, source_target_pairs={{0,24},{8,16},{16,8},{24,0},{1,25},{9,17},{17,9},{25,1},{2,26},{10... | collective-permute-start | bytes 589832 | tf_op jit(solution)/shard_map/ppermute | solution.py:54
  206.2 18.1 %all-to-all-start.1 = ((f32[32,1,64]{2,1,0:T(1,128)}), f32[32,1,64]{2,1,0:T(1,128)S(1)}, u32[]{:S(2)}, u32[]{:S(2)}) async-start(f32[32,1,64]{2,1,0:T(1,128)} %bitcast.11), calls=%async_computation.1 | async-start | bytes 32768 | tf_op jit(solution)/shard_map/all_to_all | solution.py:570
  (42 other events, 165.7 us)

commit v4 on v3

--- a/solution.py
+++ b/solution.py
@@ -236,8 +236,7 @@
         mixed = side_by_side(nn((weights * inverse).astype(bf16), values), heads)
         o_ref[here, :] = mixed
         attn_all[here, :] = mixed.astype(bf16)
-        stats_ref[b, :, :1] = peak
-        stats_ref[b, :, 1:2] = inverse
+        stats_ref[here, :] = jnp.concatenate([side_by_side(peak, heads), side_by_side(inverse, heads)], axis=1)
     rows = length // groups
     for g in range(groups):
         hand_out(u, g, attn_all[g * rows : (g + 1) * rows, :], outs)
@@ -259,7 +258,11 @@
         keys, values = kv_all[there, :HEAD_DIM], kv_all[there, HEAD_DIM:]
         queries, grads = stacked(q_all, here, heads), stacked(g_all, here, heads)
         scores = nt(queries, keys) + jnp.concatenate([bias] * heads, axis=0)
-        shares = jnp.exp(scores - stats_ref[b, :, :1]) * stats_ref[b, :, 1:2]
+        stats = stats_ref[here, :]
+        peak, inverse = (
+            jnp.concatenate([stats[:, i + h : i + h + 1] for h in range(heads)], axis=0) for i in (0, heads)
+        )
+        shares = jnp.exp(scores - peak) * inverse
         row_dot = jnp.sum(grads.astype(f32) * stacked(o_ref, here, heads), axis=1, keepdims=True)
         d_scores = (shares * (nt(grads, values) - row_dot)).astype(bf16)
         dq_all[here, :] = side_by_side(nn(d_scores, keys) * SCALE, heads)
@@ -420,7 +423,7 @@
     held = weights_here(w_qkv, w_out, gain, me, qw)
     held_near = neighbours(held, "dp")
     grad_pair = swap(grad_rows, "ulysses", 1)
-    held_arrays, held_slots = complete(held, after(held_near[0], grad_pair), held_near[1], "dp")
+    held_arrays, held_slots = complete(after(held, grad_pair), *held_near, "dp")
 
     bounds = jnp.cumsum(lengths[0]) - lengths[0]
     places = jnp.arange(length, dtype=jnp.int32)
@@ -469,11 +472,10 @@
     )(me, grad_rows, grad_pair, *held_arrays, qkv_here[1])
     grads_here = [pieces[0]] + [swap(after(pieces[i], *qkv_here[1:]), "ulysses", 2 * i) for i in range(1, sets)]
 
-    blocks = length // Q_BLOCK
     *mixed, o, stats = pl.pallas_call(
         functools.partial(forward_kernel, groups),
         out_shape=[shape(rows, qw)] * groups
-        + [shape(length, qw, dtype=f32), shape(blocks, heads * Q_BLOCK, 2, dtype=f32)],
+        + [shape(length, qw, dtype=f32), shape(length, 2 * heads, dtype=f32)],
         in_specs=[SMEM] * 2 + [VMEM] * groups + [ANY],
         out_specs=[VMEM] * (groups + 2),
         scratch_shapes=[
@@ -551,7 +553,7 @@
         name="d_tokens",
     )(me, token_rows, grad_rows, d_proj, *held_arrays, d_w_out)
 
-    proj_arrays, proj_slots = complete(d_proj, after(proj_near[0], partial_gain), after(proj_near[1], out_terms[0]), "dp")
+    proj_arrays, proj_slots = complete(after(d_proj, out_terms[0]), after(proj_near[0], partial_gain), proj_near[1], "dp")
     d_w_qkv, *terms, gain_terms = pl.pallas_call(
         functools.partial(grads_and_pass_kernel, proj_slots, 0, groups, factor),
         out_shape=[shape(block, columns, dtype=f32)] * 2 + [shape(block, columns)] * (groups - 2) + [shape(groups, n, block, dtype=f32)],
@@ -562,8 +564,8 @@
         cost_estimate=about(6),
         name="d_w_qkv",
     )(me, slices, *proj_arrays, *out_terms, partial_gain)
-    for j, term in enumerate(terms, 1):
-        d_w_qkv = d_w_qkv + swap(term, "ulysses", j).astype(f32)
+    for term in [swap(terms[j - 1], "ulysses", j) for j in reversed(range(1, groups))]:
+        d_w_qkv = d_w_qkv + term.astype(f32)
     for term in out_terms:
         d_w_out = d_w_out + term.astype(f32)
     d_gain = gain_terms.reshape(groups * n, block)

time: 226 us -> 222 us (0.982)
  local copies, waits for them, and re-layouts: 18.4 us -> 16 us
    unnamed x88 -> x84, local copies, waits for them, and re-layouts: 11.2 us -> 9.81 us
  transfers between devices with their start and end apart: 46 -> 46, of which waited for: 11 -> 12; matrix products, arithmetic and copies ran while one was open for 5% -> 4% of each run, Pallas kernels for 21% -> 21%
where the time goes in v4:
time: 222 us; the launch traced here: 221 us
  waiting for transfers between devices  79.9 us (36%)
  Pallas kernels  65.8 us (30%)
  starting transfers between devices  52.6 us (24%)
  local copies, waits for them, and re-layouts  16 us (7%)
  other arithmetic  5.96 us (3%)
    ppermute x44, waiting for transfers between devices, swap(): return lax.ppermute(a, axis, [(i, i ^ bit) for i in range(n)])  67 us
    ppermute x44, starting transfers between devices, swap(): return lax.ppermute(a, axis, [(i, i ^ bit) for i in range(n)])  44.9 us
    all_to_all x1, waiting for transfers between devices, body(): lax.all_to_all(d_gain, ('ulysses', 'dp'), 0, 0, tiled=True).sum(axis=0)  12.9 us
    pallas_call x1, Pallas kernels, body(): pl.pallas_call(functools.partial(backward_kernel, groups), out_shape=[sha...  12.5 us
    unnamed x84, local copies, waits for them, and re-layouts  9.81 us
    pallas_call x1, Pallas kernels, body(): pl.pallas_call(functools.partial(forward_kernel, groups), out_shape=[shap...  8.4 us
    pallas_call x1, Pallas kernels, body(): pl.pallas_call(functools.partial(tokens_kernel, held_slots, len(held_arra...  8.21 us
    pallas_call x1, Pallas kernels, body(): pl.pallas_call(functools.partial(proj_kernel, held_slots, len(held_arrays...  8.1 us
  transfers between devices with their start and end apart: 46, of which 12 were waited for; matrix products, arithmetic and copies ran while one was open for 4% of the time, Pallas kernels for 21%

profile of v4, /device:TPU:0, one launch (start us, length us, event | category | flops | bytes accessed | tf_op | source)
XLA Modules:
  0.0 221.3 jit_solution(6753150487931130932)
XLA Ops:
  0.6 1.2 broadcast_in_dim.32.gain_ref
  2.5 2.4 %weights_here.1.refs_0_ = bf16[272,2048]{1,0:T(8,128)(2,1)} custom-call(s32[2]{0:T(128)} %pad_add_fusion.me_ref, bf16[256,1536]{1,0:T(8,128)(2,1)} %w_qkv_ref.1, bf16[256,1024]{1,0:T(8,128)(2,1)} %w_out_ref.1, bf16[1,256]{1,0:T(2,128)(2,1)} %broadcast_in_dim.32.gain_ref), custom_call_target="tpu_custom_call" | custom-call | flops 2000000000 | bytes 6000000 | tf_op jit(solution)/shard_map/weights_here/pallas_call | solution.py:379
  4.9 3.0 %collective-permute-start.2 = (bf16[272,2048]{1,0:T(8,128)(2,1)}, bf16[272,2048]{1,0:T(8,128)(2,1)S(1)}, u32[]{:S(2)}, u32[]{:S(2)}) collective-permute-start(bf16[272,2048]{1,0:T(8,128)(2,1)} %weights_here.1.refs_0_), channel_id=1, source_target_pairs={{0,4},{1,5},{2,6},{3,7},{4,0},{5,1},{6,2},{7,3},{8,12},{9,13},{10,... | collective-permute-start | bytes 3342344 | tf_op jit(solution)/shard_map/ppermute | solution.py:54
  7.9 1.5 collective-permute-start.1
  9.4 1.6 collective-permute-start
  11.0 21.7 %collective-permute-done.2.refs_2_ = bf16[272,2048]{1,0:T(8,128)(2,1)S(1)} collective-permute-done((bf16[272,2048]{1,0:T(8,128)(2,1)}, bf16[272,2048]{1,0:T(8,128)(2,1)S(1)}, u32[]{:S(2)}, u32[]{:S(2)}) %collective-permute-start.2) | collective-permute-done | bytes 1114144 | tf_op jit(solution)/shard_map/ppermute | solution.py:54
  32.7 1.8 collective-permute-start.4
  35.6 1.1 slice.24
  36.7 1.6 collective-permute-start.3
  38.9 12.3 %collective-permute-done.3.refs_3_ = bf16[128,2048]{1,0:T(8,128)(2,1)} collective-permute-done((bf16[128,2048]{1,0:T(8,128)(2,1)S(1)}, bf16[128,2048]{1,0:T(8,128)(2,1)}, u32[]{:S(2)}, u32[]{:S(2)}) %collective-permute-start.3) | collective-permute-done | bytes 524320 | tf_op jit(solution)/shard_map/ppermute | solution.py:54
  51.9 1.9 fusion
  54.6 8.1 %proj.1 = (bf16[256,384]{1,0:T(8,128)(2,1)}, bf16[256,384]{1,0:T(8,128)(2,1)}, bf16[256,384]{1,0:T(8,128)(2,1)}, bf16[256,384]{1,0:T(8,128)(2,1)}, bf16[256,2048]{1,0:T(8,128)(2,1)}) custom-call(s32[2]{0:T(128)} %pad_add_fusion.me_ref, bf16[256,2048]{1,0:T(8,128)(2,1)} %bitcast.12, f32[256,128]{1,0:T(8,128)} %get-tuple-element.63.cos_ref, ...), custom_call_target="tpu_custom_call" | custom-call | flops 8000000000 | bytes 24000000 | tf_op jit(solution)/shard_map/proj/pallas_call | solution.py:439
  62.7 1.6 collective-permute-start.10
  64.4 2.6 %collective-permute-start.11 = (bf16[256,384]{1,0:T(8,128)(2,1)}, bf16[256,384]{1,0:T(8,128)(2,1)S(1)}, u32[]{:S(2)}, u32[]{:S(2)}) collective-permute-start(bf16[256,384]{1,0:T(8,128)(2,1)} %get-tuple-element.34), channel_id=1, source_target_pairs={{0,16},{8,24},{16,0},{24,8},{1,17},{9,25},{17,1},{25,9},{2,18},{10... | collective-permute-start | bytes 589832 | tf_op jit(solution)/shard_map/ppermute | solution.py:54
  67.2 3.4 %slices.1.refs_4_ = bf16[8,512,256]{2,1,0:T(8,128)(2,1)} custom-call(bf16[256,2048]{1,0:T(8,128)(2,1)} %get-tuple-element.36.normed_ref, bf16[256,2048]{1,0:T(8,128)(2,1)} %bitcast.15), custom_call_target="tpu_custom_call" | custom-call | flops 3000000000 | bytes 9000000 | tf_op jit(solution)/shard_map/slices/pallas_call | solution.py:451
  70.6 3.8 %all-to-all-start = ((bf16[8,512,256]{2,1,0:T(8,128)(2,1)}), bf16[8,512,256]{2,1,0:T(8,128)(2,1)S(1)}, u32[]{:S(2)}, u32[]{:S(2)}) async-start(bf16[8,512,256]{2,1,0:T(8,128)(2,1)} %slices.1.refs_4_), calls=%async_computation | async-start | bytes 4194304 | tf_op jit(solution)/shard_map/all_to_all | solution.py:461
  75.1 6.3 %d_attn.1 = (bf16[512,256]{1,0:T(8,128)(2,1)}, bf16[512,256]{1,0:T(8,128)(2,1)}) custom-call(s32[2]{0:T(128)} %pad_add_fusion.me_ref, bf16[256,2048]{1,0:T(8,128)(2,1)} %bitcast.16, bf16[256,2048]{1,0:T(8,128)(2,1)} %copy-done.5, bf16[272,2048]{1,0:T(8,128)(2,1)} %after.6.refs_0_, bf16[272,2048]{1,0:T(8,128)(2,1)} %collective-permute-done.1.refs_1_, ...), custom_call_target="tpu_custom_call" | custom-call | flops 6000000000 | bytes 18000000 | tf_op jit(solution)/shard_map/d_attn/pallas_call | solution.py:463
  82.5 4.5 %collective-permute-start.13 = (bf16[512,256]{1,0:T(8,128)(2,1)}, bf16[512,256]{1,0:T(8,128)(2,1)S(1)}, u32[]{:S(2)}, u32[]{:S(2)}) collective-permute-start(bf16[512,256]{1,0:T(8,128)(2,1)} %after.7), channel_id=1, source_target_pairs={{0,16},{8,24},{16,0},{24,8},{1,17},{9,25},{17,1},{25,9},{2,18},{10... | collective-permute-start | bytes 786440 | tf_op jit(solution)/shard_map/ppermute | solution.py:54
  87.0 8.4 %forward.1 = (bf16[256,256]{1,0:T(8,128)(2,1)}, bf16[256,256]{1,0:T(8,128)(2,1)}, bf16[256,256]{1,0:T(8,128)(2,1)}, bf16[256,256]{1,0:T(8,128)(2,1)}, f32[1024,256]{1,0:T(8,128)}, /*index=5*/f32[1024,8]{1,0:T(8,128)}) custom-call(s32[2]{0:T(128)} %pad_add_fusion.me_ref, s32[10]{0:T(128)} %bitcast.18, bf16[256,384]{1,0:T(8,128)(2,1)} %get-tuple-element.32.refs_0_, ...), custom_call_target="tpu_custom_call" | custom-call | flops 10000000000 | bytes 30000000 | tf_op jit(solution)/shard_map/forward/pallas_call | solution.py:475
  95.4 1.9 collective-permute-start.18
  97.3 2.5 %collective-permute-start.19 = (bf16[256,256]{1,0:T(8,128)(2,1)}, bf16[256,256]{1,0:T(8,128)(2,1)S(1)}, u32[]{:S(2)}, u32[]{:S(2)}) collective-permute-start(bf16[256,256]{1,0:T(8,128)(2,1)} %get-tuple-element.48), channel_id=1, source_target_pairs={{0,24},{8,16},{16,8},{24,0},{1,25},{9,17},{17,9},{25,1},{2,26},{10... | collective-permute-start | bytes 393224 | tf_op jit(solution)/shard_map/ppermute | solution.py:54
  100.5 12.5 %backward.1 = (bf16[256,384]{1,0:T(8,128)(2,1)}, bf16[256,384]{1,0:T(8,128)(2,1)}, bf16[256,384]{1,0:T(8,128)(2,1)}, bf16[256,384]{1,0:T(8,128)(2,1)}) custom-call(s32[2]{0:T(128)} %pad_add_fusion.me_ref, s32[10]{0:T(128)} %bitcast.19, f32[1024,128]{1,0:T(8,128)} %copy-done.9, f32[1024,128]{1,0:T(8,128)} %copy-done.8, f32[1024,256]{1,0:T(8,128)} %get-tuple-element.37.o_ref, ...), custom_call_target="tpu_custom_call" | custom-call | flops 15000000512 | bytes 45000000 | tf_op jit(solution)/shard_map/backward/pallas_call | solution.py:492
  114.4 2.0 join_attn.1.refs_0_
  117.0 1.5 collective-permute-start.21
  118.5 3.1 %collective-permute-start.15 = (bf16[256,384]{1,0:T(8,128)(2,1)S(1)}, bf16[256,384]{1,0:T(8,128)(2,1)S(1)}, u32[]{:S(2)}, u32[]{:S(2)}) collective-permute-start(bf16[256,384]{1,0:T(8,128)(2,1)S(1)} %copy-done.33), channel_id=1, source_target_pairs={{0,16},{8,24},{16,0},{24,8},{1,17},{9,25},{17,1},{25,9},{2,18},{10... | collective-permute-start | bytes 589832 | tf_op jit(solution)/shard_map/ppermute | solution.py:54
  121.7 1.3 collective-permute-start.16
  122.9 3.1 %collective-permute-done.14.refs_1_ = bf16[256,384]{1,0:T(8,128)(2,1)S(1)} collective-permute-done((bf16[256,384]{1,0:T(8,128)(2,1)S(1)}, bf16[256,384]{1,0:T(8,128)(2,1)S(1)}, u32[]{:S(2)}, u32[]{:S(2)}) %collective-permute-start.14) | collective-permute-done | bytes 196640 | tf_op jit(solution)/shard_map/ppermute | solution.py:54
  126.0 9.9 %collective-permute-done.15.refs_2_ = bf16[256,384]{1,0:T(8,128)(2,1)S(1)} collective-permute-done((bf16[256,384]{1,0:T(8,128)(2,1)S(1)}, bf16[256,384]{1,0:T(8,128)(2,1)S(1)}, u32[]{:S(2)}, u32[]{:S(2)}) %collective-permute-start.15) | collective-permute-done | bytes 196640 | tf_op jit(solution)/shard_map/ppermute | solution.py:54
  137.6 2.5 %join_proj.1.refs_1_.d_proj_ref.refs_0_ = bf16[256,1536]{1,0:T(8,128)(2,1)} custom-call(s32[2]{0:T(128)} %pad_add_fusion.me_ref, bf16[256,384]{1,0:T(8,128)(2,1)} %get-tuple-element.41.refs_5_.refs_0_, bf16[256,384]{1,0:T(8,128)(2,1)} %copy-done.35, bf16[256,384]{1,0:T(8,128)(2,1)} %copy-done.36, bf16[256,384]{1,0:T(8,128)(2,1)} %copy-done.37, ...), custom_call_target="tpu_custom_call" | custom-call | flops 3000000000 | bytes 9000000 | tf_op jit(solution)/shard_map/join_proj/pallas_call | solution.py:520
  143.2 6.6 %collective-permute-done.23.refs_4_ = bf16[128,1024]{1,0:T(8,128)(2,1)S(1)} collective-permute-done((bf16[128,1024]{1,0:T(8,128)(2,1)S(1)}, bf16[128,1024]{1,0:T(8,128)(2,1)S(1)}, u32[]{:S(2)}, u32[]{:S(2)}) %collective-permute-start.23) | collective-permute-done | bytes 262176 | tf_op jit(solution)/shard_map/ppermute | solution.py:54
  149.8 1.5 collective-permute-done.22.refs_3_
  151.4 1.7 collective-permute-start.30
  155.2 5.4 %d_w_out.1 = (f32[64,1024]{1,0:T(8,128)}, f32[64,1024]{1,0:T(8,128)}, bf16[64,1024]{1,0:T(8,128)(2,1)}, bf16[64,1024]{1,0:T(8,128)(2,1)}) custom-call(s32[2]{0:T(128)} %pad_add_fusion.me_ref, bf16[8,512,256]{2,1,0:T(8,128)(2,1)} %copy-done.1, bf16[256,1024]{1,0:T(8,128)(2,1)} %join_attn.1.refs_0_, bf16[256,1024]{1,0:T(8,128)(2,1)} %after.8.refs_1_, ...), custom_call_target="tpu_custom_call" | custom-call | flops 5000000000 | bytes 15000000 | tf_op jit(solution)/shard_map/d_w_out/pallas_call | solution.py:532
  160.6 2.6 %collective-permute-start.29 = (f32[64,1024]{1,0:T(8,128)}, f32[64,1024]{1,0:T(8,128)S(1)}, u32[]{:S(2)}, u32[]{:S(2)}) collective-permute-start(f32[64,1024]{1,0:T(8,128)} %get-tuple-element.51), channel_id=1, source_target_pairs={{0,8},{8,0},{16,24},{24,16},{1,9},{9,1},{17,25},{25,17},{2,10},{10... | collective-permute-start | bytes 786440 | tf_op jit(solution)/shard_map/ppermute | solution.py:54
  163.2 1.1 collective-permute-start.39
  164.3 1.4 collective-permute-start.40
  165.7 8.2 %d_tokens.1 = (bf16[256,2048]{1,0:T(8,128)(2,1)}, f32[4,8,64]{2,1,0:T(8,128)}) custom-call(s32[2]{0:T(128)} %pad_add_fusion.me_ref, bf16[256,2048]{1,0:T(8,128)(2,1)} %bitcast.13, bf16[256,2048]{1,0:T(8,128)(2,1)} %bitcast.17, bf16[256,1536]{1,0:T(8,128)(2,1)} %join_proj.1.refs_1_.d_proj_ref.refs_0_, bf16[272,2048]{1,0:T(8,128)(2,1)} %after.6.refs_0_, ...), custom_call_target="tpu_custom_call" | custom-call | flops 8000000000 | bytes 24000000 | tf_op jit(solution)/shard_map/d_tokens/pallas_call | solution.py:545
  174.8 1.0 slice.28
  175.9 1.6 collective-permute-start.32
  178.9 8.6 %collective-permute-done.32.refs_3_ = bf16[128,1536]{1,0:T(8,128)(2,1)S(1)} collective-permute-done((bf16[128,1536]{1,0:T(8,128)(2,1)S(1)}, bf16[128,1536]{1,0:T(8,128)(2,1)S(1)}, u32[]{:S(2)}, u32[]{:S(2)}) %collective-permute-start.32) | collective-permute-done | bytes 393248 | tf_op jit(solution)/shard_map/ppermute | solution.py:54
  187.5 1.3 collective-permute-done.33.refs_4_
  189.2 1.3 collective-permute-done.38.refs_9_
  191.4 6.5 %d_w_qkv.1 = (f32[64,1536]{1,0:T(8,128)}, f32[64,1536]{1,0:T(8,128)}, bf16[64,1536]{1,0:T(8,128)(2,1)}, bf16[64,1536]{1,0:T(8,128)(2,1)}, f32[4,8,64]{2,1,0:T(8,128)}) custom-call(s32[2]{0:T(128)} %pad_add_fusion.me_ref, bf16[8,512,256]{2,1,0:T(8,128)(2,1)} %copy-done.1, bf16[256,1536]{1,0:T(8,128)(2,1)} %after.10.refs_0_, bf16[256,1536]{1,0:T(8,128)(2,1)} %after.11.refs_1_, ...), custom_call_target="tpu_custom_call" | custom-call | flops 6000000000 | bytes 18000000 | tf_op jit(solution)/shard_map/d_w_qkv/pallas_call | solution.py:557
  197.9 1.1 collective-permute-start.43
  199.0 2.5 %collective-permute-start.41 = (bf16[64,1536]{1,0:T(8,128)(2,1)}, bf16[64,1536]{1,0:T(8,128)(2,1)S(1)}, u32[]{:S(2)}, u32[]{:S(2)}) collective-permute-start(bf16[64,1536]{1,0:T(8,128)(2,1)} %get-tuple-element.56), channel_id=1, source_target_pairs={{0,24},{8,16},{16,8},{24,0},{1,25},{9,17},{17,9},{25,1},{2,26},{10... | collective-permute-start | bytes 589832 | tf_op jit(solution)/shard_map/ppermute | solution.py:54
  201.4 3.9 %all-to-all-start.1 = ((f32[32,1,64]{2,1,0:T(1,128)}), f32[32,1,64]{2,1,0:T(1,128)S(1)}, u32[]{:S(2)}, u32[]{:S(2)}) async-start(f32[32,1,64]{2,1,0:T(1,128)} %bitcast.11), calls=%async_computation.1 | async-start | bytes 32768 | tf_op jit(solution)/shard_map/all_to_all | solution.py:572
  205.3 1.7 convert_add_fusion
  207.1 12.9 %all-to-all-done.1 = f32[32,1,64]{2,1,0:T(1,128)S(1)} async-done(((f32[32,1,64]{2,1,0:T(1,128)}), f32[32,1,64]{2,1,0:T(1,128)S(1)}, u32[]{:S(2)}, u32[]{:S(2)}) %all-to-all-start.1) | async-done | bytes 8224 | tf_op jit(solution)/shard_map/all_to_all | solution.py:572
  (166 shorter events, 20.3 us)
Async XLA Ops:
  4.9 29.6 %copy-start.41 = (s32[1,10]{1,0:T(1,128)S(1)}, s32[1,10]{1,0:T(1,128)}, u32[]{:S(2)}) copy-start(s32[1,10]{1,0:T(1,128)} %param.8) | copy-start | bytes 124
  4.9 27.7 %collective-permute-start.2 = (bf16[272,2048]{1,0:T(8,128)(2,1)}, bf16[272,2048]{1,0:T(8,128)(2,1)S(1)}, u32[]{:S(2)}, u32[]{:S(2)}) collective-permute-start(bf16[272,2048]{1,0:T(8,128)(2,1)} %weights_here.1.refs_0_), channel_id=1, source_target_pairs={{0,4},{1,5},{2,6},{3,7},{4,0},{5,1},{6,2},{7,3},{8,12},{9,13},{10,... | collective-permute-start | bytes 3342344 | tf_op jit(solution)/shard_map/ppermute | solution.py:54
  7.9 26.8 %collective-permute-start.1 = (bf16[272,2048]{1,0:T(8,128)(2,1)}, bf16[272,2048]{1,0:T(8,128)(2,1)}, u32[]{:S(2)}, u32[]{:S(2)}) collective-permute-start(bf16[272,2048]{1,0:T(8,128)(2,1)} %weights_here.1.refs_0_), channel_id=1, source_target_pairs={{0,2},{1,3},{2,0},{3,1},{4,6},{5,7},{6,4},{7,5},{8,10},{9,11},{10,... | collective-permute-start | bytes 3342344 | tf_op jit(solution)/shard_map/ppermute | solution.py:54
  9.4 25.3 %collective-permute-start = (bf16[256,2048]{1,0:T(8,128)(2,1)}, bf16[256,2048]{1,0:T(8,128)(2,1)S(1)}, u32[]{:S(2)}, u32[]{:S(2)}) collective-permute-start(bf16[256,2048]{1,0:T(8,128)(2,1)} %bitcast.14), channel_id=1, source_target_pairs={{0,8},{8,0},{16,24},{24,16},{1,9},{9,1},{17,25},{25,17},{2,10},{10... | collective-permute-start | bytes 3145736 | tf_op jit(solution)/shard_map/ppermute | solution.py:54
  32.7 18.5 %collective-permute-start.4 = (bf16[144,2048]{1,0:T(8,128)(2,1)S(1)}, bf16[144,2048]{1,0:T(8,128)(2,1)}, u32[]{:S(2)}, u32[]{:S(2)}) collective-permute-start(bf16[144,2048]{1,0:T(8,128)(2,1)S(1)} %slice.25), channel_id=1, source_target_pairs={{0,2},{1,3},{2,0},{3,1},{4,6},{5,7},{6,4},{7,5},{8,10},{9,11},{10,... | collective-permute-start | bytes 1769480 | tf_op jit(solution)/shard_map/ppermute | solution.py:54
  35.6 18.9 %collective-permute-start.5 = (bf16[272,2048]{1,0:T(8,128)(2,1)}, bf16[272,2048]{1,0:T(8,128)(2,1)}, u32[]{:S(2)}, u32[]{:S(2)}) collective-permute-start(bf16[272,2048]{1,0:T(8,128)(2,1)} %after.6.refs_0_), channel_id=1, source_target_pairs={{0,1},{1,0},{2,3},{3,2},{4,5},{5,4},{6,7},{7,6},{8,9},{9,8},{10,11... | collective-permute-start | bytes 3342344 | tf_op jit(solution)/shard_map/ppermute | solution.py:54
  36.7 14.5 %collective-permute-start.3 = (bf16[128,2048]{1,0:T(8,128)(2,1)S(1)}, bf16[128,2048]{1,0:T(8,128)(2,1)}, u32[]{:S(2)}, u32[]{:S(2)}) collective-permute-start(bf16[128,2048]{1,0:T(8,128)(2,1)S(1)} %slice.24), channel_id=1, source_target_pairs={{0,4},{1,5},{2,6},{3,7},{4,0},{5,1},{6,2},{7,3},{8,12},{9,13},{10,... | collective-permute-start | bytes 1572872 | tf_op jit(solution)/shard_map/ppermute | solution.py:54
  38.3 16.3 %collective-permute-start.6 = (bf16[272,2048]{1,0:T(8,128)(2,1)}, bf16[272,2048]{1,0:T(8,128)(2,1)}, u32[]{:S(2)}, u32[]{:S(2)}) collective-permute-start(bf16[272,2048]{1,0:T(8,128)(2,1)} %collective-permute-done.1.refs_1_), channel_id=1, source_target_pairs={{0,1},{1,0},{2,3},{3,2},{4,5},{5,4},{6,7},{7,6},{8,9},{9,8},{10,11... | collective-permute-start | bytes 3342344 | tf_op jit(solution)/shard_map/ppermute | solution.py:54
  38.5 16.1 %collective-permute-start.7 = (bf16[272,2048]{1,0:T(8,128)(2,1)S(1)}, bf16[272,2048]{1,0:T(8,128)(2,1)}, u32[]{:S(2)}, u32[]{:S(2)}) collective-permute-start(bf16[272,2048]{1,0:T(8,128)(2,1)S(1)} %collective-permute-done.2.refs_2_), channel_id=1, source_target_pairs={{0,1},{1,0},{2,3},{3,2},{4,5},{5,4},{6,7},{7,6},{8,9},{9,8},{10,11... | collective-permute-start | bytes 3342344 | tf_op jit(solution)/shard_map/ppermute | solution.py:54
  51.2 3.4 %collective-permute-start.8 = (bf16[128,2048]{1,0:T(8,128)(2,1)}, bf16[128,2048]{1,0:T(8,128)(2,1)}, u32[]{:S(2)}, u32[]{:S(2)}) collective-permute-start(bf16[128,2048]{1,0:T(8,128)(2,1)} %collective-permute-done.3.refs_3_), channel_id=1, source_target_pairs={{0,1},{1,0},{2,3},{3,2},{4,5},{5,4},{6,7},{7,6},{8,9},{9,8},{10,11... | collective-permute-start | bytes 1572872 | tf_op jit(solution)/shard_map/ppermute | solution.py:54
  51.2 3.4 %collective-permute-start.9 = (bf16[144,2048]{1,0:T(8,128)(2,1)}, bf16[144,2048]{1,0:T(8,128)(2,1)}, u32[]{:S(2)}, u32[]{:S(2)}) collective-permute-start(bf16[144,2048]{1,0:T(8,128)(2,1)} %collective-permute-done.4.refs_4_), channel_id=1, source_target_pairs={{0,1},{1,0},{2,3},{3,2},{4,5},{5,4},{6,7},{7,6},{8,9},{9,8},{10,11... | collective-permute-start | bytes 1769480 | tf_op jit(solution)/shard_map/ppermute | solution.py:54
  62.7 11.7 %collective-permute-start.10 = (bf16[256,384]{1,0:T(8,128)(2,1)}, bf16[256,384]{1,0:T(8,128)(2,1)S(1)}, u32[]{:S(2)}, u32[]{:S(2)}) collective-permute-start(bf16[256,384]{1,0:T(8,128)(2,1)} %get-tuple-element.33), channel_id=1, source_target_pairs={{0,8},{8,0},{16,24},{24,16},{1,9},{9,1},{17,25},{25,17},{2,10},{10... | collective-permute-start | bytes 589832 | tf_op jit(solution)/shard_map/ppermute | solution.py:54
  64.4 17.3 %collective-permute-start.11 = (bf16[256,384]{1,0:T(8,128)(2,1)}, bf16[256,384]{1,0:T(8,128)(2,1)S(1)}, u32[]{:S(2)}, u32[]{:S(2)}) collective-permute-start(bf16[256,384]{1,0:T(8,128)(2,1)} %get-tuple-element.34), channel_id=1, source_target_pairs={{0,16},{8,24},{16,0},{24,8},{1,17},{9,25},{17,1},{25,9},{2,18},{10... | collective-permute-start | bytes 589832 | tf_op jit(solution)/shard_map/ppermute | solution.py:54
  67.0 14.8 %collective-permute-start.12 = (bf16[256,384]{1,0:T(8,128)(2,1)}, bf16[256,384]{1,0:T(8,128)(2,1)S(1)}, u32[]{:S(2)}, u32[]{:S(2)}) collective-permute-start(bf16[256,384]{1,0:T(8,128)(2,1)} %get-tuple-element.35), channel_id=1, source_target_pairs={{0,24},{8,16},{16,8},{24,0},{1,25},{9,17},{17,9},{25,1},{2,26},{10... | collective-permute-start | bytes 589832 | tf_op jit(solution)/shard_map/ppermute | solution.py:54
  70.6 42.4 %all-to-all-start = ((bf16[8,512,256]{2,1,0:T(8,128)(2,1)}), bf16[8,512,256]{2,1,0:T(8,128)(2,1)S(1)}, u32[]{:S(2)}, u32[]{:S(2)}) async-start(bf16[8,512,256]{2,1,0:T(8,128)(2,1)} %slices.1.refs_4_), calls=%async_computation | async-start | bytes 4194304 | tf_op jit(solution)/shard_map/all_to_all | solution.py:461
  82.5 17.3 %collective-permute-start.13 = (bf16[512,256]{1,0:T(8,128)(2,1)}, bf16[512,256]{1,0:T(8,128)(2,1)S(1)}, u32[]{:S(2)}, u32[]{:S(2)}) collective-permute-start(bf16[512,256]{1,0:T(8,128)(2,1)} %after.7), channel_id=1, source_target_pairs={{0,16},{8,24},{16,0},{24,8},{1,17},{9,25},{17,1},{25,9},{2,18},{10... | collective-permute-start | bytes 786440 | tf_op jit(solution)/shard_map/ppermute | solution.py:54
  95.4 17.6 %collective-permute-start.17 = (bf16[256,256]{1,0:T(8,128)(2,1)}, bf16[256,256]{1,0:T(8,128)(2,1)S(1)}, u32[]{:S(2)}, u32[]{:S(2)}) collective-permute-start(bf16[256,256]{1,0:T(8,128)(2,1)} %get-tuple-element.46), channel_id=1, source_target_pairs={{0,8},{8,0},{16,24},{24,16},{1,9},{9,1},{17,25},{25,17},{2,10},{10... | collective-permute-start | bytes 393224 | tf_op jit(solution)/shard_map/ppermute | solution.py:54
  95.4 17.6 %collective-permute-start.18 = (bf16[256,256]{1,0:T(8,128)(2,1)}, bf16[256,256]{1,0:T(8,128)(2,1)S(1)}, u32[]{:S(2)}, u32[]{:S(2)}) collective-permute-start(bf16[256,256]{1,0:T(8,128)(2,1)} %get-tuple-element.47), channel_id=1, source_target_pairs={{0,16},{8,24},{16,0},{24,8},{1,17},{9,25},{17,1},{25,9},{2,18},{10... | collective-permute-start | bytes 393224 | tf_op jit(solution)/shard_map/ppermute | solution.py:54
  97.3 15.7 %collective-permute-start.19 = (bf16[256,256]{1,0:T(8,128)(2,1)}, bf16[256,256]{1,0:T(8,128)(2,1)S(1)}, u32[]{:S(2)}, u32[]{:S(2)}) collective-permute-start(bf16[256,256]{1,0:T(8,128)(2,1)} %get-tuple-element.48), channel_id=1, source_target_pairs={{0,24},{8,16},{16,8},{24,0},{1,25},{9,17},{17,9},{25,1},{2,26},{10... | collective-permute-start | bytes 393224 | tf_op jit(solution)/shard_map/ppermute | solution.py:54
  116.5 19.4 %collective-permute-start.20 = (bf16[256,1024]{1,0:T(8,128)(2,1)}, bf16[256,1024]{1,0:T(8,128)(2,1)S(1)}, u32[]{:S(2)}, u32[]{:S(2)}) collective-permute-start(bf16[256,1024]{1,0:T(8,128)(2,1)} %join_attn.1.refs_0_), channel_id=1, source_target_pairs={{0,2},{1,3},{2,0},{3,1},{4,6},{5,7},{6,4},{7,5},{8,10},{9,11},{10,... | collective-permute-start | bytes 1572872 | tf_op jit(solution)/shard_map/ppermute | solution.py:54
  117.0 18.9 %collective-permute-start.21 = (bf16[256,1024]{1,0:T(8,128)(2,1)}, bf16[256,1024]{1,0:T(8,128)(2,1)S(1)}, u32[]{:S(2)}, u32[]{:S(2)}) collective-permute-start(bf16[256,1024]{1,0:T(8,128)(2,1)} %join_attn.1.refs_0_), channel_id=1, source_target_pairs={{0,4},{1,5},{2,6},{3,7},{4,0},{5,1},{6,2},{7,3},{8,12},{9,13},{10,... | collective-permute-start | bytes 1572872 | tf_op jit(solution)/shard_map/ppermute | solution.py:54
  118.5 7.5 %collective-permute-start.14 = (bf16[256,384]{1,0:T(8,128)(2,1)S(1)}, bf16[256,384]{1,0:T(8,128)(2,1)S(1)}, u32[]{:S(2)}, u32[]{:S(2)}) collective-permute-start(bf16[256,384]{1,0:T(8,128)(2,1)S(1)} %copy-done.34), channel_id=1, source_target_pairs={{0,8},{8,0},{16,24},{24,16},{1,9},{9,1},{17,25},{25,17},{2,10},{10... | collective-permute-start | bytes 589832 | tf_op jit(solution)/shard_map/ppermute | solution.py:54
  118.5 17.3 %collective-permute-start.15 = (bf16[256,384]{1,0:T(8,128)(2,1)S(1)}, bf16[256,384]{1,0:T(8,128)(2,1)S(1)}, u32[]{:S(2)}, u32[]{:S(2)}) collective-permute-start(bf16[256,384]{1,0:T(8,128)(2,1)S(1)} %copy-done.33), channel_id=1, source_target_pairs={{0,16},{8,24},{16,0},{24,8},{1,17},{9,25},{17,1},{25,9},{2,18},{10... | collective-permute-start | bytes 589832 | tf_op jit(solution)/shard_map/ppermute | solution.py:54
  121.7 14.2 %collective-permute-start.16 = (bf16[256,384]{1,0:T(8,128)(2,1)S(1)}, bf16[256,384]{1,0:T(8,128)(2,1)S(1)}, u32[]{:S(2)}, u32[]{:S(2)}) collective-permute-start(bf16[256,384]{1,0:T(8,128)(2,1)S(1)} %copy-done.32), channel_id=1, source_target_pairs={{0,24},{8,16},{16,8},{24,0},{1,25},{9,17},{17,9},{25,1},{2,26},{10... | collective-permute-start | bytes 589832 | tf_op jit(solution)/shard_map/ppermute | solution.py:54
  126.0 25.3 %collective-permute-start.24 = (bf16[256,1024]{1,0:T(8,128)(2,1)}, bf16[256,1024]{1,0:T(8,128)(2,1)S(1)}, u32[]{:S(2)}, u32[]{:S(2)}) collective-permute-start(bf16[256,1024]{1,0:T(8,128)(2,1)} %join_attn.1.refs_0_), channel_id=1, source_target_pairs={{0,1},{1,0},{2,3},{3,2},{4,5},{5,4},{6,7},{7,6},{8,9},{9,8},{10,11... | collective-permute-start | bytes 1572872 | tf_op jit(solution)/shard_map/ppermute | solution.py:54
  141.0 12.0 %collective-permute-start.26 = (bf16[256,1024]{1,0:T(8,128)(2,1)}, bf16[256,1024]{1,0:T(8,128)(2,1)}, u32[]{:S(2)}, u32[]{:S(2)}) collective-permute-start(bf16[256,1024]{1,0:T(8,128)(2,1)} %after.9.refs_2_), channel_id=1, source_target_pairs={{0,1},{1,0},{2,3},{3,2},{4,5},{5,4},{6,7},{7,6},{8,9},{9,8},{10,11... | collective-permute-start | bytes 1572872 | tf_op jit(solution)/shard_map/ppermute | solution.py:54
  141.1 8.7 %collective-permute-start.23 = (bf16[128,1024]{1,0:T(8,128)(2,1)S(1)}, bf16[128,1024]{1,0:T(8,128)(2,1)S(1)}, u32[]{:S(2)}, u32[]{:S(2)}) collective-permute-start(bf16[128,1024]{1,0:T(8,128)(2,1)S(1)} %slice.27), channel_id=1, source_target_pairs={{0,2},{1,3},{2,0},{3,1},{4,6},{5,7},{6,4},{7,5},{8,10},{9,11},{10,... | collective-permute-start | bytes 786440 | tf_op jit(solution)/shard_map/ppermute | solution.py:54
  142.5 11.1 %collective-permute-start.25 = (bf16[256,1024]{1,0:T(8,128)(2,1)}, bf16[256,1024]{1,0:T(8,128)(2,1)S(1)}, u32[]{:S(2)}, u32[]{:S(2)}) collective-permute-start(bf16[256,1024]{1,0:T(8,128)(2,1)} %after.8.refs_1_), channel_id=1, source_target_pairs={{0,1},{1,0},{2,3},{3,2},{4,5},{5,4},{6,7},{7,6},{8,9},{9,8},{10,11... | collective-permute-start | bytes 1572872 | tf_op jit(solution)/shard_map/ppermute | solution.py:54
  142.8 8.6 %collective-permute-start.22 = (bf16[128,1024]{1,0:T(8,128)(2,1)S(1)}, bf16[128,1024]{1,0:T(8,128)(2,1)S(1)}, u32[]{:S(2)}, u32[]{:S(2)}) collective-permute-start(bf16[128,1024]{1,0:T(8,128)(2,1)S(1)} %slice.26), channel_id=1, source_target_pairs={{0,4},{1,5},{2,6},{3,7},{4,0},{5,1},{6,2},{7,3},{8,12},{9,13},{10,... | collective-permute-start | bytes 786440 | tf_op jit(solution)/shard_map/ppermute | solution.py:54
  149.8 3.8 %collective-permute-start.28 = (bf16[128,1024]{1,0:T(8,128)(2,1)S(1)}, bf16[128,1024]{1,0:T(8,128)(2,1)S(1)}, u32[]{:S(2)}, u32[]{:S(2)}) collective-permute-start(bf16[128,1024]{1,0:T(8,128)(2,1)S(1)} %collective-permute-done.23.refs_4_), channel_id=1, source_target_pairs={{0,1},{1,0},{2,3},{3,2},{4,5},{5,4},{6,7},{7,6},{8,9},{9,8},{10,11... | collective-permute-start | bytes 786440 | tf_op jit(solution)/shard_map/ppermute | solution.py:54
  151.3 2.3 %collective-permute-start.27 = (bf16[128,1024]{1,0:T(8,128)(2,1)S(1)}, bf16[128,1024]{1,0:T(8,128)(2,1)S(1)}, u32[]{:S(2)}, u32[]{:S(2)}) collective-permute-start(bf16[128,1024]{1,0:T(8,128)(2,1)S(1)} %collective-permute-done.22.refs_3_), channel_id=1, source_target_pairs={{0,1},{1,0},{2,3},{3,2},{4,5},{5,4},{6,7},{7,6},{8,9},{9,8},{10,11... | collective-permute-start | bytes 786440 | tf_op jit(solution)/shard_map/ppermute | solution.py:54
  151.4 22.6 %collective-permute-start.30 = (bf16[256,1536]{1,0:T(8,128)(2,1)S(1)}, bf16[256,1536]{1,0:T(8,128)(2,1)S(1)}, u32[]{:S(2)}, u32[]{:S(2)}) collective-permute-start(bf16[256,1536]{1,0:T(8,128)(2,1)S(1)} %copy-done), channel_id=1, source_target_pairs={{0,2},{1,3},{2,0},{3,1},{4,6},{5,7},{6,4},{7,5},{8,10},{9,11},{10,... | collective-permute-start | bytes 2359304 | tf_op jit(solution)/shard_map/ppermute | solution.py:54
  153.1 22.9 %collective-permute-start.31 = (bf16[256,1536]{1,0:T(8,128)(2,1)S(1)}, bf16[256,1536]{1,0:T(8,128)(2,1)S(1)}, u32[]{:S(2)}, u32[]{:S(2)}) collective-permute-start(bf16[256,1536]{1,0:T(8,128)(2,1)S(1)} %copy-done), channel_id=1, source_target_pairs={{0,4},{1,5},{2,6},{3,7},{4,0},{5,1},{6,2},{7,3},{8,12},{9,13},{10,... | collective-permute-start | bytes 2359304 | tf_op jit(solution)/shard_map/ppermute | solution.py:54
  160.6 16.9 %collective-permute-start.29 = (f32[64,1024]{1,0:T(8,128)}, f32[64,1024]{1,0:T(8,128)S(1)}, u32[]{:S(2)}, u32[]{:S(2)}) collective-permute-start(f32[64,1024]{1,0:T(8,128)} %get-tuple-element.51), channel_id=1, source_target_pairs={{0,8},{8,0},{16,24},{24,16},{1,9},{9,1},{17,25},{25,17},{2,10},{10... | collective-permute-start | bytes 786440 | tf_op jit(solution)/shard_map/ppermute | solution.py:54
  163.2 15.1 %collective-permute-start.39 = (bf16[64,1024]{1,0:T(8,128)(2,1)}, bf16[64,1024]{1,0:T(8,128)(2,1)S(1)}, u32[]{:S(2)}, u32[]{:S(2)}) collective-permute-start(bf16[64,1024]{1,0:T(8,128)(2,1)} %get-tuple-element.53), channel_id=1, source_target_pairs={{0,16},{8,24},{16,0},{24,8},{1,17},{9,25},{17,1},{25,9},{2,18},{10... | collective-permute-start | bytes 393224 | tf_op jit(solution)/shard_map/ppermute | solution.py:54
  164.3 14.2 %collective-permute-start.40 = (bf16[64,1024]{1,0:T(8,128)(2,1)}, bf16[64,1024]{1,0:T(8,128)(2,1)S(1)}, u32[]{:S(2)}, u32[]{:S(2)}) collective-permute-start(bf16[64,1024]{1,0:T(8,128)(2,1)} %get-tuple-element.54), channel_id=1, source_target_pairs={{0,24},{8,16},{16,8},{24,0},{1,25},{9,17},{17,9},{25,1},{2,26},{10... | collective-permute-start | bytes 393224 | tf_op jit(solution)/shard_map/ppermute | solution.py:54
  175.8 13.0 %collective-permute-start.35 = (bf16[256,1536]{1,0:T(8,128)(2,1)}, bf16[256,1536]{1,0:T(8,128)(2,1)}, u32[]{:S(2)}, u32[]{:S(2)}) collective-permute-start(bf16[256,1536]{1,0:T(8,128)(2,1)} %after.11.refs_1_), channel_id=1, source_target_pairs={{0,1},{1,0},{2,3},{3,2},{4,5},{5,4},{6,7},{7,6},{8,9},{9,8},{10,11... | collective-permute-start | bytes 2359304 | tf_op jit(solution)/shard_map/ppermute | solution.py:54
  175.9 11.5 %collective-permute-start.32 = (bf16[128,1536]{1,0:T(8,128)(2,1)S(1)}, bf16[128,1536]{1,0:T(8,128)(2,1)S(1)}, u32[]{:S(2)}, u32[]{:S(2)}) collective-permute-start(bf16[128,1536]{1,0:T(8,128)(2,1)S(1)} %slice.28), channel_id=1, source_target_pairs={{0,4},{1,5},{2,6},{3,7},{4,0},{5,1},{6,2},{7,3},{8,12},{9,13},{10,... | collective-permute-start | bytes 1179656 | tf_op jit(solution)/shard_map/ppermute | solution.py:54
  177.6 11.2 %collective-permute-start.33 = (bf16[128,1536]{1,0:T(8,128)(2,1)S(1)}, bf16[128,1536]{1,0:T(8,128)(2,1)S(1)}, u32[]{:S(2)}, u32[]{:S(2)}) collective-permute-start(bf16[128,1536]{1,0:T(8,128)(2,1)S(1)} %slice.29), channel_id=1, source_target_pairs={{0,2},{1,3},{2,0},{3,1},{4,6},{5,7},{6,4},{7,5},{8,10},{9,11},{10,... | collective-permute-start | bytes 1179656 | tf_op jit(solution)/shard_map/ppermute | solution.py:54
  178.3 27.1 %copy-start.12 = (f32[64,1024]{1,0:T(8,128)S(1)}, f32[64,1024]{1,0:T(8,128)}, u32[]{:S(2)}) copy-start(f32[64,1024]{1,0:T(8,128)} %get-tuple-element.49.refs_10_) | copy-start | bytes 786436
  178.3 10.5 %collective-permute-start.36 = (bf16[256,1536]{1,0:T(8,128)(2,1)S(1)}, bf16[256,1536]{1,0:T(8,128)(2,1)S(1)}, u32[]{:S(2)}, u32[]{:S(2)}) collective-permute-start(bf16[256,1536]{1,0:T(8,128)(2,1)S(1)} %collective-permute-done.31.refs_2_), channel_id=1, source_target_pairs={{0,1},{1,0},{2,3},{3,2},{4,5},{5,4},{6,7},{7,6},{8,9},{9,8},{10,11... | collective-permute-start | bytes 2359304 | tf_op jit(solution)/shard_map/ppermute | solution.py:54
  178.5 10.7 %collective-permute-start.34 = (bf16[256,1536]{1,0:T(8,128)(2,1)}, bf16[256,1536]{1,0:T(8,128)(2,1)S(1)}, u32[]{:S(2)}, u32[]{:S(2)}) collective-permute-start(bf16[256,1536]{1,0:T(8,128)(2,1)} %after.10.refs_0_), channel_id=1, source_target_pairs={{0,1},{1,0},{2,3},{3,2},{4,5},{5,4},{6,7},{7,6},{8,9},{9,8},{10,11... | collective-permute-start | bytes 2359304 | tf_op jit(solution)/shard_map/ppermute | solution.py:54
  187.5 1.7 collective-permute-start.37
  188.8 1.7 collective-permute-start.38
  197.9 22.6 %collective-permute-start.43 = (f32[64,1536]{1,0:T(8,128)}, f32[64,1536]{1,0:T(8,128)S(1)}, u32[]{:S(2)}, u32[]{:S(2)}) collective-permute-start(f32[64,1536]{1,0:T(8,128)} %get-tuple-element.58), channel_id=1, source_target_pairs={{0,8},{8,0},{16,24},{24,16},{1,9},{9,1},{17,25},{25,17},{2,10},{10... | collective-permute-start | bytes 1179656 | tf_op jit(solution)/shard_map/ppermute | solution.py:54
  199.0 21.6 %collective-permute-start.41 = (bf16[64,1536]{1,0:T(8,128)(2,1)}, bf16[64,1536]{1,0:T(8,128)(2,1)S(1)}, u32[]{:S(2)}, u32[]{:S(2)}) collective-permute-start(bf16[64,1536]{1,0:T(8,128)(2,1)} %get-tuple-element.56), channel_id=1, source_target_pairs={{0,24},{8,16},{16,8},{24,0},{1,25},{9,17},{17,9},{25,1},{2,26},{10... | collective-permute-start | bytes 589832 | tf_op jit(solution)/shard_map/ppermute | solution.py:54
  201.4 19.1 %collective-permute-start.42 = (bf16[64,1536]{1,0:T(8,128)(2,1)}, bf16[64,1536]{1,0:T(8,128)(2,1)S(1)}, u32[]{:S(2)}, u32[]{:S(2)}) collective-permute-start(bf16[64,1536]{1,0:T(8,128)(2,1)} %get-tuple-element.57), channel_id=1, source_target_pairs={{0,16},{8,24},{16,0},{24,8},{1,17},{9,25},{17,1},{25,9},{2,18},{10... | collective-permute-start | bytes 589832 | tf_op jit(solution)/shard_map/ppermute | solution.py:54
  201.4 18.5 %all-to-all-start.1 = ((f32[32,1,64]{2,1,0:T(1,128)}), f32[32,1,64]{2,1,0:T(1,128)S(1)}, u32[]{:S(2)}, u32[]{:S(2)}) async-start(f32[32,1,64]{2,1,0:T(1,128)} %bitcast.11), calls=%async_computation.1 | async-start | bytes 32768 | tf_op jit(solution)/shard_map/all_to_all | solution.py:572
  (40 other events, 168.6 us)
